TPU v7x, 512 devices: a whole 4x8x8 slice. The times are simulated.
512 devices in a mesh: tm: 64 (over x, z, y_hi), tmpl: 8 (over y_lo, core).
Axes of the slice: x: 4, y: 8 (y_hi: 2, y_lo: 4; y = y_hi * 4 + y_lo), z: 8, core: 2. Of those that a mesh axis runs over, the one named last changes fastest.
Arguments:
- raw: bfloat16 [2048, 64, 8, 256], P('tm', None, 'tmpl')
- avail: int32 [64, 8, 2048], P(None, 'tmpl', 'tm'), may hold values from 0 to 1, as said below
- templates: bfloat16 [128, 8, 192], P('tmpl'), may hold values from -0.4375 to 0.4375
- stations: int32 [128, 8], replicated, may hold values from 0 to 2047, as said below
- shifts: int32 [128, 8], replicated, may hold values from 0 to 63
Outputs:
- stack: float32 [128, 131072], P(None, ('tm', 'tmpl'))
Inputs may be any that keep to these rules, and one draw needn't show every extreme that they name: `avail`: in each window and each block of 32 consecutive station numbers, at least 8 and at most 24 stations are available; every such block has exactly 24 available in some window, and some window has exactly 24 in every block. Each row names 8 different stations.
All inputs are finite; a program needn't handle non-finite values.
Results may differ from a plain program's by a relative error of at most 0.024.
Values may be sent and summed in bfloat16 or wider, within the bound.
No kernel may reach another device: no remote copies, remote signals or barrier semaphores. Data moves between devices by JAX's collectives and lax.ppermute only.
A program may use at most 64 MiB of HBM per device.

v0:
```python
import math

import jax
import jax.numpy as jnp
from jax import lax
from jax.sharding import PartitionSpec as P

L = 192
SMAX = 64


epsilon = 1e-05


def shifted(value, axis, by):
    count = lax.axis_size(axis)
    pairs = [(i, i + by) for i in range(count) if 0 <= i + by < count]
    return lax.ppermute(value, axis, pairs)


def forward_table(count, span):
    sample = jnp.arange(count, dtype=jnp.int32)[:, None]
    frequency = jnp.arange(span, dtype=jnp.int32)[None, :]
    angle = (sample * frequency % span).astype(jnp.float32) * (2.0 * math.pi / span)
    return jnp.concatenate([jnp.cos(angle), -jnp.sin(angle)], axis=1).astype(jnp.bfloat16)


def inverse_table(span, width):
    frequency = jnp.arange(span, dtype=jnp.int32)[:, None]
    lag = jnp.arange(width, dtype=jnp.int32)[None, :]
    angle = (frequency * lag % span).astype(jnp.float32) * (2.0 * math.pi / span)
    return jnp.concatenate([jnp.cos(angle), -jnp.sin(angle)], axis=0).astype(jnp.bfloat16)


def wave_spectra(waves, table):
    count = waves.shape[0]
    flat = waves.reshape(count * waves.shape[1], waves.shape[2])
    spectra = jnp.dot(flat, table[: waves.shape[2]], preferred_element_type=jnp.float32)
    return spectra.astype(jnp.bfloat16).reshape(count, waves.shape[1], table.shape[1])


def network_stack(spectra, present_flags, template_spec, lists, moves, inverse):
    span = inverse.shape[0] // 2
    group = lists.shape[0]
    listed = lists.shape[1]
    station_ids = jnp.arange(spectra.shape[0], dtype=jnp.int32)
    selector = (lists.reshape(group * listed)[:, None] == station_ids[None, :]).astype(jnp.bfloat16)
    picked = jnp.dot(selector, spectra, preferred_element_type=jnp.float32).reshape(
        group, listed, 2 * span
    )
    weight = jnp.dot(selector, present_flags, preferred_element_type=jnp.float32).reshape(
        group, listed
    )
    data_real = picked[..., :span]
    data_imag = picked[..., span:]
    wave_real = template_spec[..., :span].astype(jnp.float32)
    wave_imag = template_spec[..., span:].astype(jnp.float32)
    frequency = jnp.arange(span, dtype=jnp.int32)
    angle = (moves[:, :, None] * frequency[None, None, :] % span).astype(jnp.float32) * (
        2.0 * math.pi / span
    )
    cosine = jnp.cos(angle)
    sine_part = jnp.sin(angle)
    prod_real = data_real * wave_real + data_imag * wave_imag
    prod_imag = data_imag * wave_real - data_real * wave_imag
    summed_real = jnp.sum(weight[:, :, None] * (prod_real * cosine - prod_imag * sine_part), axis=1)
    summed_imag = jnp.sum(weight[:, :, None] * (prod_real * sine_part + prod_imag * cosine), axis=1)
    joined = jnp.concatenate([summed_real, summed_imag], axis=1).astype(jnp.bfloat16)
    series = jnp.dot(joined, inverse, preferred_element_type=jnp.float32)
    number = jnp.maximum(jnp.sum(weight, axis=1), 1.0)
    return series / (span * number[:, None])


def shards(raw, avail, templates, stations, shifts):
    width = raw.shape[3]
    span = width + L + SMAX
    waves = raw[:, :, 0, :]
    status = jnp.transpose(avail[:, 0, :])
    flags = status.astype(jnp.bfloat16)
    masked = waves * flags[:, :, None]
    got_waves, got_flags = (
        lax.all_to_all(masked, "tm", split_axis=1, concat_axis=0, tiled=True),
        lax.all_to_all(flags, "tm", split_axis=1, concat_axis=0, tiled=True),
    )
    block = got_waves[:, 0, :]
    present = got_flags[:, 0].astype(jnp.float32)
    following = shifted(block, ("tm", "tmpl"), -1)
    segment = jnp.concatenate([block, following], axis=1)
    power = jnp.mean(jnp.square(block.astype(jnp.float32)), axis=1)
    factor = present * lax.rsqrt(power + epsilon)
    scaled = (segment.astype(jnp.float32) * factor[:, None]).astype(jnp.bfloat16)
    table = forward_table(span, span)
    spectra = jnp.dot(scaled, table, preferred_element_type=jnp.float32).astype(jnp.bfloat16)
    present_flags = present.astype(jnp.bfloat16)
    inverse = inverse_table(span, width)
    template_spec = wave_spectra(lax.all_gather(templates, "tmpl", axis=0, tiled=True), table)
    count = template_spec.shape[0]
    group = math.gcd(count, 16)

    def one_group(items):
        return network_stack(spectra, present_flags, items[0], items[1], items[2], inverse)

    grouped = lax.map(
        one_group,
        (
            template_spec.reshape(
                count // group, group, template_spec.shape[1], template_spec.shape[2]
            ),
            stations.reshape(count // group, group, stations.shape[1]),
            shifts.reshape(count // group, group, shifts.shape[1]),
        ),
    )
    return grouped.reshape(count, width)


def solution(mesh):
    return jax.shard_map(
        shards,
        mesh=mesh,
        in_specs=(
            P("tm", None, "tmpl", None),
            P(None, "tmpl", "tm"),
            P("tmpl", None, None),
            P(),
            P(),
        ),
        out_specs=P(None, ("tm", "tmpl")),
        check_vma=False,
    )
```

profile of v0, /device:TPU:6, one launch (start us, length us, event | category | flops | bytes accessed | tf_op | source)
XLA Modules:
  0.0 152.5 jit_solution(8184674221368676026)
XLA Ops:
  0.0 0.8 convert_bitcast_fusion.1
  0.9 2.8 %bitcast_multiply_fusion = bf16[32,64,256]{2,0,1:T(8,128)(2,1)} fusion(bf16[32,64,1,256]{3,1,2,0:T(8,128)(2,1)} %param.7, bf16[32,64]{0,1:T(8,128)(2,1)S(1)} %copy.23), kind=kLoop, calls=%fused_computation.52 | loop fusion | flops 524288 | bytes 2101248 | tf_op jit(solution)/shard_map/mul | solution.py:80
  3.7 19.6 %all-to-all-start.1 = ((bf16[32,64,256]{2,0,1:T(8,128)(2,1)}), bf16[32,64,256]{2,0,1:T(8,128)(2,1)}, u32[]{:S(2)}, u32[]{:S(2)}) async-start(bf16[32,64,256]{2,0,1:T(8,128)(2,1)} %bitcast_multiply_fusion), calls=%async_computation.1 | async-start | bytes 2097152 | tf_op jit(solution)/shard_map/all_to_all | solution.py:82
  23.3 0.7 copy.21
  24.0 4.3 %negate_convert_fusion = (bf16[512,512]{1,0:T(8,128)(2,1)S(1)}, bf16[512,512]{1,0:T(8,128)(2,1)S(1)}) fusion(), kind=kLoop, calls=%fused_computation.53 | loop fusion | flops 4456448 | bytes 1048576 | tf_op jit(solution)/shard_map/convert.5
  28.4 29.4 %all_gather.3 = bf16[128,8,192]{2,1,0:T(8,128)(2,1)} all-gather(bf16[16,8,192]{2,1,0:T(8,128)(2,1)S(1)} %copy-done.1), channel_id=1, replica_groups=mesh['tm'=64,'tmpl'=8] {'tmpl'}, dimensions={0}, use_global_device_ids=true | all-gather | bytes 442368 | tf_op jit(solution)/shard_map/all_gather | solution.py:96
  57.8 14.5 %all-to-all-start = ((bf16[32,64,1]{0,2,1:T(2,128)(2,1)}), bf16[32,64,1]{0,2,1:T(2,128)(2,1)S(1)}, u32[]{:S(2)}, u32[]{:S(2)}) async-start(bf16[32,64,1]{0,2,1:T(2,128)(2,1)} %copy.21), calls=%async_computation | async-start | bytes 65536 | tf_op jit(solution)/shard_map/all_to_all | solution.py:83
  72.2 7.5 %collective-permute-start = (bf16[2048,256]{1,0:T(8,128)(2,1)}, bf16[2048,256]{1,0:T(8,128)(2,1)}, u32[]{:S(2)}, u32[]{:S(2)}) collective-permute-start(bf16[2048,256]{1,0:T(8,128)(2,1)} %bitcast.14), channel_id=1, source_target_pairs={{1,0},{2,1},{3,2},{4,3},{5,4},{6,5},{7,6},{8,7},{9,8},{10,9},{11,1... | collective-permute-start | bytes 3145736 | tf_op jit(solution)/shard_map/ppermute | solution.py:18
  79.8 1.7 %convolution_convert_fusion.1 = bf16[1024,1024]{0,1:T(8,128)(2,1)S(1)} fusion(bf16[128,8,192]{2,1,0:T(8,128)(2,1)} %all_gather.3, bf16[512,512]{1,0:T(8,128)(2,1)S(1)} %get-tuple-element.152, bf16[512,512]{1,0:T(8,128)(2,1)S(1)} %get-tuple-element.153), kind=kOutput, calls=%fused_computation.42 | convolution fusion | flops 404488192 | bytes 3538944 | tf_op jit(solution)/shard_map/dot_general | solution.py:38
  81.5 2.2 %negate_convert_fusion.1 = (bf16[512,256]{1,0:T(8,128)(2,1)S(1)}, bf16[512,256]{1,0:T(8,128)(2,1)S(1)}) fusion(), kind=kLoop, calls=%fused_computation.66 | loop fusion | flops 2228224 | bytes 524288 | tf_op jit(solution)/shard_map/convert.3
  83.9 0.7 reshape.63
  84.8 1.6 %multiply_reduce_fusion.2 = f32[64,32]{1,0:T(8,128)S(1)} fusion(bf16[32,64,256]{2,0,1:T(8,128)(2,1)} %all-to-all-done.1), kind=kLoop, calls=%fused_computation.41 | loop fusion | flops 1570816 | bytes 1056768 | tf_op jit(solution)/shard_map/reduce_sum | solution.py:89
  86.4 5.9 %collective-permute-done = bf16[2048,256]{1,0:T(8,128)(2,1)} collective-permute-done((bf16[2048,256]{1,0:T(8,128)(2,1)}, bf16[2048,256]{1,0:T(8,128)(2,1)}, u32[]{:S(2)}, u32[]{:S(2)}) %collective-permute-start) | collective-permute-done | bytes 1048608 | tf_op jit(solution)/shard_map/ppermute | solution.py:18
  92.4 6.0 %convolution_convert_fusion = bf16[2048,1024]{1,0:T(8,128)(2,1)} fusion(bf16[2048,256]{1,0:T(8,128)(2,1)} %collective-permute-done, bf16[2048,256]{1,0:T(8,128)(2,1)} %bitcast.14, f32[2048]{0:T(1024)S(1)} %convert_multiply_fusion.4, bf16[512,512]{1,0:T(8,128)(2,1)S(1)} %get-tuple-element.152, bf16[512,512]{1,0:T(8,128)(2,1)} %copy-done), kind=kOutput, calls=%fused_computation.36 | convolution fusion | flops 2157969408 | bytes 7348224 | tf_op jit(solution)/shard_map/dot_general | solution.py:93
  98.4 54.1 %while.12 = (s32[]{:T(128)}, f32[8,16,256]{2,1,0:T(8,128)}, s32[8,16,8]{2,1,0:T(8,128)S(1)}, bf16[2048]{0:T(1024)(128)(2,1)S(1)}, bf16[2048,1024]{1,0:T(8,128)(2...) while((s32[]{:T(128)}, f32[8,16,256]{2,1,0:T(8,128)}, ...), condition=%wide.region_5.6_spmd, body=%wide.region_1.5_spmd.sunk | while | flops 548458624 | bytes 6656885 | solution.py:103
  98.9 3.0 %convolution_bitcast_fusion.5 = f32[16,8,1024]{2,1,0:T(8,128)S(1)} fusion(bf16[2048,1024]{1,0:T(8,128)(2,1)} %get-tuple-element.233, s32[128]{0:T(128)S(1)} %eq.59), kind=kOutput, calls=%fused_computation.clone.1 | convolution fusion | flops 537133056 | bytes 4719104 | tf_op jit(solution)/shard_map/while/body/eval_jaxpr/dot_general | solution.py:48
  101.9 0.8 constant_dynamic-slice_fusion.4
  102.7 1.5 multiply_reduce_fusion.4
  104.3 0.8 fusion.55
  105.6 3.0 %convolution_bitcast_fusion.5 = f32[16,8,1024]{2,1,0:T(8,128)S(1)} fusion(bf16[2048,1024]{1,0:T(8,128)(2,1)} %get-tuple-element.233, s32[128]{0:T(128)S(1)} %eq.59), kind=kOutput, calls=%fused_computation.clone.1 | convolution fusion | flops 537133056 | bytes 4719104 | tf_op jit(solution)/shard_map/while/body/eval_jaxpr/dot_general | solution.py:48
  108.6 0.8 constant_dynamic-slice_fusion.4
  109.5 1.5 multiply_reduce_fusion.4
  111.1 0.8 fusion.55
  112.0 0.3 convolution_bitcast_fusion.4
  112.4 3.0 %convolution_bitcast_fusion.5 = f32[16,8,1024]{2,1,0:T(8,128)S(1)} fusion(bf16[2048,1024]{1,0:T(8,128)(2,1)} %get-tuple-element.233, s32[128]{0:T(128)S(1)} %eq.59), kind=kOutput, calls=%fused_computation.clone.1 | convolution fusion | flops 537133056 | bytes 4719104 | tf_op jit(solution)/shard_map/while/body/eval_jaxpr/dot_general | solution.py:48
  115.4 0.8 constant_dynamic-slice_fusion.4
  116.2 1.5 multiply_reduce_fusion.4
  117.8 0.8 fusion.55
  119.2 3.0 %convolution_bitcast_fusion.5 = f32[16,8,1024]{2,1,0:T(8,128)S(1)} fusion(bf16[2048,1024]{1,0:T(8,128)(2,1)} %get-tuple-element.233, s32[128]{0:T(128)S(1)} %eq.59), kind=kOutput, calls=%fused_computation.clone.1 | convolution fusion | flops 537133056 | bytes 4719104 | tf_op jit(solution)/shard_map/while/body/eval_jaxpr/dot_general | solution.py:48
  122.2 0.8 constant_dynamic-slice_fusion.4
  123.0 1.5 multiply_reduce_fusion.4
  124.6 0.8 fusion.55
  125.9 3.0 %convolution_bitcast_fusion.5 = f32[16,8,1024]{2,1,0:T(8,128)S(1)} fusion(bf16[2048,1024]{1,0:T(8,128)(2,1)} %get-tuple-element.233, s32[128]{0:T(128)S(1)} %eq.59), kind=kOutput, calls=%fused_computation.clone.1 | convolution fusion | flops 537133056 | bytes 4719104 | tf_op jit(solution)/shard_map/while/body/eval_jaxpr/dot_general | solution.py:48
  128.9 0.8 constant_dynamic-slice_fusion.4
  129.8 1.5 multiply_reduce_fusion.4
  131.4 0.8 fusion.55
  132.7 3.0 %convolution_bitcast_fusion.5 = f32[16,8,1024]{2,1,0:T(8,128)S(1)} fusion(bf16[2048,1024]{1,0:T(8,128)(2,1)} %get-tuple-element.233, s32[128]{0:T(128)S(1)} %eq.59), kind=kOutput, calls=%fused_computation.clone.1 | convolution fusion | flops 537133056 | bytes 4719104 | tf_op jit(solution)/shard_map/while/body/eval_jaxpr/dot_general | solution.py:48
  135.7 0.8 constant_dynamic-slice_fusion.4
  136.5 1.5 multiply_reduce_fusion.4
  138.1 0.8 fusion.55
  139.5 3.0 %convolution_bitcast_fusion.5 = f32[16,8,1024]{2,1,0:T(8,128)S(1)} fusion(bf16[2048,1024]{1,0:T(8,128)(2,1)} %get-tuple-element.233, s32[128]{0:T(128)S(1)} %eq.59), kind=kOutput, calls=%fused_computation.clone.1 | convolution fusion | flops 537133056 | bytes 4719104 | tf_op jit(solution)/shard_map/while/body/eval_jaxpr/dot_general | solution.py:48
  142.4 0.8 constant_dynamic-slice_fusion.4
  143.3 1.5 multiply_reduce_fusion.4
  144.9 0.8 fusion.55
  146.2 3.0 %convolution_bitcast_fusion.5 = f32[16,8,1024]{2,1,0:T(8,128)S(1)} fusion(bf16[2048,1024]{1,0:T(8,128)(2,1)} %get-tuple-element.233, s32[128]{0:T(128)S(1)} %eq.59), kind=kOutput, calls=%fused_computation.clone.1 | convolution fusion | flops 537133056 | bytes 4719104 | tf_op jit(solution)/shard_map/while/body/eval_jaxpr/dot_general | solution.py:48
  149.2 0.8 constant_dynamic-slice_fusion.4
  150.1 1.5 multiply_reduce_fusion.4
  151.7 0.8 fusion.55
  (90 shorter events, 6.1 us)
Async XLA Ops:
  0.0 28.4 %copy-start.1 = (bf16[16,8,192]{2,1,0:T(8,128)(2,1)S(1)}, bf16[16,8,192]{2,1,0:T(8,128)(2,1)}, u32[]{:S(2)}) copy-start(bf16[16,8,192]{2,1,0:T(8,128)(2,1)} %param.9) | copy-start | bytes 147460
  3.7 80.1 %copy-start.2 = (s32[128,8]{0,1:T(8,128)S(1)}, s32[128,8]{0,1:T(8,128)}, u32[]{:S(2)}) copy-start(s32[128,8]{0,1:T(8,128)} %param.10) | copy-start | bytes 12292
  3.7 80.2 %copy-start.3 = (s32[128,8]{0,1:T(8,128)S(1)}, s32[128,8]{0,1:T(8,128)}, u32[]{:S(2)}) copy-start(s32[128,8]{0,1:T(8,128)} %param.11) | copy-start | bytes 12292
  3.7 54.1 %all-to-all-start.1 = ((bf16[32,64,256]{2,0,1:T(8,128)(2,1)}), bf16[32,64,256]{2,0,1:T(8,128)(2,1)}, u32[]{:S(2)}, u32[]{:S(2)}) async-start(bf16[32,64,256]{2,0,1:T(8,128)(2,1)} %bitcast_multiply_fusion), calls=%async_computation.1 | async-start | bytes 2097152 | tf_op jit(solution)/shard_map/all_to_all | solution.py:82
  28.4 55.3 %copy-start = (bf16[512,512]{1,0:T(8,128)(2,1)}, bf16[512,512]{1,0:T(8,128)(2,1)S(1)}, u32[]{:S(2)}) copy-start(bf16[512,512]{1,0:T(8,128)(2,1)S(1)} %get-tuple-element.153) | copy-start | bytes 1572868
  57.8 26.8 %all-to-all-start = ((bf16[32,64,1]{0,2,1:T(2,128)(2,1)}), bf16[32,64,1]{0,2,1:T(2,128)(2,1)S(1)}, u32[]{:S(2)}, u32[]{:S(2)}) async-start(bf16[32,64,1]{0,2,1:T(2,128)(2,1)} %copy.21), calls=%async_computation | async-start | bytes 65536 | tf_op jit(solution)/shard_map/all_to_all | solution.py:83
  72.2 20.1 %collective-permute-start = (bf16[2048,256]{1,0:T(8,128)(2,1)}, bf16[2048,256]{1,0:T(8,128)(2,1)}, u32[]{:S(2)}, u32[]{:S(2)}) collective-permute-start(bf16[2048,256]{1,0:T(8,128)(2,1)} %bitcast.14), channel_id=1, source_target_pairs={{1,0},{2,1},{3,2},{4,3},{5,4},{6,5},{7,6},{8,7},{9,8},{10,9},{11,1... | collective-permute-start | bytes 3145736 | tf_op jit(solution)/shard_map/ppermute | solution.py:18
where the time goes:
time: 154 us; the launch traced here: 152 us
  starting transfers between devices  41.6 us (27%)
  matrix products  40.4 us (26%)
  blocking collectives  29.4 us (19%)
  other arithmetic  24.5 us (16%)
  local copies, waits for them, and re-layouts  10.3 us (7%)
  waiting for transfers between devices  5.94 us (4%)
    all_gather x1, blocking collectives, shards(): lax.all_gather(templates, 'tmpl', axis=0, tiled=True)  29.4 us
    dot_general x8, matrix products, network_stack(): jnp.dot(selector, spectra, preferred_element_type=jnp.float32)  23.6 us
    all_to_all x1, starting transfers between devices, shards(): lax.all_to_all(masked, 'tm', split_axis=1, concat_axis=0, tiled=True)  19.6 us
    all_to_all x1, starting transfers between devices, shards(): lax.all_to_all(flags, 'tm', split_axis=1, concat_axis=0, tiled=True)  14.5 us
    reduce_sum x8, other arithmetic, network_stack(): jnp.sum(weight[:, :, None] * (prod_real * cosine - prod_imag * sine_part)...  11.7 us
    ppermute x1, starting transfers between devices, shifted(): return lax.ppermute(value, axis, pairs)  7.51 us
    another operation x2, other arithmetic  6.54 us
    dot_general x8, matrix products, network_stack(): series = jnp.dot(joined, inverse, preferred_element_type=jnp.float32)  6.35 us
  transfers between devices with their start and end apart: 3, of which 1 were waited for; matrix products, arithmetic and copies ran while one was open for 8% of the time, Pallas kernels for 0%

commit v1 on v0

v1 whole, which is shorter than its diff:
```python
import functools
import math

import jax
import jax.numpy as jnp
import numpy as np
from jax import lax
from jax.experimental import pallas as pl
from jax.experimental.pallas import tpu as pltpu
from jax.sharding import PartitionSpec as P

L = 192
SMAX = 64
CAP = 24
GROUP = 16
MISSING = 4096.0
LIMIT = 3e38

epsilon = 1e-05


def cosine_rows(span, width):
    half = span // 2
    frequency = np.arange(half)[:, None]
    sample = np.arange(width)[None, :]
    angle = (frequency * sample % span) * (2.0 * math.pi / span)
    real = np.cos(angle)
    imag = -np.sin(angle)
    imag[0] = np.cos(math.pi * np.arange(width))
    return real, imag


def forward_rows(span, width):
    real, imag = cosine_rows(span, width)
    return jnp.asarray(np.concatenate([real, imag]).astype(jnp.bfloat16))


def inverse_rows(span, width):
    real, imag = cosine_rows(span, width)
    real, imag = 2.0 * real, 2.0 * imag
    real[0] *= 0.5
    imag[0] *= 0.5
    table = np.concatenate([real, imag])
    flip = np.where(np.arange(span // 2) % 2 == 0, 1.0, -1.0)
    after = table * np.concatenate([flip, flip])[:, None]
    return (
        jnp.asarray(table.T.astype(jnp.bfloat16)),
        jnp.asarray(after.T.astype(jnp.bfloat16)),
    )


def phase_tables(span, moves):
    angle = (np.arange(span // 2)[:, None] * np.arange(moves)[None, :] % span) * (2.0 * math.pi / span)
    parts = []
    for value in (np.cos(angle), np.sin(angle)):
        high = value.astype(jnp.bfloat16)
        parts.append(high)
        parts.append((value - high.astype(np.float64)).astype(jnp.bfloat16))
    return jnp.asarray(np.concatenate(parts))


def dot(a, b):
    return jnp.dot(a, b, preferred_element_type=jnp.float32)


def dot_rows(a, b):
    return lax.dot_general(a, b, (((1,), (1,)), ((), ())), preferred_element_type=jnp.float32)


def iota(shape, dim):
    return lax.broadcasted_iota(jnp.int32, shape, dim)


def to_row(column, eye):
    return jnp.sum(jnp.where(eye, column, 0.0), axis=0, keepdims=True)


def to_column(row, eye):
    return jnp.sum(jnp.where(eye, row, 0.0), axis=1, keepdims=True)


def pack_kernel(avail_ref, raw_ref, out_ref):
    count = raw_ref.shape[0]
    part = raw_ref.shape[1]
    windows = avail_ref.shape[1]
    status = avail_ref[...].astype(jnp.float32)
    flags = jnp.transpose(status).astype(jnp.bfloat16)
    place = (iota((count, 128), 0) == iota((count, 128), 1)).astype(jnp.bfloat16)
    before = (iota((count, 128), 0) < iota((count, 128), 1)).astype(jnp.bfloat16)
    first = pl.program_id(0) * part
    pick = (iota((part, windows), 1) == iota((part, windows), 0) + first).astype(jnp.bfloat16)
    flags = dot(pick, flags).astype(jnp.bfloat16)
    present = dot(flags, place)
    code = jnp.where(present > 0.5, dot(flags, before), MISSING)
    lanes = count * GROUP
    spread = (iota((128, lanes), 0) == iota((128, lanes), 1) // GROUP).astype(jnp.bfloat16)
    for block in range(part // GROUP):
        own = code[block * GROUP : (block + 1) * GROUP]
        wide = dot(own.astype(jnp.bfloat16), spread)
        wide = jnp.where(iota((GROUP, lanes), 1) % GROUP == iota((GROUP, lanes), 0), wide, -1.0)
        slot = iota((GROUP, CAP, lanes), 1).astype(jnp.float32)
        mover = jnp.where(wide[:, None, :] == slot, 1.0, 0.0).reshape(GROUP * CAP, lanes).astype(jnp.bfloat16)
        waves = raw_ref[:, block * GROUP : (block + 1) * GROUP, :].reshape(lanes, raw_ref.shape[2])
        moved = dot(mover, waves)
        for window in range(GROUP):
            rows = moved[window * CAP : (window + 1) * CAP]
            extra = jnp.broadcast_to(own[window : window + 1], (8, 128))
            out_ref[block * GROUP + window] = jnp.concatenate([rows[:, :128], rows[:, 128:], extra], axis=0).astype(
                jnp.bfloat16
            )


def wave_kernel(who_ref, near_ref, next_ref, far_ref, other_ref, moves_ref, lists_ref, forward_ref, phase_ref,
                real_ref, imag_ref, top_ref, block_ref, lane_ref, rows_ref):
    yl = who_ref[0] // 2
    core = who_ref[0] % 2
    listed, group = near_ref.shape[1], near_ref.shape[2]
    columns = listed * 128
    rows_ref[...] = jnp.zeros_like(rows_ref)
    for owner in range(8):
        away = lax.bitwise_xor(owner // 2, yl)
        cross = lax.bitwise_xor(owner % 2, core)
        sources = ((0, near_ref, 0), (1, next_ref, 0), (2, far_ref, 0), (3, far_ref, 1))
        for distance, ref, at in sources:
            @pl.when(jnp.logical_and(cross == 0, away == distance))
            def _():
                for q in range(listed):
                    rows_ref[q * 128 + owner * group : q * 128 + (owner + 1) * group, 0:L] = ref[at, q]
            @pl.when(jnp.logical_and(cross == 1, away == distance))
            def _():
                for q in range(listed):
                    rows_ref[q * 128 + owner * group : q * 128 + (owner + 1) * group, 0:L] = other_ref[distance, q]
    half = forward_ref.shape[0] // 2
    eye = iota((128, 128), 0) == iota((128, 128), 1)
    for q in range(listed):
        cols = slice(q * 128, (q + 1) * 128)
        spectrum = dot_rows(forward_ref[...], rows_ref[cols, :])
        move = moves_ref[q : q + 1, :]
        chosen = (iota((SMAX, 128), 0) == move).astype(jnp.bfloat16)
        angles = dot(phase_ref[...], chosen)
        cosine = angles[:half] + angles[half : 2 * half]
        sine = angles[2 * half : 3 * half] + angles[3 * half :]
        real, imag = spectrum[:half], spectrum[half:]
        sign = 1.0 - 2.0 * (move % 2).astype(jnp.float32)
        zero = iota((half, 128), 0) == 0
        real_ref[:, cols] = jnp.where(zero, real, real * cosine + imag * sine)
        imag_ref[:, cols] = jnp.where(zero, 0.0, real * sine - imag * cosine)
        top_ref[:, cols] = jnp.broadcast_to(imag[0:1] * sign, (8, 128))
        station = to_column(lists_ref[q : q + 1, :].astype(jnp.float32), eye).astype(jnp.int32)
        block_ref[cols, :] = (iota((128, 128), 1) == station // 32).astype(jnp.bfloat16)
        lane = iota((128, 128), 1)
        lane_ref[cols, :] = jnp.logical_or(lane == station % 32, lane == 64).astype(jnp.bfloat16)


def pick_kernel(got_ref, block_ref, lane_ref, scaled_ref, level_ref, factor_ref):
    blocks = got_ref.shape[0]
    slots = blocks * CAP
    codes = got_ref[:, 2 * CAP : 2 * CAP + 8, :].astype(jnp.float32)[:, 0, :]
    start = iota((blocks, 128), 0).astype(jnp.float32) * CAP
    codes = jnp.where(iota((blocks, 128), 1) == 64, start, codes).astype(jnp.bfloat16)
    codes = jnp.concatenate([codes, jnp.zeros((128 - blocks, 128), jnp.bfloat16)], axis=0)
    low = got_ref[:, 0:CAP, :].reshape(slots, 128)
    high = got_ref[:, CAP : 2 * CAP, :].reshape(slots, 128)
    waves = jnp.concatenate([low, high], axis=1)
    width = waves.shape[1]
    eye = iota((128, 128), 0) == iota((128, 128), 1)
    total = jnp.zeros((1, 128), jnp.float32)
    listed = block_ref.shape[0] // 128
    for q in range(listed):
        cols = slice(q * 128, (q + 1) * 128)
        target = jnp.sum(
            dot(block_ref[cols, :], codes) * lane_ref[cols, :].astype(jnp.float32), axis=1, keepdims=True
        )
        chosen = jnp.where(iota((128, slots), 1).astype(jnp.float32) == target, 1.0, 0.0).astype(jnp.bfloat16)
        rows = dot(chosen, waves)
        power = jnp.sum(rows * rows, axis=1, keepdims=True) * (1.0 / width)
        present = jnp.where(target < MISSING * 0.5, 1.0, 0.0)
        safe = jnp.minimum(power, LIMIT) + epsilon
        scaled_ref[cols, :] = (rows * lax.rsqrt(safe)).astype(jnp.bfloat16)
        level_ref[q : q + 1, :] = to_row(jnp.sqrt(safe), eye)
        factor_ref[q : q + 1, :] = to_row(present * lax.rsqrt(power + epsilon), eye)
        total = total + to_row(present, eye)
    factor_ref[listed : listed + 8, :] = jnp.broadcast_to(1.0 / jnp.maximum(total, 1.0), (8, 128))


def own_kernel(scaled_ref, factor_ref, real_ref, imag_ref, top_ref, forward_ref, inverse_ref, mixed_ref, out_ref):
    half = real_ref.shape[0]
    listed = real_ref.shape[1] // 128
    sums = [jnp.zeros((half, 128), jnp.float32), jnp.zeros((half, 128), jnp.float32)]
    zero = iota((half, 128), 0) == 0
    for q in range(listed):
        cols = slice(q * 128, (q + 1) * 128)
        spectrum = dot_rows(forward_ref[...], scaled_ref[cols, :])
        real, imag = spectrum[:half], spectrum[half:]
        wave_real, wave_imag = real_ref[:, cols], imag_ref[:, cols]
        mixed_real = wave_real * real - wave_imag * imag
        straight = jnp.where(zero, top_ref[0:1, cols], wave_real)
        mixed_imag = straight * imag + wave_imag * real
        mixed_ref[:half, cols] = mixed_real.astype(jnp.bfloat16)
        mixed_ref[half:, cols] = mixed_imag.astype(jnp.bfloat16)
        weight = jnp.where(factor_ref[q : q + 1, :] > 0.0, 1.0, 0.0)
        sums[0] = sums[0] + weight * mixed_real
        sums[1] = sums[1] + weight * mixed_imag
    joined = jnp.concatenate(sums, axis=0).astype(jnp.bfloat16)
    span = 2 * half
    series = dot(inverse_ref[...], joined) * (factor_ref[listed : listed + 1, :] * (1.0 / span))
    out_ref[...] = jnp.transpose(series)


def after_kernel(mixed_ref, level_ref, factor_ref, inverse_ref, out_ref):
    span = mixed_ref.shape[0]
    listed = mixed_ref.shape[1] // 128
    weights = level_ref[...] * factor_ref[0:listed, :]
    total = jnp.zeros((span, 128), jnp.float32)
    for q in range(listed):
        total = total + weights[q : q + 1, :] * mixed_ref[:, q * 128 : (q + 1) * 128].astype(jnp.float32)
    series = dot(inverse_ref[...], total.astype(jnp.bfloat16)) * (factor_ref[listed : listed + 1, :] * (1.0 / span))
    out_ref[...] = jnp.transpose(series).astype(jnp.bfloat16)


def params():
    return pltpu.CompilerParams(vmem_limit_bytes=48 * 1024 * 1024)


def pack(status, waves):
    count, windows, width = waves.shape
    part = windows // 2
    rows = 2 * CAP + 8
    return pl.pallas_call(
        pack_kernel,
        out_shape=jax.ShapeDtypeStruct((windows, rows, 128), jnp.bfloat16),
        grid=(windows // part,),
        in_specs=[
            pl.BlockSpec((count, windows), lambda i: (0, 0)),
            pl.BlockSpec((count, part, width), lambda i: (0, i, 0)),
        ],
        out_specs=pl.BlockSpec((part, rows, 128), lambda i: (i, 0, 0)),
        compiler_params=params(),
        name="pack",
    )(status, waves)


def vmem(n):
    return [pl.BlockSpec(memory_space=pltpu.VMEM)] * n


def wave(who, near, after, far, other, moves, lists, forward, phases):
    half = forward.shape[0] // 2
    columns = lists.shape[0] * 128
    return pl.pallas_call(
        wave_kernel,
        out_shape=(
            jax.ShapeDtypeStruct((half, columns), jnp.float32),
            jax.ShapeDtypeStruct((half, columns), jnp.float32),
            jax.ShapeDtypeStruct((8, columns), jnp.float32),
            jax.ShapeDtypeStruct((columns, 128), jnp.bfloat16),
            jax.ShapeDtypeStruct((columns, 128), jnp.bfloat16),
        ),
        in_specs=[pl.BlockSpec(memory_space=pltpu.SMEM)] + vmem(8),
        out_specs=tuple(vmem(5)),
        scratch_shapes=[pltpu.VMEM((columns, forward.shape[1]), jnp.bfloat16)],
        compiler_params=params(),
        name="wave",
    )(who, near, after, far, other, moves, lists, forward, phases)


def pick(got, block, lane):
    columns = block.shape[0]
    listed = columns // 128
    return pl.pallas_call(
        pick_kernel,
        out_shape=(
            jax.ShapeDtypeStruct((columns, 256), jnp.bfloat16),
            jax.ShapeDtypeStruct((listed, 128), jnp.float32),
            jax.ShapeDtypeStruct((listed + 8, 128), jnp.float32),
        ),
        in_specs=vmem(3),
        out_specs=tuple(vmem(3)),
        compiler_params=params(),
        name="pick",
    )(got, block, lane)


def own_part(scaled, factor, real, imag, top, forward, inverse):
    span, columns = forward.shape[0], real.shape[1]
    return pl.pallas_call(
        own_kernel,
        out_shape=(
            jax.ShapeDtypeStruct((span, columns), jnp.bfloat16),
            jax.ShapeDtypeStruct((128, inverse.shape[0]), jnp.float32),
        ),
        in_specs=vmem(7),
        out_specs=tuple(vmem(2)),
        compiler_params=params(),
        name="own_part",
    )(scaled, factor, real, imag, top, forward, inverse)


def after_part(mixed, level, factor, inverse):
    return pl.pallas_call(
        after_kernel,
        out_shape=jax.ShapeDtypeStruct((128, inverse.shape[0]), jnp.bfloat16),
        in_specs=vmem(4),
        out_specs=vmem(1)[0],
        compiler_params=params(),
        name="after_part",
    )(mixed, level, factor, inverse)


def exchange(value, bit):
    return lax.ppermute(value, "tmpl", [(i, i ^ bit) for i in range(8)])


def shifted(value, by):
    axis = ("tm", "tmpl")
    count = lax.axis_size(axis)
    return lax.ppermute(value, axis, [(i, i + by) for i in range(count) if 0 <= i + by < count])


def shards(raw, avail, templates, stations, shifts):
    width = raw.shape[3]
    span = width + L + SMAX
    forward = forward_rows(span, width)
    inverse, inverse_after = inverse_rows(span, width)
    phases = phase_tables(span, SMAX)
    near = jnp.transpose(templates, (1, 0, 2))[None]
    after = exchange(near, 2)
    pair = jnp.concatenate([near, after])
    payload = pack(jnp.transpose(avail[:, 0, :]), raw[:, :, 0, :])
    got = lax.all_to_all(payload, "tm", split_axis=0, concat_axis=0, tiled=True)
    far = exchange(pair, 4)
    other = exchange(jnp.concatenate([pair, far]), 1)
    who = lax.axis_index("tmpl").reshape(1)
    real, imag, top, block, lane = wave(
        who, near, after, far, other, jnp.transpose(shifts), jnp.transpose(stations), forward, phases
    )
    scaled, level, factor = pick(got, block, lane)
    before = shifted(factor, 1)
    mixed, own = own_part(scaled, factor, real, imag, top, forward, inverse)
    late = shifted(after_part(mixed, level, before, inverse_after), -1)
    return own + late.astype(jnp.float32)


def solution(mesh):
    return jax.shard_map(
        shards,
        mesh=mesh,
        in_specs=(
            P("tm", None, "tmpl", None),
            P(None, "tmpl", "tm"),
            P("tmpl", None, None),
            P(),
            P(),
        ),
        out_specs=P(None, ("tm", "tmpl")),
        check_vma=False,
    )
```

time: 154 us -> 84.4 us (0.55)
  matrix products: 40.4 us -> 0 us
  waiting for transfers between devices: 5.94 us -> 36.2 us
  blocking collectives: 29.4 us -> 0 us
  other arithmetic: 24.5 us -> 0.75 us
  starting transfers between devices: 41.6 us -> 29.9 us
  Pallas kernels: 0 us -> 8.28 us
  local copies, waits for them, and re-layouts: 10.3 us -> 8.51 us
    dot_general x26 -> x0, matrix products: 40.4 us -> none  [the longest x8 23.6 us: network_stack(): jnp.dot(selector, spectra, preferred_element_type=jnp.float32)]
    ppermute x1 -> x5, waiting for transfers between devices: 5.93 us -> 36.2 us  [the longest x3 28.4 us: exchange(): return lax.ppermute(value, 'tmpl', [(i, i ^ bit) for i in range(8)])]
    all_gather x1 -> x0, blocking collectives: 29.4 us -> none  [shards(): lax.all_gather(templates, 'tmpl', axis=0, tiled=True)]
    all_to_all x2 -> x1, starting transfers between devices: 34.1 us -> 19.4 us  [shards(): got = lax.all_to_all(payload, 'tm', split_axis=0, concat_axis=0, tiled=True)]
    reduce_sum x17 -> x0, other arithmetic: 14.2 us -> none  [the longest x8 11.7 us: network_stack(): jnp.sum(weight[:, :, None] * (prod_real * cosine - prod_imag * sine_part)...]
    unnamed x9 -> x35, local copies, waits for them, and re-layouts: 0.12 us -> 8.51 us
    pallas_call x0 -> x5, Pallas kernels: none -> 8.28 us  [the longest x1 2.46 us: pack(): pl.pallas_call(pack_kernel, out_shape=jax.ShapeDtypeStruct((windows, rows...]
    another operation x2 -> x0, other arithmetic: 6.54 us -> none
  transfers between devices with their start and end apart: 3 -> 6, of which waited for: 1 -> 5; matrix products, arithmetic and copies ran while one was open for 8% -> 0% of each run, Pallas kernels for 0% -> 4%
where the time goes in v1:
time: 84.4 us; the launch traced here: 83.9 us
  waiting for transfers between devices  36.2 us (43%)
  starting transfers between devices  29.9 us (35%)
  local copies, waits for them, and re-layouts  8.51 us (10%)
  Pallas kernels  8.28 us (10%)
    ppermute x3, waiting for transfers between devices, exchange(): return lax.ppermute(value, 'tmpl', [(i, i ^ bit) for i in range(8)])  28.4 us
    all_to_all x1, starting transfers between devices, shards(): got = lax.all_to_all(payload, 'tm', split_axis=0, concat_axis=0, tiled=True)  19.4 us
    unnamed x35, local copies, waits for them, and re-layouts  8.51 us
    ppermute x2, waiting for transfers between devices, shifted(): lax.ppermute(value, axis, [(i, i + by) for i in range(count) if 0 <= i +...  7.85 us
    ppermute x3, starting transfers between devices, exchange(): return lax.ppermute(value, 'tmpl', [(i, i ^ bit) for i in range(8)])  6.56 us
    ppermute x2, starting transfers between devices, shifted(): lax.ppermute(value, axis, [(i, i + by) for i in range(count) if 0 <= i +...  3.96 us
    pallas_call x1, Pallas kernels, pack(): pl.pallas_call(pack_kernel, out_shape=jax.ShapeDtypeStruct((windows, rows...  2.46 us
    pallas_call x1, Pallas kernels, pick(): pl.pallas_call(pick_kernel, out_shape=(jax.ShapeDtypeStruct((columns, 256...  2.18 us
  transfers between devices with their start and end apart: 6, of which 5 were waited for; matrix products, arithmetic and copies ran while one was open for 0% of the time, Pallas kernels for 4%

profile of v1, /device:TPU:6, one launch (start us, length us, event | category | flops | bytes accessed | tf_op | source)
XLA Modules:
  0.0 83.9 jit_solution(14591734785120727497)
XLA Ops:
  0.0 0.0 copy-start.1
  0.0 1.2 %copy-done.1 = bf16[32,64,1,256]{3,1,2,0:T(8,128)(2,1)S(1)} copy-done((bf16[32,64,1,256]{3,1,2,0:T(8,128)(2,1)S(1)}, bf16[32,64,1,256]{3,1,2,0:T(8,128)(2,1)}, u32[]{:S(2)}) %copy-start.1) | copy-done | bytes 1048600
  1.2 0.0 copy-start.13
  1.2 0.7 copy-done.13
  1.9 2.5 %pack.1 = bf16[64,56,128]{2,1,0:T(8,128)(2,1)} custom-call(s32[32,64]{1,0:T(8,128)S(1)} %bitcast.17, bf16[32,64,256]{2,1,0:T(8,128)(2,1)S(1)} %bitcast.12), custom_call_target="tpu_custom_call" | custom-call | tf_op jit(solution)/shard_map/pack/pallas_call | solution.py:229
  4.4 0.0 copy-start.16
  4.4 19.4 %all-to-all-start = ((bf16[64,56,128]{2,1,0:T(8,128)(2,1)}), bf16[64,56,128]{2,1,0:T(8,128)(2,1)S(1)}, u32[]{:S(2)}, u32[]{:S(2)}) async-start(bf16[64,56,128]{2,1,0:T(8,128)(2,1)} %pack.1), calls=%async_computation | async-start | bytes 1835008 | tf_op jit(solution)/shard_map/all_to_all | solution.py:330
  23.8 0.0 copy-done.16
  23.9 2.6 %collective-permute-start = (bf16[1,8,16,192]{3,2,1,0:T(8,128)(2,1)S(1)}, bf16[1,8,16,192]{3,2,1,0:T(8,128)(2,1)S(1)}, u32[]{:S(2)}, u32[]{:S(2)}) collective-permute-start(bf16[1,8,16,192]{3,2,1,0:T(8,128)(2,1)S(1)} %bitcast.13), channel_id=1, source_target_pairs={{0,2},{1,3},{2,0},{3,1},{4,6},{5,7},{6,4},{7,5},{8,10},{9,11},{10,... | collective-permute-start | bytes 147464 | tf_op jit(solution)/shard_map/ppermute | solution.py:311
  26.4 19.1 %collective-permute-done.next_ref = bf16[1,8,16,192]{3,2,1,0:T(8,128)(2,1)S(1)} collective-permute-done((bf16[1,8,16,192]{3,2,1,0:T(8,128)(2,1)S(1)}, bf16[1,8,16,192]{3,2,1,0:T(8,128)(2,1)S(1)}, u32[]{:S(2)}, u32[]{:S(2)}) %collective-permute-start) | collective-permute-done | bytes 49184 | tf_op jit(solution)/shard_map/ppermute | solution.py:311
  45.6 0.0 copy-start
  45.6 2.1 %collective-permute-start.1 = (bf16[2,8,16,192]{3,2,1,0:T(8,128)(2,1)S(1)}, bf16[2,8,16,192]{3,2,1,0:T(8,128)(2,1)S(1)}, u32[]{:S(2)}, u32[]{:S(2)}) collective-permute-start(bf16[2,8,16,192]{3,2,1,0:T(8,128)(2,1)S(1)} %pad_maximum_fusion.1), channel_id=1, source_target_pairs={{0,4},{1,5},{2,6},{3,7},{4,0},{5,1},{6,2},{7,3},{8,12},{9,13},{10,... | collective-permute-start | bytes 294920 | tf_op jit(solution)/shard_map/ppermute | solution.py:311
  47.6 7.8 %collective-permute-done.1.far_ref = bf16[2,8,16,192]{3,2,1,0:T(8,128)(2,1)S(1)} collective-permute-done((bf16[2,8,16,192]{3,2,1,0:T(8,128)(2,1)S(1)}, bf16[2,8,16,192]{3,2,1,0:T(8,128)(2,1)S(1)}, u32[]{:S(2)}, u32[]{:S(2)}) %collective-permute-start.1) | collective-permute-done | bytes 98336 | tf_op jit(solution)/shard_map/ppermute | solution.py:311
  55.5 0.1 pad_maximum_fusion
  55.5 1.9 %collective-permute-start.2 = (bf16[4,8,16,192]{3,2,1,0:T(8,128)(2,1)S(1)}, bf16[4,8,16,192]{3,2,1,0:T(8,128)(2,1)S(1)}, u32[]{:S(2)}, u32[]{:S(2)}) collective-permute-start(bf16[4,8,16,192]{3,2,1,0:T(8,128)(2,1)S(1)} %pad_maximum_fusion), channel_id=1, source_target_pairs={{0,1},{1,0},{2,3},{3,2},{4,5},{5,4},{6,7},{7,6},{8,9},{9,8},{10,11... | collective-permute-start | bytes 589832 | tf_op jit(solution)/shard_map/ppermute | solution.py:311
  57.5 0.0 copy-start.15
  57.5 0.0 copy-start.14
  57.5 1.5 %collective-permute-done.2.other_ref = bf16[4,8,16,192]{3,2,1,0:T(8,128)(2,1)S(1)} collective-permute-done((bf16[4,8,16,192]{3,2,1,0:T(8,128)(2,1)S(1)}, bf16[4,8,16,192]{3,2,1,0:T(8,128)(2,1)S(1)}, u32[]{:S(2)}, u32[]{:S(2)}) %collective-permute-start.2) | collective-permute-done | bytes 196640 | tf_op jit(solution)/shard_map/ppermute | solution.py:311
  59.0 0.0 copy-start.9
  59.0 0.7 copy-done.9
  59.7 0.0 copy-done
  59.7 0.0 copy-done.15
  59.7 0.0 copy-done.14
  59.7 0.0 copy-start.4
  59.7 0.9 %copy-done.4 = bf16[1024,64]{1,0:T(8,128)(2,1)S(1)} copy-done((bf16[1024,64]{1,0:T(8,128)(2,1)S(1)}, bf16[1024,64]{1,0:T(8,128)(2,1)}, u32[]{:S(2)}) %copy-start.4) | copy-done | bytes 131096
  60.6 0.0 copy-start.10
  60.6 0.9 %copy-done.10 = bf16[4,8,16,192]{3,2,1,0:T(8,128)(2,1)S(1)} copy-done((bf16[4,8,16,192]{3,2,1,0:T(8,128)(2,1)S(1)}, bf16[4,8,16,192]{3,2,1,0:T(8,128)(2,1)}, u32[]{:S(2)}) %copy-start.10) | copy-done | bytes 196632
  61.6 2.0 %wave.1 = (f32[256,1024]{1,0:T(8,128)S(1)}, f32[256,1024]{1,0:T(8,128)S(1)}, f32[8,1024]{1,0:T(8,128)S(1)}, bf16[1024,128]{1,0:T(8,128)(2,1)S(1)}, bf16[1024,128]{1,0:T(8,128)(2,1)S(1)}) custom-call(s32[1]{0:T(128)} %bitcast.3.who_ref, bf16[1,8,16,192]{3,2,1,0:T(8,128)(2,1)S(1)} %bitcast.16, bf16[1,8,16,192]{3,2,1,0:T(8,128)(2,1)S(1)} %collective-permute-done.next_ref, ...), custom_call_target="tpu_custom_call" | custom-call | tf_op jit(solution)/shard_map/wave/pallas_call | solution.py:250
  63.6 0.0 copy-start.5
  63.6 0.7 copy-done.5
  64.3 0.0 copy-start.7
  64.3 0.7 copy-done.7
  65.0 0.6 copy-done.11
  65.6 0.0 all-to-all-done.got_ref
  65.6 0.9 %copy-done.6 = bf16[1024,128]{1,0:T(8,128)(2,1)S(1)} copy-done((bf16[1024,128]{1,0:T(8,128)(2,1)S(1)}, bf16[1024,128]{1,0:T(8,128)(2,1)}, u32[]{:S(2)}) %copy-start.6) | copy-done | bytes 262168
  66.6 0.9 %copy-done.8 = bf16[1024,128]{1,0:T(8,128)(2,1)S(1)} copy-done((bf16[1024,128]{1,0:T(8,128)(2,1)S(1)}, bf16[1024,128]{1,0:T(8,128)(2,1)}, u32[]{:S(2)}) %copy-start.8) | copy-done | bytes 262168
  67.5 2.2 %pick.1 = (bf16[1024,256]{1,0:T(8,128)(2,1)S(1)}, f32[8,128]{1,0:T(8,128)S(1)}, f32[16,128]{1,0:T(8,128)S(1)}) custom-call(bf16[64,56,128]{2,1,0:T(8,128)(2,1)S(1)} %all-to-all-done.got_ref, bf16[1024,128]{1,0:T(8,128)(2,1)S(1)} %copy-done.6, bf16[1024,128]{1,0:T(8,128)(2,1)S(1)} %copy-done.8), custom_call_target="tpu_custom_call" | custom-call | tf_op jit(solution)/shard_map/pick/pallas_call | solution.py:270
  69.7 2.0 %collective-permute-start.3 = (f32[16,128]{1,0:T(8,128)S(1)}, f32[16,128]{1,0:T(8,128)S(1)}, u32[]{:S(2)}, u32[]{:S(2)}) collective-permute-start(f32[16,128]{1,0:T(8,128)S(1)} %get-tuple-element.18.factor_ref), channel_id=1, source_target_pairs={{0,1},{1,2},{2,3},{3,4},{4,5},{5,6},{6,7},{7,8},{8,9},{9,10},{10,1... | collective-permute-start | bytes 24584 | tf_op jit(solution)/shard_map/ppermute | solution.py:317
  71.8 0.0 copy-done.2
  71.8 0.0 copy-done.12
  71.8 0.0 copy-start.3
  71.8 1.1 %own_part.1 = (bf16[512,1024]{1,0:T(8,128)(2,1)S(1)}, f32[128,256]{1,0:T(8,128)S(1)}) custom-call(bf16[1024,256]{1,0:T(8,128)(2,1)S(1)} %get-tuple-element.17.scaled_ref, f32[16,128]{1,0:T(8,128)S(1)} %get-tuple-element.18.factor_ref, f32[256,1024]{1,0:T(8,128)S(1)} %get-tuple-element.19.real_ref, f32[256,1024]{1,0:T(8,128)S(1)} %get-tuple-element.20.imag_ref, ...), custom_call_target="tpu_custom_call" | custom-call | tf_op jit(solution)/shard_map/own_part/pallas_call | solution.py:286
  73.0 6.0 %collective-permute-done.3.factor_ref = f32[16,128]{1,0:T(8,128)S(1)} collective-permute-done((f32[16,128]{1,0:T(8,128)S(1)}, f32[16,128]{1,0:T(8,128)S(1)}, u32[]{:S(2)}, u32[]{:S(2)}) %collective-permute-start.3) | collective-permute-done | bytes 8224 | tf_op jit(solution)/shard_map/ppermute | solution.py:317
  78.9 0.0 copy-done.3
  78.9 0.5 after_part.1
  79.4 1.9 %collective-permute-start.4 = (bf16[128,256]{1,0:T(8,128)(2,1)S(1)}, bf16[128,256]{1,0:T(8,128)(2,1)S(1)}, u32[]{:S(2)}, u32[]{:S(2)}) collective-permute-start(bf16[128,256]{1,0:T(8,128)(2,1)S(1)} %after_part.1), channel_id=1, source_target_pairs={{1,0},{2,1},{3,2},{4,3},{5,4},{6,5},{7,6},{8,7},{9,8},{10,9},{11,1... | collective-permute-start | bytes 196616 | tf_op jit(solution)/shard_map/ppermute | solution.py:317
  81.3 1.9 %collective-permute-done.4 = bf16[128,256]{1,0:T(8,128)(2,1)S(1)} collective-permute-done((bf16[128,256]{1,0:T(8,128)(2,1)S(1)}, bf16[128,256]{1,0:T(8,128)(2,1)S(1)}, u32[]{:S(2)}, u32[]{:S(2)}) %collective-permute-start.4) | collective-permute-done | bytes 65568 | tf_op jit(solution)/shard_map/ppermute | solution.py:317
  83.2 0.7 convert_add_fusion
  (7 shorter events, 0.0 us)
Async XLA Ops:
  0.0 1.2 %copy-start.1 = (bf16[32,64,1,256]{3,1,2,0:T(8,128)(2,1)S(1)}, bf16[32,64,1,256]{3,1,2,0:T(8,128)(2,1)}, u32[]{:S(2)}) copy-start(bf16[32,64,1,256]{3,1,2,0:T(8,128)(2,1)} %param.9) | copy-start | bytes 3145732
  1.2 0.7 copy-start.13
  4.4 19.4 %copy-start.16 = (bf16[16,8,192]{2,1,0:T(8,128)(2,1)S(1)}, bf16[16,8,192]{2,1,0:T(8,128)(2,1)}, u32[]{:S(2)}) copy-start(bf16[16,8,192]{2,1,0:T(8,128)(2,1)} %param.11) | copy-start | bytes 147460
  4.4 61.2 %all-to-all-start = ((bf16[64,56,128]{2,1,0:T(8,128)(2,1)}), bf16[64,56,128]{2,1,0:T(8,128)(2,1)S(1)}, u32[]{:S(2)}, u32[]{:S(2)}) async-start(bf16[64,56,128]{2,1,0:T(8,128)(2,1)} %pack.1), calls=%async_computation | async-start | bytes 1835008 | tf_op jit(solution)/shard_map/all_to_all | solution.py:330
  23.9 21.7 %collective-permute-start = (bf16[1,8,16,192]{3,2,1,0:T(8,128)(2,1)S(1)}, bf16[1,8,16,192]{3,2,1,0:T(8,128)(2,1)S(1)}, u32[]{:S(2)}, u32[]{:S(2)}) collective-permute-start(bf16[1,8,16,192]{3,2,1,0:T(8,128)(2,1)S(1)} %bitcast.13), channel_id=1, source_target_pairs={{0,2},{1,3},{2,0},{3,1},{4,6},{5,7},{6,4},{7,5},{8,10},{9,11},{10,... | collective-permute-start | bytes 147464 | tf_op jit(solution)/shard_map/ppermute | solution.py:311
  45.6 14.1 %copy-start = (bf16[512,256]{1,0:T(8,128)(2,1)S(1)}, bf16[512,256]{1,0:T(8,128)(2,1)}, u32[]{:S(2)}) copy-start(bf16[512,256]{1,0:T(8,128)(2,1)} %constant.12.clone.forward_ref) | copy-start | bytes 786436
  45.6 9.9 %collective-permute-start.1 = (bf16[2,8,16,192]{3,2,1,0:T(8,128)(2,1)S(1)}, bf16[2,8,16,192]{3,2,1,0:T(8,128)(2,1)S(1)}, u32[]{:S(2)}, u32[]{:S(2)}) collective-permute-start(bf16[2,8,16,192]{3,2,1,0:T(8,128)(2,1)S(1)} %pad_maximum_fusion.1), channel_id=1, source_target_pairs={{0,4},{1,5},{2,6},{3,7},{4,0},{5,1},{6,2},{7,3},{8,12},{9,13},{10,... | collective-permute-start | bytes 294920 | tf_op jit(solution)/shard_map/ppermute | solution.py:311
  55.5 3.4 %collective-permute-start.2 = (bf16[4,8,16,192]{3,2,1,0:T(8,128)(2,1)S(1)}, bf16[4,8,16,192]{3,2,1,0:T(8,128)(2,1)S(1)}, u32[]{:S(2)}, u32[]{:S(2)}) collective-permute-start(bf16[4,8,16,192]{3,2,1,0:T(8,128)(2,1)S(1)} %pad_maximum_fusion), channel_id=1, source_target_pairs={{0,1},{1,0},{2,3},{3,2},{4,5},{5,4},{6,7},{7,6},{8,9},{9,8},{10,11... | collective-permute-start | bytes 589832 | tf_op jit(solution)/shard_map/ppermute | solution.py:311
  57.5 2.2 %copy-start.15 = (s32[128,8]{0,1:T(8,128)S(1)}, s32[128,8]{0,1:T(8,128)}, u32[]{:S(2)}) copy-start(s32[128,8]{0,1:T(8,128)} %param.12) | copy-start | bytes 12292
  57.5 2.2 %copy-start.14 = (s32[128,8]{0,1:T(8,128)S(1)}, s32[128,8]{0,1:T(8,128)}, u32[]{:S(2)}) copy-start(s32[128,8]{0,1:T(8,128)} %param.13) | copy-start | bytes 12292
  59.0 0.7 copy-start.9
  59.7 1.0 %copy-start.4 = (bf16[1024,64]{1,0:T(8,128)(2,1)S(1)}, bf16[1024,64]{1,0:T(8,128)(2,1)}, u32[]{:S(2)}) copy-start(bf16[1024,64]{1,0:T(8,128)(2,1)} %constant.15.clone.phase_ref) | copy-start | bytes 393220
  60.6 0.9 %copy-start.10 = (bf16[4,8,16,192]{3,2,1,0:T(8,128)(2,1)S(1)}, bf16[4,8,16,192]{3,2,1,0:T(8,128)(2,1)}, u32[]{:S(2)}) copy-start(bf16[4,8,16,192]{3,2,1,0:T(8,128)(2,1)} %copy-done.9) | copy-start | bytes 589828
  63.6 0.7 copy-start.5
  64.3 0.7 copy-start.7
  65.0 0.6 copy-start.11
  65.6 1.0 %copy-start.6 = (bf16[1024,128]{1,0:T(8,128)(2,1)S(1)}, bf16[1024,128]{1,0:T(8,128)(2,1)}, u32[]{:S(2)}) copy-start(bf16[1024,128]{1,0:T(8,128)(2,1)} %copy-done.5) | copy-start | bytes 786436
  66.6 0.9 %copy-start.8 = (bf16[1024,128]{1,0:T(8,128)(2,1)S(1)}, bf16[1024,128]{1,0:T(8,128)(2,1)}, u32[]{:S(2)}) copy-start(bf16[1024,128]{1,0:T(8,128)(2,1)} %copy-done.7) | copy-start | bytes 786436
  67.5 4.2 %copy-start.2 = (bf16[256,512]{1,0:T(8,128)(2,1)S(1)}, bf16[256,512]{1,0:T(8,128)(2,1)}, u32[]{:S(2)}) copy-start(bf16[256,512]{1,0:T(8,128)(2,1)} %constant.13.clone.inverse_ref) | copy-start | bytes 786436
  67.5 4.3 %copy-start.12 = (f32[8,1024]{1,0:T(8,128)S(1)}, f32[8,1024]{1,0:T(8,128)}, u32[]{:S(2)}) copy-start(f32[8,1024]{1,0:T(8,128)} %copy-done.11) | copy-start | bytes 98308
  69.7 9.2 %collective-permute-start.3 = (f32[16,128]{1,0:T(8,128)S(1)}, f32[16,128]{1,0:T(8,128)S(1)}, u32[]{:S(2)}, u32[]{:S(2)}) collective-permute-start(f32[16,128]{1,0:T(8,128)S(1)} %get-tuple-element.18.factor_ref), channel_id=1, source_target_pairs={{0,1},{1,2},{2,3},{3,4},{4,5},{5,6},{6,7},{7,8},{8,9},{9,10},{10,1... | collective-permute-start | bytes 24584 | tf_op jit(solution)/shard_map/ppermute | solution.py:317
  71.8 7.1 %copy-start.3 = (bf16[256,512]{1,0:T(8,128)(2,1)S(1)}, bf16[256,512]{1,0:T(8,128)(2,1)}, u32[]{:S(2)}) copy-start(bf16[256,512]{1,0:T(8,128)(2,1)} %constant.14.clone.inverse_ref) | copy-start | bytes 786436
  79.4 3.8 %collective-permute-start.4 = (bf16[128,256]{1,0:T(8,128)(2,1)S(1)}, bf16[128,256]{1,0:T(8,128)(2,1)S(1)}, u32[]{:S(2)}, u32[]{:S(2)}) collective-permute-start(bf16[128,256]{1,0:T(8,128)(2,1)S(1)} %after_part.1), channel_id=1, source_target_pairs={{1,0},{2,1},{3,2},{4,3},{5,4},{6,5},{7,6},{8,7},{9,8},{10,9},{11,1... | collective-permute-start | bytes 196616 | tf_op jit(solution)/shard_map/ppermute | solution.py:317

commit v2 on v1

--- a/solution.py
+++ b/solution.py
@@ -79,76 +79,58 @@
     return jnp.sum(jnp.where(eye, row, 0.0), axis=1, keepdims=True)
 
 
-def pack_kernel(avail_ref, raw_ref, out_ref):
-    count = raw_ref.shape[0]
-    part = raw_ref.shape[1]
-    windows = avail_ref.shape[1]
-    status = avail_ref[...].astype(jnp.float32)
-    flags = jnp.transpose(status).astype(jnp.bfloat16)
+def pack_kernel(avail_ref, raw_ref, out_ref, waves_ref, done_ref, get_sem, put_sem):
+    count, windows, width = raw_ref.shape
+    parts = windows // GROUP
+
+    def fetch(part):
+        rows = pl.ds(part * GROUP, GROUP)
+        return pltpu.make_async_copy(raw_ref.at[:, rows, :], waves_ref.at[part], get_sem.at[part])
+
+    def store(part):
+        rows = pl.ds(part * GROUP, GROUP)
+        return pltpu.make_async_copy(done_ref.at[rows], out_ref.at[rows], put_sem.at[part])
+
+    for part in range(parts):
+        fetch(part).start()
+    flags = jnp.transpose(avail_ref[...].astype(jnp.float32)).astype(jnp.bfloat16)
     place = (iota((count, 128), 0) == iota((count, 128), 1)).astype(jnp.bfloat16)
     before = (iota((count, 128), 0) < iota((count, 128), 1)).astype(jnp.bfloat16)
-    first = pl.program_id(0) * part
-    pick = (iota((part, windows), 1) == iota((part, windows), 0) + first).astype(jnp.bfloat16)
-    flags = dot(pick, flags).astype(jnp.bfloat16)
-    present = dot(flags, place)
-    code = jnp.where(present > 0.5, dot(flags, before), MISSING)
+    code = jnp.where(dot(flags, place) > 0.5, dot(flags, before), MISSING)
     lanes = count * GROUP
     spread = (iota((128, lanes), 0) == iota((128, lanes), 1) // GROUP).astype(jnp.bfloat16)
-    for block in range(part // GROUP):
-        own = code[block * GROUP : (block + 1) * GROUP]
+    slot = iota((GROUP, CAP, lanes), 1).astype(jnp.float32)
+    for part in range(parts):
+        own = code[part * GROUP : (part + 1) * GROUP]
         wide = dot(own.astype(jnp.bfloat16), spread)
         wide = jnp.where(iota((GROUP, lanes), 1) % GROUP == iota((GROUP, lanes), 0), wide, -1.0)
-        slot = iota((GROUP, CAP, lanes), 1).astype(jnp.float32)
         mover = jnp.where(wide[:, None, :] == slot, 1.0, 0.0).reshape(GROUP * CAP, lanes).astype(jnp.bfloat16)
-        waves = raw_ref[:, block * GROUP : (block + 1) * GROUP, :].reshape(lanes, raw_ref.shape[2])
-        moved = dot(mover, waves)
+        fetch(part).wait()
+        moved = dot(mover, waves_ref[part].reshape(lanes, width))
         for window in range(GROUP):
             rows = moved[window * CAP : (window + 1) * CAP]
             extra = jnp.broadcast_to(own[window : window + 1], (8, 128))
-            out_ref[block * GROUP + window] = jnp.concatenate([rows[:, :128], rows[:, 128:], extra], axis=0).astype(
+            done_ref[part * GROUP + window] = jnp.concatenate([rows[:, :128], rows[:, 128:], extra], axis=0).astype(
                 jnp.bfloat16
             )
-
-
-def wave_kernel(who_ref, near_ref, next_ref, far_ref, other_ref, moves_ref, lists_ref, forward_ref, phase_ref,
-                real_ref, imag_ref, top_ref, block_ref, lane_ref, rows_ref):
-    yl = who_ref[0] // 2
-    core = who_ref[0] % 2
-    listed, group = near_ref.shape[1], near_ref.shape[2]
-    columns = listed * 128
-    rows_ref[...] = jnp.zeros_like(rows_ref)
-    for owner in range(8):
-        away = lax.bitwise_xor(owner // 2, yl)
-        cross = lax.bitwise_xor(owner % 2, core)
-        sources = ((0, near_ref, 0), (1, next_ref, 0), (2, far_ref, 0), (3, far_ref, 1))
-        for distance, ref, at in sources:
-            @pl.when(jnp.logical_and(cross == 0, away == distance))
-            def _():
-                for q in range(listed):
-                    rows_ref[q * 128 + owner * group : q * 128 + (owner + 1) * group, 0:L] = ref[at, q]
-            @pl.when(jnp.logical_and(cross == 1, away == distance))
-            def _():
-                for q in range(listed):
-                    rows_ref[q * 128 + owner * group : q * 128 + (owner + 1) * group, 0:L] = other_ref[distance, q]
-    half = forward_ref.shape[0] // 2
+        store(part).start()
+    for part in range(parts):
+        store(part).wait()
+
+
+def table_kernel(moves_ref, lists_ref, phase_ref, cosine_ref, sine_ref, sign_ref, block_ref, lane_ref):
+    half = cosine_ref.shape[0]
     eye = iota((128, 128), 0) == iota((128, 128), 1)
-    for q in range(listed):
+    for q in range(moves_ref.shape[0]):
         cols = slice(q * 128, (q + 1) * 128)
-        spectrum = dot_rows(forward_ref[...], rows_ref[cols, :])
         move = moves_ref[q : q + 1, :]
-        chosen = (iota((SMAX, 128), 0) == move).astype(jnp.bfloat16)
-        angles = dot(phase_ref[...], chosen)
-        cosine = angles[:half] + angles[half : 2 * half]
-        sine = angles[2 * half : 3 * half] + angles[3 * half :]
-        real, imag = spectrum[:half], spectrum[half:]
-        sign = 1.0 - 2.0 * (move % 2).astype(jnp.float32)
-        zero = iota((half, 128), 0) == 0
-        real_ref[:, cols] = jnp.where(zero, real, real * cosine + imag * sine)
-        imag_ref[:, cols] = jnp.where(zero, 0.0, real * sine - imag * cosine)
-        top_ref[:, cols] = jnp.broadcast_to(imag[0:1] * sign, (8, 128))
+        angles = dot(phase_ref[...], (iota((SMAX, 128), 0) == move).astype(jnp.bfloat16))
+        cosine_ref[:, cols] = angles[:half] + angles[half : 2 * half]
+        sine_ref[:, cols] = angles[2 * half : 3 * half] + angles[3 * half :]
+        sign_ref[q : q + 1, :] = 1.0 - 2.0 * (move % 2).astype(jnp.float32)
         station = to_column(lists_ref[q : q + 1, :].astype(jnp.float32), eye).astype(jnp.int32)
-        block_ref[cols, :] = (iota((128, 128), 1) == station // 32).astype(jnp.bfloat16)
         lane = iota((128, 128), 1)
+        block_ref[cols, :] = (lane == station // 32).astype(jnp.bfloat16)
         lane_ref[cols, :] = jnp.logical_or(lane == station % 32, lane == 64).astype(jnp.bfloat16)
 
 
@@ -183,18 +165,36 @@
     factor_ref[listed : listed + 8, :] = jnp.broadcast_to(1.0 / jnp.maximum(total, 1.0), (8, 128))
 
 
-def own_kernel(scaled_ref, factor_ref, real_ref, imag_ref, top_ref, forward_ref, inverse_ref, mixed_ref, out_ref):
-    half = real_ref.shape[0]
-    listed = real_ref.shape[1] // 128
+def own_kernel(who_ref, pair_ref, right_ref, cross_ref, left_ref, scaled_ref, factor_ref, cosine_ref, sine_ref,
+               sign_ref, forward_ref, inverse_ref, mixed_ref, out_ref, rows_ref):
+    half = cosine_ref.shape[0]
+    listed = cosine_ref.shape[1] // 128
+    span = 2 * half
+    chip, core = who_ref[0] // 2, who_ref[0] % 2
+    group = pair_ref.shape[2]
+    rows_ref[:, 128:] = jnp.zeros((listed * 128, rows_ref.shape[1] - 128), jnp.bfloat16)
+    for away, ref in enumerate((pair_ref, right_ref, cross_ref, left_ref)):
+        for other in range(2):
+            owner = lax.rem(chip + away, 4) * 2 + lax.rem(core + other, 2)
+            for q in range(listed):
+                at = pl.ds(pl.multiple_of(q * 128 + owner * group, group), group)
+                rows_ref[at, 0:128] = ref[other, q]
+                tail = ref[other, listed + q % 4]
+                rows_ref[at, 128:L] = tail[:, : L - 128] if q < 4 else tail[:, L - 128 :]
     sums = [jnp.zeros((half, 128), jnp.float32), jnp.zeros((half, 128), jnp.float32)]
     zero = iota((half, 128), 0) == 0
     for q in range(listed):
         cols = slice(q * 128, (q + 1) * 128)
+        template = dot_rows(forward_ref[...], rows_ref[cols, :])
         spectrum = dot_rows(forward_ref[...], scaled_ref[cols, :])
         real, imag = spectrum[:half], spectrum[half:]
-        wave_real, wave_imag = real_ref[:, cols], imag_ref[:, cols]
+        cosine, sine = cosine_ref[:, cols], sine_ref[:, cols]
+        wave_real = template[:half] * cosine + template[half:] * sine
+        wave_imag = template[:half] * sine - template[half:] * cosine
+        wave_real = jnp.where(zero, template[:half], wave_real)
+        wave_imag = jnp.where(zero, 0.0, wave_imag)
+        straight = jnp.where(zero, template[half:] * sign_ref[q : q + 1, :], wave_real)
         mixed_real = wave_real * real - wave_imag * imag
-        straight = jnp.where(zero, top_ref[0:1, cols], wave_real)
         mixed_imag = straight * imag + wave_imag * real
         mixed_ref[:half, cols] = mixed_real.astype(jnp.bfloat16)
         mixed_ref[half:, cols] = mixed_imag.astype(jnp.bfloat16)
@@ -202,7 +202,6 @@
         sums[0] = sums[0] + weight * mixed_real
         sums[1] = sums[1] + weight * mixed_imag
     joined = jnp.concatenate(sums, axis=0).astype(jnp.bfloat16)
-    span = 2 * half
     series = dot(inverse_ref[...], joined) * (factor_ref[listed : listed + 1, :] * (1.0 / span))
     out_ref[...] = jnp.transpose(series)
 
@@ -219,49 +218,51 @@
 
 
 def params():
-    return pltpu.CompilerParams(vmem_limit_bytes=48 * 1024 * 1024)
+    return pltpu.CompilerParams(vmem_limit_bytes=16 * 1024 * 1024)
+
+
+def vmem(n):
+    return [pl.BlockSpec(memory_space=pltpu.VMEM)] * n
 
 
 def pack(status, waves):
     count, windows, width = waves.shape
-    part = windows // 2
-    rows = 2 * CAP + 8
+    parts = windows // GROUP
+    shape = (windows, 2 * CAP + 8, 128)
     return pl.pallas_call(
         pack_kernel,
-        out_shape=jax.ShapeDtypeStruct((windows, rows, 128), jnp.bfloat16),
-        grid=(windows // part,),
-        in_specs=[
-            pl.BlockSpec((count, windows), lambda i: (0, 0)),
-            pl.BlockSpec((count, part, width), lambda i: (0, i, 0)),
+        out_shape=jax.ShapeDtypeStruct(shape, jnp.bfloat16),
+        in_specs=vmem(1) + [pl.BlockSpec(memory_space=pl.ANY)],
+        out_specs=pl.BlockSpec(memory_space=pl.ANY),
+        scratch_shapes=[
+            pltpu.VMEM((parts, count, GROUP, width), jnp.bfloat16),
+            pltpu.VMEM(shape, jnp.bfloat16),
+            pltpu.SemaphoreType.DMA((parts,)),
+            pltpu.SemaphoreType.DMA((parts,)),
         ],
-        out_specs=pl.BlockSpec((part, rows, 128), lambda i: (i, 0, 0)),
         compiler_params=params(),
         name="pack",
     )(status, waves)
 
 
-def vmem(n):
-    return [pl.BlockSpec(memory_space=pltpu.VMEM)] * n
-
-
-def wave(who, near, after, far, other, moves, lists, forward, phases):
-    half = forward.shape[0] // 2
-    columns = lists.shape[0] * 128
-    return pl.pallas_call(
-        wave_kernel,
+def tables(moves, lists, phases):
+    half = phases.shape[0] // 4
+    listed = lists.shape[0]
+    columns = listed * 128
+    return pl.pallas_call(
+        table_kernel,
         out_shape=(
             jax.ShapeDtypeStruct((half, columns), jnp.float32),
             jax.ShapeDtypeStruct((half, columns), jnp.float32),
-            jax.ShapeDtypeStruct((8, columns), jnp.float32),
+            jax.ShapeDtypeStruct((listed, 128), jnp.float32),
             jax.ShapeDtypeStruct((columns, 128), jnp.bfloat16),
             jax.ShapeDtypeStruct((columns, 128), jnp.bfloat16),
         ),
-        in_specs=[pl.BlockSpec(memory_space=pltpu.SMEM)] + vmem(8),
+        in_specs=vmem(3),
         out_specs=tuple(vmem(5)),
-        scratch_shapes=[pltpu.VMEM((columns, forward.shape[1]), jnp.bfloat16)],
-        compiler_params=params(),
-        name="wave",
-    )(who, near, after, far, other, moves, lists, forward, phases)
+        compiler_params=params(),
+        name="tables",
+    )(moves, lists, phases)
 
 
 def pick(got, block, lane):
@@ -281,19 +282,20 @@
     )(got, block, lane)
 
 
-def own_part(scaled, factor, real, imag, top, forward, inverse):
-    span, columns = forward.shape[0], real.shape[1]
+def own_part(who, blocks, scaled, factor, cosine, sine, sign, forward, inverse):
+    span, columns = forward.shape[0], cosine.shape[1]
     return pl.pallas_call(
         own_kernel,
         out_shape=(
             jax.ShapeDtypeStruct((span, columns), jnp.bfloat16),
             jax.ShapeDtypeStruct((128, inverse.shape[0]), jnp.float32),
         ),
-        in_specs=vmem(7),
+        in_specs=[pl.BlockSpec(memory_space=pltpu.SMEM)] + vmem(11),
         out_specs=tuple(vmem(2)),
+        scratch_shapes=[pltpu.VMEM((columns, forward.shape[1]), jnp.bfloat16)],
         compiler_params=params(),
         name="own_part",
-    )(scaled, factor, real, imag, top, forward, inverse)
+    )(who, *blocks, scaled, factor, cosine, sine, sign, forward, inverse)
 
 
 def after_part(mixed, level, factor, inverse):
@@ -307,8 +309,17 @@
     )(mixed, level, factor, inverse)
 
 
-def exchange(value, bit):
-    return lax.ppermute(value, "tmpl", [(i, i ^ bit) for i in range(8)])
+def other_core(value):
+    return lax.ppermute(value, "tmpl", [(i, i ^ 1) for i in range(8)])
+
+
+def along_ring(value, by):
+    pairs = []
+    for i in range(lax.axis_size(("tm", "tmpl"))):
+        tm, chip, core = i // 8, i // 2 % 4, i % 2
+        to = (tm % 2 * 4 + chip + by) % 8
+        pairs.append((i, (tm // 2 * 2 + to // 4) * 8 + to % 4 * 2 + core))
+    return lax.ppermute(value, ("tm", "tmpl"), pairs)
 
 
 def shifted(value, by):
@@ -323,22 +334,22 @@
     forward = forward_rows(span, width)
     inverse, inverse_after = inverse_rows(span, width)
     phases = phase_tables(span, SMAX)
-    near = jnp.transpose(templates, (1, 0, 2))[None]
-    after = exchange(near, 2)
-    pair = jnp.concatenate([near, after])
+    own = jnp.transpose(templates, (1, 0, 2))
+    tail = jnp.concatenate([own[:4, :, 128:], own[4:, :, 128:]], axis=2)
+    own = jnp.concatenate([own[:, :, :128], tail], axis=0)
+    other = other_core(own)
     payload = pack(jnp.transpose(avail[:, 0, :]), raw[:, :, 0, :])
+    payload, other = lax.optimization_barrier((payload, other))
     got = lax.all_to_all(payload, "tm", split_axis=0, concat_axis=0, tiled=True)
-    far = exchange(pair, 4)
-    other = exchange(jnp.concatenate([pair, far]), 1)
+    pair = jnp.stack([own, other])
+    blocks = (pair, along_ring(pair, -1), along_ring(pair, 2), along_ring(pair, 1))
     who = lax.axis_index("tmpl").reshape(1)
-    real, imag, top, block, lane = wave(
-        who, near, after, far, other, jnp.transpose(shifts), jnp.transpose(stations), forward, phases
-    )
+    cosine, sine, sign, block, lane = tables(jnp.transpose(shifts), jnp.transpose(stations), phases)
     scaled, level, factor = pick(got, block, lane)
     before = shifted(factor, 1)
-    mixed, own = own_part(scaled, factor, real, imag, top, forward, inverse)
+    mixed, stack = own_part(who, blocks, scaled, factor, cosine, sine, sign, forward, inverse)
     late = shifted(after_part(mixed, level, before, inverse_after), -1)
-    return own + late.astype(jnp.float32)
+    return stack + late.astype(jnp.float32)
 
 
 def solution(mesh):

time: 84.4 us -> 78 us (0.924)
  the two profiles are of different devices: /device:TPU:6 before, /device:TPU:2 now
where the time goes in v2:
time: 78 us; the launch traced here: 77.4 us
  starting transfers between devices  37.2 us (48%)
  waiting for transfers between devices  22 us (28%)
  Pallas kernels  9.19 us (12%)
  local copies, waits for them, and re-layouts  7.32 us (9%)
  other arithmetic  1.49 us (2%)
    all_to_all x1, starting transfers between devices, shards(): got = lax.all_to_all(payload, 'tm', split_axis=0, concat_axis=0, tiled=True)  19.1 us
    all_to_all x1, waiting for transfers between devices, shards(): got = lax.all_to_all(payload, 'tm', split_axis=0, concat_axis=0, tiled=True)  17.7 us
    ppermute x3, starting transfers between devices, along_ring(): return lax.ppermute(value, ('tm', 'tmpl'), pairs)  8.76 us
    ppermute x2, starting transfers between devices, shifted(): lax.ppermute(value, axis, [(i, i + by) for i in range(count) if 0 <= i +...  7.42 us
    unnamed x25, local copies, waits for them, and re-layouts  7.3 us
    ppermute x2, waiting for transfers between devices, shifted(): lax.ppermute(value, axis, [(i, i + by) for i in range(count) if 0 <= i +...  4.26 us
    pallas_call x1, Pallas kernels, own_part(): pl.pallas_call(own_kernel, out_shape=(jax.ShapeDtypeStruct((span, columns...  2.94 us
    pallas_call x1, Pallas kernels, pack(): pl.pallas_call(pack_kernel, out_shape=jax.ShapeDtypeStruct(shape, jnp.bfl...  2.62 us
  transfers between devices with their start and end apart: 7, of which 3 were waited for; matrix products, arithmetic and copies ran while one was open for 1% of the time, Pallas kernels for 11%

profile of v2, /device:TPU:2, one launch (start us, length us, event | category | flops | bytes accessed | tf_op | source)
XLA Modules:
  0.0 77.4 jit_solution(184341953000819648)
XLA Ops:
  0.0 0.9 %copy.12 = bf16[16,8,192]{2,0,1:T(8,128)(2,1)S(1)} copy(bf16[16,8,192]{2,1,0:T(8,128)(2,1)} %param.11) | data formatting | bytes 98304 | tf_op args[2]
  0.9 0.0 copy-start.9
  0.9 0.1 maximum_maximum_fusion
  1.0 1.9 %collective-permute-start = (bf16[12,16,128]{2,1,0:T(8,128)(2,1)S(1)}, bf16[12,16,128]{2,1,0:T(8,128)(2,1)S(1)}, u32[]{:S(2)}, u32[]{:S(2)}) collective-permute-start(bf16[12,16,128]{2,1,0:T(8,128)(2,1)S(1)} %maximum_maximum_fusion), channel_id=1, source_target_pairs={{0,1},{1,0},{2,3},{3,2},{4,5},{5,4},{6,7},{7,6},{8,9},{9,8},{10,11... | collective-permute-start | bytes 147464 | tf_op jit(solution)/shard_map/ppermute | solution.py:313
  2.9 0.0 copy-done.9
  2.9 0.0 copy-start
  2.9 1.2 %copy-done = bf16[32,64,1,256]{3,1,2,0:T(8,128)(2,1)S(1)} copy-done((bf16[32,64,1,256]{3,1,2,0:T(8,128)(2,1)S(1)}, bf16[32,64,1,256]{3,1,2,0:T(8,128)(2,1)}, u32[]{:S(2)}) %copy-start) | copy-done | bytes 1048600
  4.1 2.6 %pack.1 = bf16[64,56,128]{2,1,0:T(8,128)(2,1)} custom-call(s32[32,64]{1,0:T(8,128)S(1)} %bitcast.14, bf16[32,64,256]{2,1,0:T(8,128)(2,1)S(1)} %bitcast.13), custom_call_target="tpu_custom_call" | custom-call | tf_op jit(solution)/shard_map/pack/pallas_call | solution.py:232
  6.8 0.0 collective-permute-done
  6.8 19.1 %all-to-all-start = ((bf16[64,56,128]{2,1,0:T(8,128)(2,1)}), bf16[64,56,128]{2,1,0:T(8,128)(2,1)S(1)}, u32[]{:S(2)}, u32[]{:S(2)}) async-start(bf16[64,56,128]{2,1,0:T(8,128)(2,1)} %pack.1), calls=%async_computation | async-start | bytes 1835008 | tf_op jit(solution)/shard_map/all_to_all | solution.py:343
  25.9 0.0 copy-start.3
  25.9 0.1 fusion.1
  26.0 0.0 copy-start.10
  26.0 0.0 copy-start.11
  26.0 0.7 pad_maximum_fusion.pair_ref
  26.7 4.9 %collective-permute-start.1 = (bf16[2,12,16,128]{3,2,1,0:T(8,128)(2,1)}, bf16[2,12,16,128]{3,2,1,0:T(8,128)(2,1)}, u32[]{:S(2)}, u32[]{:S(2)}) collective-permute-start(bf16[2,12,16,128]{3,2,1,0:T(8,128)(2,1)} %pad_maximum_fusion.pair_ref), channel_id=1, source_target_pairs={{0,14},{1,15},{2,0},{3,1},{4,2},{5,3},{6,4},{7,5},{8,6},{9,7},{10,... | collective-permute-start | bytes 294920 | tf_op jit(solution)/shard_map/ppermute | solution.py:322
  31.6 1.9 %collective-permute-start.2 = (bf16[2,12,16,128]{3,2,1,0:T(8,128)(2,1)}, bf16[2,12,16,128]{3,2,1,0:T(8,128)(2,1)}, u32[]{:S(2)}, u32[]{:S(2)}) collective-permute-start(bf16[2,12,16,128]{3,2,1,0:T(8,128)(2,1)} %pad_maximum_fusion.pair_ref), channel_id=1, source_target_pairs={{0,4},{1,5},{2,6},{3,7},{4,8},{5,9},{6,10},{7,11},{8,12},{9,13},{1... | collective-permute-start | bytes 294920 | tf_op jit(solution)/shard_map/ppermute | solution.py:322
  33.5 1.9 %collective-permute-start.3 = (bf16[2,12,16,128]{3,2,1,0:T(8,128)(2,1)}, bf16[2,12,16,128]{3,2,1,0:T(8,128)(2,1)}, u32[]{:S(2)}, u32[]{:S(2)}) collective-permute-start(bf16[2,12,16,128]{3,2,1,0:T(8,128)(2,1)} %pad_maximum_fusion.pair_ref), channel_id=1, source_target_pairs={{0,2},{1,3},{2,4},{3,5},{4,6},{5,7},{6,8},{7,9},{8,10},{9,11},{10,... | collective-permute-start | bytes 294920 | tf_op jit(solution)/shard_map/ppermute | solution.py:322
  35.5 0.0 copy-done.3
  35.5 0.0 copy-done.10
  35.5 0.0 copy-done.11
  35.5 1.0 %tables.1 = (f32[256,1024]{1,0:T(8,128)S(1)}, f32[256,1024]{1,0:T(8,128)S(1)}, f32[8,128]{1,0:T(8,128)S(1)}, bf16[1024,128]{1,0:T(8,128)(2,1)S(1)}, bf16[1024,128]{1,0:T(8,128)(2,1)S(1)}) custom-call(s32[8,128]{1,0:T(8,128)S(1)} %bitcast.15, s32[8,128]{1,0:T(8,128)S(1)} %bitcast.16, bf16[1024,64]{1,0:T(8,128)(2,1)S(1)} %copy-done.3), custom_call_target="tpu_custom_call" | custom-call | tf_op jit(solution)/shard_map/tables/pallas_call | solution.py:252
  36.5 0.0 copy-start.5
  36.5 0.7 copy-done.5
  37.2 0.0 copy-start.7
  37.2 0.7 copy-done.7
  37.9 17.7 %all-to-all-done.got_ref = bf16[64,56,128]{2,1,0:T(8,128)(2,1)S(1)} async-done(((bf16[64,56,128]{2,1,0:T(8,128)(2,1)}), bf16[64,56,128]{2,1,0:T(8,128)(2,1)S(1)}, u32[]{:S(2)}, u32[]{:S(2)}) %all-to-all-start) | async-done | bytes 917536 | tf_op jit(solution)/shard_map/all_to_all | solution.py:343
  55.6 0.0 copy-start.6
  55.6 0.9 %copy-done.6 = bf16[1024,128]{1,0:T(8,128)(2,1)S(1)} copy-done((bf16[1024,128]{1,0:T(8,128)(2,1)S(1)}, bf16[1024,128]{1,0:T(8,128)(2,1)}, u32[]{:S(2)}) %copy-start.6) | copy-done | bytes 262168
  56.6 0.0 copy-start.8
  56.6 0.9 %copy-done.8 = bf16[1024,128]{1,0:T(8,128)(2,1)S(1)} copy-done((bf16[1024,128]{1,0:T(8,128)(2,1)S(1)}, bf16[1024,128]{1,0:T(8,128)(2,1)}, u32[]{:S(2)}) %copy-start.8) | copy-done | bytes 262168
  57.5 2.2 %pick.1 = (bf16[1024,256]{1,0:T(8,128)(2,1)S(1)}, f32[8,128]{1,0:T(8,128)S(1)}, f32[16,128]{1,0:T(8,128)S(1)}) custom-call(bf16[64,56,128]{2,1,0:T(8,128)(2,1)S(1)} %all-to-all-done.got_ref, bf16[1024,128]{1,0:T(8,128)(2,1)S(1)} %copy-done.6, bf16[1024,128]{1,0:T(8,128)(2,1)S(1)} %copy-done.8), custom_call_target="tpu_custom_call" | custom-call | tf_op jit(solution)/shard_map/pick/pallas_call | solution.py:271
  59.7 1.9 %collective-permute-start.4 = (f32[16,128]{1,0:T(8,128)S(1)}, f32[16,128]{1,0:T(8,128)S(1)}, u32[]{:S(2)}, u32[]{:S(2)}) collective-permute-start(f32[16,128]{1,0:T(8,128)S(1)} %get-tuple-element.22.factor_ref), channel_id=1, source_target_pairs={{0,1},{1,2},{2,3},{3,4},{4,5},{5,6},{6,7},{7,8},{8,9},{9,10},{10,1... | collective-permute-start | bytes 24584 | tf_op jit(solution)/shard_map/ppermute | solution.py:328
  61.6 0.0 collective-permute-done.1.right_ref
  61.6 0.0 collective-permute-done.2.cross_ref
  61.6 0.0 collective-permute-done.3.left_ref
  61.7 0.0 copy-start.1
  61.7 0.9 %copy-done.1 = bf16[512,256]{1,0:T(8,128)(2,1)S(1)} copy-done((bf16[512,256]{1,0:T(8,128)(2,1)S(1)}, bf16[512,256]{1,0:T(8,128)(2,1)}, u32[]{:S(2)}) %copy-start.1) | copy-done | bytes 262168
  62.6 0.0 copy-start.2
  62.6 0.9 %copy-done.2 = bf16[256,512]{1,0:T(8,128)(2,1)S(1)} copy-done((bf16[256,512]{1,0:T(8,128)(2,1)S(1)}, bf16[256,512]{1,0:T(8,128)(2,1)}, u32[]{:S(2)}) %copy-start.2) | copy-done | bytes 262168
  63.6 0.0 copy-start.4
  63.6 2.9 %own_part.1 = (bf16[512,1024]{1,0:T(8,128)(2,1)S(1)}, f32[128,256]{1,0:T(8,128)S(1)}) custom-call(s32[1]{0:T(128)} %bitcast.who_ref, bf16[2,12,16,128]{3,2,1,0:T(8,128)(2,1)} %pad_maximum_fusion.pair_ref, bf16[2,12,16,128]{3,2,1,0:T(8,128)(2,1)} %collective-permute-done.1.right_ref, bf16[2,12,16,128]{3,2,1,0:T(8,128)(2,1)} %collective-permute-done.2.cross_ref, ...), custom_call_target="tpu_custom_call" | custom-call | tf_op jit(solution)/shard_map/own_part/pallas_call | solution.py:287
  66.5 2.4 %collective-permute-done.4.factor_ref = f32[16,128]{1,0:T(8,128)S(1)} collective-permute-done((f32[16,128]{1,0:T(8,128)S(1)}, f32[16,128]{1,0:T(8,128)S(1)}, u32[]{:S(2)}, u32[]{:S(2)}) %collective-permute-start.4) | collective-permute-done | bytes 8224 | tf_op jit(solution)/shard_map/ppermute | solution.py:328
  68.9 0.0 copy-done.4
  68.9 0.5 after_part.1
  69.4 5.5 %collective-permute-start.5 = (bf16[128,256]{1,0:T(8,128)(2,1)S(1)}, bf16[128,256]{1,0:T(8,128)(2,1)S(1)}, u32[]{:S(2)}, u32[]{:S(2)}) collective-permute-start(bf16[128,256]{1,0:T(8,128)(2,1)S(1)} %after_part.1), channel_id=1, source_target_pairs={{1,0},{2,1},{3,2},{4,3},{5,4},{6,5},{7,6},{8,7},{9,8},{10,9},{11,1... | collective-permute-start | bytes 196616 | tf_op jit(solution)/shard_map/ppermute | solution.py:328
  74.9 1.9 %collective-permute-done.5 = bf16[128,256]{1,0:T(8,128)(2,1)S(1)} collective-permute-done((bf16[128,256]{1,0:T(8,128)(2,1)S(1)}, bf16[128,256]{1,0:T(8,128)(2,1)S(1)}, u32[]{:S(2)}, u32[]{:S(2)}) %collective-permute-start.5) | collective-permute-done | bytes 65568 | tf_op jit(solution)/shard_map/ppermute | solution.py:328
  76.8 0.7 convert_add_fusion
  (2 shorter events, 0.0 us)
Async XLA Ops:
  0.9 2.0 %copy-start.9 = (s32[64,1,32]{0,2,1:T(8,128)S(1)}, s32[64,1,32]{0,2,1:T(8,128)}, u32[]{:S(2)}) copy-start(s32[64,1,32]{0,2,1:T(8,128)} %param.10) | copy-start | bytes 24580
  1.0 5.8 %collective-permute-start = (bf16[12,16,128]{2,1,0:T(8,128)(2,1)S(1)}, bf16[12,16,128]{2,1,0:T(8,128)(2,1)S(1)}, u32[]{:S(2)}, u32[]{:S(2)}) collective-permute-start(bf16[12,16,128]{2,1,0:T(8,128)(2,1)S(1)} %maximum_maximum_fusion), channel_id=1, source_target_pairs={{0,1},{1,0},{2,3},{3,2},{4,5},{5,4},{6,7},{7,6},{8,9},{9,8},{10,11... | collective-permute-start | bytes 147464 | tf_op jit(solution)/shard_map/ppermute | solution.py:313
  2.9 1.2 %copy-start = (bf16[32,64,1,256]{3,1,2,0:T(8,128)(2,1)S(1)}, bf16[32,64,1,256]{3,1,2,0:T(8,128)(2,1)}, u32[]{:S(2)}) copy-start(bf16[32,64,1,256]{3,1,2,0:T(8,128)(2,1)} %param.9) | copy-start | bytes 3145732
  6.8 48.8 %all-to-all-start = ((bf16[64,56,128]{2,1,0:T(8,128)(2,1)}), bf16[64,56,128]{2,1,0:T(8,128)(2,1)S(1)}, u32[]{:S(2)}, u32[]{:S(2)}) async-start(bf16[64,56,128]{2,1,0:T(8,128)(2,1)} %pack.1), calls=%async_computation | async-start | bytes 1835008 | tf_op jit(solution)/shard_map/all_to_all | solution.py:343
  25.9 9.5 %copy-start.3 = (bf16[1024,64]{1,0:T(8,128)(2,1)S(1)}, bf16[1024,64]{1,0:T(8,128)(2,1)}, u32[]{:S(2)}) copy-start(bf16[1024,64]{1,0:T(8,128)(2,1)} %constant.15.clone.phase_ref) | copy-start | bytes 393220
  26.0 9.5 %copy-start.10 = (s32[128,8]{0,1:T(8,128)S(1)}, s32[128,8]{0,1:T(8,128)}, u32[]{:S(2)}) copy-start(s32[128,8]{0,1:T(8,128)} %param.13) | copy-start | bytes 12292
  26.0 9.5 %copy-start.11 = (s32[128,8]{0,1:T(8,128)S(1)}, s32[128,8]{0,1:T(8,128)}, u32[]{:S(2)}) copy-start(s32[128,8]{0,1:T(8,128)} %param.12) | copy-start | bytes 12292
  26.7 34.9 %collective-permute-start.1 = (bf16[2,12,16,128]{3,2,1,0:T(8,128)(2,1)}, bf16[2,12,16,128]{3,2,1,0:T(8,128)(2,1)}, u32[]{:S(2)}, u32[]{:S(2)}) collective-permute-start(bf16[2,12,16,128]{3,2,1,0:T(8,128)(2,1)} %pad_maximum_fusion.pair_ref), channel_id=1, source_target_pairs={{0,14},{1,15},{2,0},{3,1},{4,2},{5,3},{6,4},{7,5},{8,6},{9,7},{10,... | collective-permute-start | bytes 294920 | tf_op jit(solution)/shard_map/ppermute | solution.py:322
  31.6 30.0 %collective-permute-start.2 = (bf16[2,12,16,128]{3,2,1,0:T(8,128)(2,1)}, bf16[2,12,16,128]{3,2,1,0:T(8,128)(2,1)}, u32[]{:S(2)}, u32[]{:S(2)}) collective-permute-start(bf16[2,12,16,128]{3,2,1,0:T(8,128)(2,1)} %pad_maximum_fusion.pair_ref), channel_id=1, source_target_pairs={{0,4},{1,5},{2,6},{3,7},{4,8},{5,9},{6,10},{7,11},{8,12},{9,13},{1... | collective-permute-start | bytes 294920 | tf_op jit(solution)/shard_map/ppermute | solution.py:322
  33.5 28.1 %collective-permute-start.3 = (bf16[2,12,16,128]{3,2,1,0:T(8,128)(2,1)}, bf16[2,12,16,128]{3,2,1,0:T(8,128)(2,1)}, u32[]{:S(2)}, u32[]{:S(2)}) collective-permute-start(bf16[2,12,16,128]{3,2,1,0:T(8,128)(2,1)} %pad_maximum_fusion.pair_ref), channel_id=1, source_target_pairs={{0,2},{1,3},{2,4},{3,5},{4,6},{5,7},{6,8},{7,9},{8,10},{9,11},{10,... | collective-permute-start | bytes 294920 | tf_op jit(solution)/shard_map/ppermute | solution.py:322
  36.5 0.7 copy-start.5
  37.2 0.7 copy-start.7
  55.6 1.0 %copy-start.6 = (bf16[1024,128]{1,0:T(8,128)(2,1)S(1)}, bf16[1024,128]{1,0:T(8,128)(2,1)}, u32[]{:S(2)}) copy-start(bf16[1024,128]{1,0:T(8,128)(2,1)} %copy-done.5) | copy-start | bytes 786436
  56.6 0.9 %copy-start.8 = (bf16[1024,128]{1,0:T(8,128)(2,1)S(1)}, bf16[1024,128]{1,0:T(8,128)(2,1)}, u32[]{:S(2)}) copy-start(bf16[1024,128]{1,0:T(8,128)(2,1)} %copy-done.7) | copy-start | bytes 786436
  59.7 9.2 %collective-permute-start.4 = (f32[16,128]{1,0:T(8,128)S(1)}, f32[16,128]{1,0:T(8,128)S(1)}, u32[]{:S(2)}, u32[]{:S(2)}) collective-permute-start(f32[16,128]{1,0:T(8,128)S(1)} %get-tuple-element.22.factor_ref), channel_id=1, source_target_pairs={{0,1},{1,2},{2,3},{3,4},{4,5},{5,6},{6,7},{7,8},{8,9},{9,10},{10,1... | collective-permute-start | bytes 24584 | tf_op jit(solution)/shard_map/ppermute | solution.py:328
  61.7 1.0 %copy-start.1 = (bf16[512,256]{1,0:T(8,128)(2,1)S(1)}, bf16[512,256]{1,0:T(8,128)(2,1)}, u32[]{:S(2)}) copy-start(bf16[512,256]{1,0:T(8,128)(2,1)} %constant.12.clone.forward_ref) | copy-start | bytes 786436
  62.6 0.9 %copy-start.2 = (bf16[256,512]{1,0:T(8,128)(2,1)S(1)}, bf16[256,512]{1,0:T(8,128)(2,1)}, u32[]{:S(2)}) copy-start(bf16[256,512]{1,0:T(8,128)(2,1)} %constant.13.clone.inverse_ref) | copy-start | bytes 786436
  63.6 5.3 %copy-start.4 = (bf16[256,512]{1,0:T(8,128)(2,1)S(1)}, bf16[256,512]{1,0:T(8,128)(2,1)}, u32[]{:S(2)}) copy-start(bf16[256,512]{1,0:T(8,128)(2,1)} %constant.14.clone.inverse_ref) | copy-start | bytes 786436
  69.4 7.4 %collective-permute-start.5 = (bf16[128,256]{1,0:T(8,128)(2,1)S(1)}, bf16[128,256]{1,0:T(8,128)(2,1)S(1)}, u32[]{:S(2)}, u32[]{:S(2)}) collective-permute-start(bf16[128,256]{1,0:T(8,128)(2,1)S(1)} %after_part.1), channel_id=1, source_target_pairs={{1,0},{2,1},{3,2},{4,3},{5,4},{6,5},{7,6},{8,7},{9,8},{10,9},{11,1... | collective-permute-start | bytes 196616 | tf_op jit(solution)/shard_map/ppermute | solution.py:328

commit v3 on v2

--- a/solution.py
+++ b/solution.py
@@ -88,7 +88,7 @@
         return pltpu.make_async_copy(raw_ref.at[:, rows, :], waves_ref.at[part], get_sem.at[part])
 
     def store(part):
-        rows = pl.ds(part * GROUP, GROUP)
+        rows = pl.ds(windows - (part + 1) * GROUP, GROUP)
         return pltpu.make_async_copy(done_ref.at[rows], out_ref.at[rows], put_sem.at[part])
 
     for part in range(parts):
@@ -110,7 +110,7 @@
         for window in range(GROUP):
             rows = moved[window * CAP : (window + 1) * CAP]
             extra = jnp.broadcast_to(own[window : window + 1], (8, 128))
-            done_ref[part * GROUP + window] = jnp.concatenate([rows[:, :128], rows[:, 128:], extra], axis=0).astype(
+            done_ref[windows - 1 - part * GROUP - window] = jnp.concatenate([rows[:, :128], rows[:, 128:], extra], axis=0).astype(
                 jnp.bfloat16
             )
         store(part).start()
@@ -118,23 +118,38 @@
         store(part).wait()
 
 
-def table_kernel(moves_ref, lists_ref, phase_ref, cosine_ref, sine_ref, sign_ref, block_ref, lane_ref):
-    half = cosine_ref.shape[0]
-    eye = iota((128, 128), 0) == iota((128, 128), 1)
-    for q in range(moves_ref.shape[0]):
-        cols = slice(q * 128, (q + 1) * 128)
+def wave_kernel(who_ref, pair_ref, right_ref, cross_ref, left_ref, moves_ref, forward_ref, phase_ref,
+                wave_ref, top_ref, rows_ref):
+    listed, span = wave_ref.shape[0], wave_ref.shape[1]
+    half = span // 2
+    chip, core = who_ref[0] // 2, who_ref[0] % 2
+    group = pair_ref.shape[2]
+    rows_ref[:, 128:] = jnp.zeros((listed * 128, rows_ref.shape[1] - 128), jnp.bfloat16)
+    for away, ref in enumerate((pair_ref, right_ref, cross_ref, left_ref)):
+        for other in range(2):
+            owner = lax.rem(chip + away, 4) * 2 + lax.rem(core + other, 2)
+            for q in range(listed):
+                at = pl.ds(pl.multiple_of(q * 128 + owner * group, group), group)
+                rows_ref[at, 0:128] = ref[other, q]
+                tail = ref[other, listed + q % 4]
+                rows_ref[at, 128:L] = tail[:, : L - 128] if q < 4 else tail[:, L - 128 :]
+    zero = iota((half, 128), 0) == 0
+    for q in range(listed):
         move = moves_ref[q : q + 1, :]
         angles = dot(phase_ref[...], (iota((SMAX, 128), 0) == move).astype(jnp.bfloat16))
-        cosine_ref[:, cols] = angles[:half] + angles[half : 2 * half]
-        sine_ref[:, cols] = angles[2 * half : 3 * half] + angles[3 * half :]
-        sign_ref[q : q + 1, :] = 1.0 - 2.0 * (move % 2).astype(jnp.float32)
-        station = to_column(lists_ref[q : q + 1, :].astype(jnp.float32), eye).astype(jnp.int32)
-        lane = iota((128, 128), 1)
-        block_ref[cols, :] = (lane == station // 32).astype(jnp.bfloat16)
-        lane_ref[cols, :] = jnp.logical_or(lane == station % 32, lane == 64).astype(jnp.bfloat16)
-
-
-def pick_kernel(got_ref, block_ref, lane_ref, scaled_ref, level_ref, factor_ref):
+        cosine = angles[:half] + angles[half : 2 * half]
+        sine = angles[2 * half : 3 * half] + angles[3 * half :]
+        sign = 1.0 - 2.0 * (move % 2).astype(jnp.float32)
+        if q % 2 == 0:
+            spectra = dot_rows(forward_ref[...], rows_ref[q * 128 : (q + 2) * 128, :])
+        spectrum = spectra[:, q % 2 * 128 : (q % 2 + 1) * 128]
+        real, imag = spectrum[:half], spectrum[half:]
+        wave_ref[q, :half] = jnp.where(zero, real, real * cosine + imag * sine).astype(jnp.bfloat16)
+        wave_ref[q, half:] = jnp.where(zero, 0.0, real * sine - imag * cosine).astype(jnp.bfloat16)
+        top_ref[q : q + 1, :] = imag[0:1] * sign
+
+
+def pick_kernel(got_ref, lists_ref, scaled_ref, level_ref, factor_ref):
     blocks = got_ref.shape[0]
     slots = blocks * CAP
     codes = got_ref[:, 2 * CAP : 2 * CAP + 8, :].astype(jnp.float32)[:, 0, :]
@@ -146,54 +161,47 @@
     waves = jnp.concatenate([low, high], axis=1)
     width = waves.shape[1]
     eye = iota((128, 128), 0) == iota((128, 128), 1)
+    lane = iota((256, 128), 1)
     total = jnp.zeros((1, 128), jnp.float32)
-    listed = block_ref.shape[0] // 128
-    for q in range(listed):
-        cols = slice(q * 128, (q + 1) * 128)
-        target = jnp.sum(
-            dot(block_ref[cols, :], codes) * lane_ref[cols, :].astype(jnp.float32), axis=1, keepdims=True
-        )
-        chosen = jnp.where(iota((128, slots), 1).astype(jnp.float32) == target, 1.0, 0.0).astype(jnp.bfloat16)
+    listed = lists_ref.shape[0]
+    for pair in range(listed // 2):
+        both = (2 * pair, 2 * pair + 1)
+        columns = [to_column(lists_ref[q : q + 1, :].astype(jnp.float32), eye) for q in both]
+        station = jnp.concatenate(columns, axis=0).astype(jnp.int32)
+        holder = (lane == blocks - 1 - station // 32).astype(jnp.bfloat16)
+        mask = jnp.logical_or(lane == station % 32, lane == 64)
+        target = jnp.sum(jnp.where(mask, dot(holder, codes), 0.0), axis=1, keepdims=True)
+        chosen = jnp.where(iota((256, slots), 1).astype(jnp.float32) == target, 1.0, 0.0).astype(jnp.bfloat16)
         rows = dot(chosen, waves)
         power = jnp.sum(rows * rows, axis=1, keepdims=True) * (1.0 / width)
         present = jnp.where(target < MISSING * 0.5, 1.0, 0.0)
         safe = jnp.minimum(power, LIMIT) + epsilon
-        scaled_ref[cols, :] = (rows * lax.rsqrt(safe)).astype(jnp.bfloat16)
-        level_ref[q : q + 1, :] = to_row(jnp.sqrt(safe), eye)
-        factor_ref[q : q + 1, :] = to_row(present * lax.rsqrt(power + epsilon), eye)
-        total = total + to_row(present, eye)
+        scaled_ref[pair * 256 : (pair + 1) * 256, :] = (rows * lax.rsqrt(safe)).astype(jnp.bfloat16)
+        level = jnp.sqrt(safe)
+        factor = present * lax.rsqrt(power + epsilon)
+        for side, q in enumerate(both):
+            at = slice(side * 128, (side + 1) * 128)
+            level_ref[q : q + 1, :] = to_row(level[at], eye)
+            factor_ref[q : q + 1, :] = to_row(factor[at], eye)
+            total = total + to_row(present[at], eye)
     factor_ref[listed : listed + 8, :] = jnp.broadcast_to(1.0 / jnp.maximum(total, 1.0), (8, 128))
 
 
-def own_kernel(who_ref, pair_ref, right_ref, cross_ref, left_ref, scaled_ref, factor_ref, cosine_ref, sine_ref,
-               sign_ref, forward_ref, inverse_ref, mixed_ref, out_ref, rows_ref):
-    half = cosine_ref.shape[0]
-    listed = cosine_ref.shape[1] // 128
-    span = 2 * half
-    chip, core = who_ref[0] // 2, who_ref[0] % 2
-    group = pair_ref.shape[2]
-    rows_ref[:, 128:] = jnp.zeros((listed * 128, rows_ref.shape[1] - 128), jnp.bfloat16)
-    for away, ref in enumerate((pair_ref, right_ref, cross_ref, left_ref)):
-        for other in range(2):
-            owner = lax.rem(chip + away, 4) * 2 + lax.rem(core + other, 2)
-            for q in range(listed):
-                at = pl.ds(pl.multiple_of(q * 128 + owner * group, group), group)
-                rows_ref[at, 0:128] = ref[other, q]
-                tail = ref[other, listed + q % 4]
-                rows_ref[at, 128:L] = tail[:, : L - 128] if q < 4 else tail[:, L - 128 :]
+def own_kernel(wave_ref, scaled_ref, factor_ref, top_ref, forward_ref, inverse_ref, mixed_ref, out_ref):
+    listed, span = wave_ref.shape[0], wave_ref.shape[1]
+    half = span // 2
+
     sums = [jnp.zeros((half, 128), jnp.float32), jnp.zeros((half, 128), jnp.float32)]
     zero = iota((half, 128), 0) == 0
     for q in range(listed):
+        if q % 2 == 0:
+            spectra = dot_rows(forward_ref[...], scaled_ref[q * 128 : (q + 2) * 128, :])
+        spectrum = spectra[:, q % 2 * 128 : (q % 2 + 1) * 128]
         cols = slice(q * 128, (q + 1) * 128)
-        template = dot_rows(forward_ref[...], rows_ref[cols, :])
-        spectrum = dot_rows(forward_ref[...], scaled_ref[cols, :])
         real, imag = spectrum[:half], spectrum[half:]
-        cosine, sine = cosine_ref[:, cols], sine_ref[:, cols]
-        wave_real = template[:half] * cosine + template[half:] * sine
-        wave_imag = template[:half] * sine - template[half:] * cosine
-        wave_real = jnp.where(zero, template[:half], wave_real)
-        wave_imag = jnp.where(zero, 0.0, wave_imag)
-        straight = jnp.where(zero, template[half:] * sign_ref[q : q + 1, :], wave_real)
+        wave_real = wave_ref[q, :half].astype(jnp.float32)
+        wave_imag = wave_ref[q, half:].astype(jnp.float32)
+        straight = jnp.where(zero, top_ref[q : q + 1, :], wave_real)
         mixed_real = wave_real * real - wave_imag * imag
         mixed_imag = straight * imag + wave_imag * real
         mixed_ref[:half, cols] = mixed_real.astype(jnp.bfloat16)
@@ -217,8 +225,8 @@
     out_ref[...] = jnp.transpose(series).astype(jnp.bfloat16)
 
 
-def params():
-    return pltpu.CompilerParams(vmem_limit_bytes=16 * 1024 * 1024)
+def params(mebibytes=16):
+    return pltpu.CompilerParams(vmem_limit_bytes=mebibytes * 1024 * 1024)
 
 
 def vmem(n):
@@ -232,70 +240,65 @@
     return pl.pallas_call(
         pack_kernel,
         out_shape=jax.ShapeDtypeStruct(shape, jnp.bfloat16),
-        in_specs=vmem(1) + [pl.BlockSpec(memory_space=pl.ANY)],
-        out_specs=pl.BlockSpec(memory_space=pl.ANY),
+        in_specs=vmem(1) + [pl.BlockSpec(memory_space=pltpu.HBM)],
+        out_specs=pl.BlockSpec(memory_space=pltpu.HBM),
         scratch_shapes=[
             pltpu.VMEM((parts, count, GROUP, width), jnp.bfloat16),
             pltpu.VMEM(shape, jnp.bfloat16),
             pltpu.SemaphoreType.DMA((parts,)),
             pltpu.SemaphoreType.DMA((parts,)),
         ],
-        compiler_params=params(),
+        compiler_params=params(63),
         name="pack",
     )(status, waves)
 
 
-def tables(moves, lists, phases):
-    half = phases.shape[0] // 4
+def wave(who, blocks, moves, forward, phases):
+    span = forward.shape[0]
+    listed = moves.shape[0]
+    return pl.pallas_call(
+        wave_kernel,
+        out_shape=(
+            jax.ShapeDtypeStruct((listed, span, 128), jnp.bfloat16),
+            jax.ShapeDtypeStruct((listed, 128), jnp.float32),
+        ),
+        in_specs=[pl.BlockSpec(memory_space=pltpu.SMEM)] + vmem(7),
+        out_specs=tuple(vmem(2)),
+        scratch_shapes=[pltpu.VMEM((listed * 128, forward.shape[1]), jnp.bfloat16)],
+        compiler_params=params(),
+        name="wave",
+    )(who, *blocks, moves, forward, phases)
+
+
+def pick(got, lists):
     listed = lists.shape[0]
-    columns = listed * 128
-    return pl.pallas_call(
-        table_kernel,
-        out_shape=(
-            jax.ShapeDtypeStruct((half, columns), jnp.float32),
-            jax.ShapeDtypeStruct((half, columns), jnp.float32),
-            jax.ShapeDtypeStruct((listed, 128), jnp.float32),
-            jax.ShapeDtypeStruct((columns, 128), jnp.bfloat16),
-            jax.ShapeDtypeStruct((columns, 128), jnp.bfloat16),
-        ),
-        in_specs=vmem(3),
-        out_specs=tuple(vmem(5)),
-        compiler_params=params(),
-        name="tables",
-    )(moves, lists, phases)
-
-
-def pick(got, block, lane):
-    columns = block.shape[0]
-    listed = columns // 128
     return pl.pallas_call(
         pick_kernel,
         out_shape=(
-            jax.ShapeDtypeStruct((columns, 256), jnp.bfloat16),
+            jax.ShapeDtypeStruct((listed * 128, 256), jnp.bfloat16),
             jax.ShapeDtypeStruct((listed, 128), jnp.float32),
             jax.ShapeDtypeStruct((listed + 8, 128), jnp.float32),
         ),
-        in_specs=vmem(3),
+        in_specs=vmem(2),
         out_specs=tuple(vmem(3)),
         compiler_params=params(),
         name="pick",
-    )(got, block, lane)
-
-
-def own_part(who, blocks, scaled, factor, cosine, sine, sign, forward, inverse):
-    span, columns = forward.shape[0], cosine.shape[1]
+    )(got, lists)
+
+
+def own_part(waves, scaled, factor, top, forward, inverse):
+    listed, span = waves.shape[0], waves.shape[1]
     return pl.pallas_call(
         own_kernel,
         out_shape=(
-            jax.ShapeDtypeStruct((span, columns), jnp.bfloat16),
+            jax.ShapeDtypeStruct((span, listed * 128), jnp.bfloat16),
             jax.ShapeDtypeStruct((128, inverse.shape[0]), jnp.float32),
         ),
-        in_specs=[pl.BlockSpec(memory_space=pltpu.SMEM)] + vmem(11),
+        in_specs=vmem(6),
         out_specs=tuple(vmem(2)),
-        scratch_shapes=[pltpu.VMEM((columns, forward.shape[1]), jnp.bfloat16)],
         compiler_params=params(),
         name="own_part",
-    )(who, *blocks, scaled, factor, cosine, sine, sign, forward, inverse)
+    )(waves, scaled, factor, top, forward, inverse)
 
 
 def after_part(mixed, level, factor, inverse):
@@ -328,26 +331,30 @@
     return lax.ppermute(value, axis, [(i, i + by) for i in range(count) if 0 <= i + by < count])
 
 
+def scatter_windows(value):
+    count, width = lax.axis_size("tm"), lax.axis_size("tmpl")
+    groups = [[(count - 1 - p) * width + j for p in range(count)] for j in range(width)]
+    return lax.all_to_all(value, ("tm", "tmpl"), split_axis=0, concat_axis=0, axis_index_groups=groups, tiled=True)
+
+
 def shards(raw, avail, templates, stations, shifts):
     width = raw.shape[3]
     span = width + L + SMAX
     forward = forward_rows(span, width)
     inverse, inverse_after = inverse_rows(span, width)
     phases = phase_tables(span, SMAX)
+    lists = jnp.transpose(stations)
+    got = scatter_windows(pack(jnp.transpose(avail[:, 0, :]), raw[:, :, 0, :]))
     own = jnp.transpose(templates, (1, 0, 2))
     tail = jnp.concatenate([own[:4, :, 128:], own[4:, :, 128:]], axis=2)
     own = jnp.concatenate([own[:, :, :128], tail], axis=0)
-    other = other_core(own)
-    payload = pack(jnp.transpose(avail[:, 0, :]), raw[:, :, 0, :])
-    payload, other = lax.optimization_barrier((payload, other))
-    got = lax.all_to_all(payload, "tm", split_axis=0, concat_axis=0, tiled=True)
-    pair = jnp.stack([own, other])
+    pair = jnp.stack([own, other_core(own)])
     blocks = (pair, along_ring(pair, -1), along_ring(pair, 2), along_ring(pair, 1))
     who = lax.axis_index("tmpl").reshape(1)
-    cosine, sine, sign, block, lane = tables(jnp.transpose(shifts), jnp.transpose(stations), phases)
-    scaled, level, factor = pick(got, block, lane)
+    waves, top = wave(who, blocks, jnp.transpose(shifts), forward, phases)
+    scaled, level, factor = pick(got, lists)
     before = shifted(factor, 1)
-    mixed, stack = own_part(who, blocks, scaled, factor, cosine, sine, sign, forward, inverse)
+    mixed, stack = own_part(waves, scaled, factor, top, forward, inverse)
     late = shifted(after_part(mixed, level, before, inverse_after), -1)
     return stack + late.astype(jnp.float32)
 

time: 78 us -> 66.3 us (0.85)
  local copies, waits for them, and re-layouts: 7.32 us -> 0.69 us
  waiting for transfers between devices: 22 us -> 16.9 us
  starting transfers between devices: 37.2 us -> 38.1 us
    all_to_all x1, waiting for transfers between devices: 17.7 us -> 9.66 us  [scatter_windows(): lax.all_to_all(value, ('tm', 'tmpl'), split_axis=0, concat_axis=0, axis_i...]
    unnamed x25 -> x15, local copies, waits for them, and re-layouts: 7.3 us -> 0.67 us
    ppermute x2, waiting for transfers between devices: 4.26 us -> 6.09 us  [shifted(): lax.ppermute(value, axis, [(i, i + by) for i in range(count) if 0 <= i +...]
    ppermute x2, starting transfers between devices: 7.42 us -> 5.6 us  [shifted(): lax.ppermute(value, axis, [(i, i + by) for i in range(count) if 0 <= i +...]
    ppermute x3, starting transfers between devices: 8.76 us -> 10.1 us  [along_ring(): return lax.ppermute(value, ('tm', 'tmpl'), pairs)]
    pallas_call x3, Pallas kernels: 6.1 us -> 4.78 us  [the longest x1 2.45 us: pick(): pl.pallas_call(pick_kernel, out_shape=(jax.ShapeDtypeStruct((listed * 128...]
    all_to_all x1, starting transfers between devices: 19.1 us -> 20.4 us  [scatter_windows(): lax.all_to_all(value, ('tm', 'tmpl'), split_axis=0, concat_axis=0, axis_i...]
    pallas_call x1, Pallas kernels: 2.62 us -> 3.86 us  [pack(): pl.pallas_call(pack_kernel, out_shape=jax.ShapeDtypeStruct(shape, jnp.bfl...]
  transfers between devices with their start and end apart: 7 -> 7, of which waited for: 3 -> 4; matrix products, arithmetic and copies ran while one was open for 1% -> 0% of each run, Pallas kernels for 11% -> 7%
where the time goes in v3:
time: 66.3 us; the launch traced here: 65.8 us
  starting transfers between devices  38.1 us (57%)
  waiting for transfers between devices  16.9 us (25%)
  Pallas kernels  9.11 us (14%)
  other arithmetic  0.85 us (1%)
  local copies, waits for them, and re-layouts  0.69 us (1%)
    all_to_all x1, starting transfers between devices, scatter_windows(): lax.all_to_all(value, ('tm', 'tmpl'), split_axis=0, concat_axis=0, axis_i...  20.4 us
    ppermute x3, starting transfers between devices, along_ring(): return lax.ppermute(value, ('tm', 'tmpl'), pairs)  10.1 us
    all_to_all x1, waiting for transfers between devices, scatter_windows(): lax.all_to_all(value, ('tm', 'tmpl'), split_axis=0, concat_axis=0, axis_i...  9.66 us
    ppermute x2, waiting for transfers between devices, shifted(): lax.ppermute(value, axis, [(i, i + by) for i in range(count) if 0 <= i +...  6.09 us
    ppermute x2, starting transfers between devices, shifted(): lax.ppermute(value, axis, [(i, i + by) for i in range(count) if 0 <= i +...  5.6 us
    pallas_call x1, Pallas kernels, pack(): pl.pallas_call(pack_kernel, out_shape=jax.ShapeDtypeStruct(shape, jnp.bfl...  3.86 us
    pallas_call x1, Pallas kernels, pick(): pl.pallas_call(pick_kernel, out_shape=(jax.ShapeDtypeStruct((listed * 128...  2.45 us
    ppermute x1, starting transfers between devices, other_core(): return lax.ppermute(value, 'tmpl', [(i, i ^ 1) for i in range(8)])  1.91 us
  transfers between devices with their start and end apart: 7, of which 4 were waited for; matrix products, arithmetic and copies ran while one was open for 0% of the time, Pallas kernels for 7%

profile of v3, /device:TPU:2, one launch (start us, length us, event | category | flops | bytes accessed | tf_op | source)
XLA Modules:
  0.0 65.8 jit_solution(13882934004338540599)
XLA Ops:
  0.0 3.9 %pack.1 = bf16[64,56,128]{2,1,0:T(8,128)(2,1)} custom-call(s32[32,64]{1,0:T(8,128)} %bitcast.19, bf16[32,64,256]{2,1,0:T(8,128)(2,1)} %bitcast.15), custom_call_target="tpu_custom_call" | custom-call | tf_op jit(solution)/shard_map/pack/pallas_call | solution.py:240
  3.9 0.0 copy-start.6
  3.9 20.4 %all-to-all-start = ((bf16[64,56,128]{2,1,0:T(8,128)(2,1)}), bf16[64,56,128]{2,1,0:T(8,128)(2,1)S(1)}, u32[]{:S(2)}, u32[]{:S(2)}) async-start(bf16[64,56,128]{2,1,0:T(8,128)(2,1)} %pack.1), calls=%async_computation | async-start | bytes 1835008 | tf_op jit(solution)/shard_map/all_to_all | solution.py:337
  24.3 0.0 copy-done.6
  24.4 0.1 maximum_maximum_fusion
  24.4 1.9 %collective-permute-start = (bf16[12,16,128]{2,1,0:T(8,128)(2,1)S(1)}, bf16[12,16,128]{2,1,0:T(8,128)(2,1)S(1)}, u32[]{:S(2)}, u32[]{:S(2)}) collective-permute-start(bf16[12,16,128]{2,1,0:T(8,128)(2,1)S(1)} %maximum_maximum_fusion), channel_id=1, source_target_pairs={{0,1},{1,0},{2,3},{3,2},{4,5},{5,4},{6,7},{7,6},{8,9},{9,8},{10,11... | collective-permute-start | bytes 147464 | tf_op jit(solution)/shard_map/ppermute | solution.py:316
  26.4 0.1 fusion.1
  26.4 1.1 %collective-permute-done = bf16[12,16,128]{2,1,0:T(8,128)(2,1)S(1)} collective-permute-done((bf16[12,16,128]{2,1,0:T(8,128)(2,1)S(1)}, bf16[12,16,128]{2,1,0:T(8,128)(2,1)S(1)}, u32[]{:S(2)}, u32[]{:S(2)}) %collective-permute-start) | collective-permute-done | bytes 49184 | tf_op jit(solution)/shard_map/ppermute | solution.py:316
  27.5 0.0 copy-start.4
  27.6 2.6 %collective-permute-start.3 = (bf16[2,12,16,128]{3,2,1,0:T(8,128)(2,1)S(1)}, bf16[2,12,16,128]{3,2,1,0:T(8,128)(2,1)S(1)}, u32[]{:S(2)}, u32[]{:S(2)}) collective-permute-start(bf16[2,12,16,128]{3,2,1,0:T(8,128)(2,1)S(1)} %pad_maximum_fusion.pair_ref), channel_id=1, source_target_pairs={{0,2},{1,3},{2,4},{3,5},{4,6},{5,7},{6,8},{7,9},{8,10},{9,11},{10,... | collective-permute-start | bytes 294920 | tf_op jit(solution)/shard_map/ppermute | solution.py:325
  30.2 4.0 %collective-permute-start.2 = (bf16[2,12,16,128]{3,2,1,0:T(8,128)(2,1)S(1)}, bf16[2,12,16,128]{3,2,1,0:T(8,128)(2,1)S(1)}, u32[]{:S(2)}, u32[]{:S(2)}) collective-permute-start(bf16[2,12,16,128]{3,2,1,0:T(8,128)(2,1)S(1)} %pad_maximum_fusion.pair_ref), channel_id=1, source_target_pairs={{0,4},{1,5},{2,6},{3,7},{4,8},{5,9},{6,10},{7,11},{8,12},{9,13},{1... | collective-permute-start | bytes 294920 | tf_op jit(solution)/shard_map/ppermute | solution.py:325
  34.2 3.6 %collective-permute-start.1 = (bf16[2,12,16,128]{3,2,1,0:T(8,128)(2,1)S(1)}, bf16[2,12,16,128]{3,2,1,0:T(8,128)(2,1)S(1)}, u32[]{:S(2)}, u32[]{:S(2)}) collective-permute-start(bf16[2,12,16,128]{3,2,1,0:T(8,128)(2,1)S(1)} %pad_maximum_fusion.pair_ref), channel_id=1, source_target_pairs={{0,14},{1,15},{2,0},{3,1},{4,2},{5,3},{6,4},{7,5},{8,6},{9,7},{10,... | collective-permute-start | bytes 294920 | tf_op jit(solution)/shard_map/ppermute | solution.py:325
  37.7 9.7 %all-to-all-done.got_ref = bf16[64,56,128]{2,1,0:T(8,128)(2,1)S(1)} async-done(((bf16[64,56,128]{2,1,0:T(8,128)(2,1)}), bf16[64,56,128]{2,1,0:T(8,128)(2,1)S(1)}, u32[]{:S(2)}, u32[]{:S(2)}) %all-to-all-start) | async-done | bytes 917536 | tf_op jit(solution)/shard_map/all_to_all | solution.py:337
  47.4 0.0 copy-done.4
  47.4 0.0 copy-start
  47.4 0.0 copy-start.1
  47.4 2.5 %pick.1 = (bf16[1024,256]{1,0:T(8,128)(2,1)S(1)}, f32[8,128]{1,0:T(8,128)S(1)}, f32[16,128]{1,0:T(8,128)S(1)}) custom-call(bf16[64,56,128]{2,1,0:T(8,128)(2,1)S(1)} %all-to-all-done.got_ref, s32[8,128]{1,0:T(8,128)S(1)} %bitcast.13), custom_call_target="tpu_custom_call" | custom-call | tf_op jit(solution)/shard_map/pick/pallas_call | solution.py:275
  49.9 1.9 %collective-permute-start.4 = (f32[16,128]{1,0:T(8,128)S(1)}, f32[16,128]{1,0:T(8,128)S(1)}, u32[]{:S(2)}, u32[]{:S(2)}) collective-permute-start(f32[16,128]{1,0:T(8,128)S(1)} %get-tuple-element.14.factor_ref), channel_id=1, source_target_pairs={{0,1},{1,2},{2,3},{3,4},{4,5},{5,6},{6,7},{7,8},{8,9},{9,10},{10,1... | collective-permute-start | bytes 24584 | tf_op jit(solution)/shard_map/ppermute | solution.py:331
  51.8 0.0 copy-start.5
  51.8 0.0 collective-permute-done.3.left_ref
  51.8 0.0 collective-permute-done.2.cross_ref
  51.8 0.0 collective-permute-done.1.right_ref
  51.8 0.0 copy-done
  51.8 0.0 copy-done.1
  51.9 0.6 copy-done.5
  52.5 0.0 copy-start.3
  52.5 1.2 %wave.1 = (bf16[8,512,128]{2,1,0:T(8,128)(2,1)S(1)}, f32[8,128]{1,0:T(8,128)S(1)}) custom-call(s32[1]{0:T(128)} %bitcast.who_ref, bf16[2,12,16,128]{3,2,1,0:T(8,128)(2,1)S(1)} %pad_maximum_fusion.pair_ref, bf16[2,12,16,128]{3,2,1,0:T(8,128)(2,1)S(1)} %collective-permute-done.1.right_ref, bf16[2,12,16,128]{3,2,1,0:T(8,128)(2,1)S(1)} %collective-permute-done.2.cross_ref, ...), custom_call_target="tpu_custom_call" | custom-call | tf_op jit(solution)/shard_map/wave/pallas_call | solution.py:259
  53.7 0.0 copy-done.3
  53.7 0.0 copy-start.2
  53.7 1.1 %own_part.1 = (bf16[512,1024]{1,0:T(8,128)(2,1)S(1)}, f32[128,256]{1,0:T(8,128)S(1)}) custom-call(bf16[8,512,128]{2,1,0:T(8,128)(2,1)S(1)} %get-tuple-element.12.wave_ref, bf16[1024,256]{1,0:T(8,128)(2,1)S(1)} %get-tuple-element.13.scaled_ref, f32[16,128]{1,0:T(8,128)S(1)} %get-tuple-element.14.factor_ref, f32[8,128]{1,0:T(8,128)S(1)} %get-tuple-element.15.top_ref, ...), custom_call_target="tpu_custom_call" | custom-call | tf_op jit(solution)/shard_map/own_part/pallas_call | solution.py:291
  54.8 4.2 %collective-permute-done.4.factor_ref = f32[16,128]{1,0:T(8,128)S(1)} collective-permute-done((f32[16,128]{1,0:T(8,128)S(1)}, f32[16,128]{1,0:T(8,128)S(1)}, u32[]{:S(2)}, u32[]{:S(2)}) %collective-permute-start.4) | collective-permute-done | bytes 8224 | tf_op jit(solution)/shard_map/ppermute | solution.py:331
  59.1 0.0 copy-done.2
  59.1 0.5 after_part.1
  59.5 3.7 %collective-permute-start.5 = (bf16[128,256]{1,0:T(8,128)(2,1)S(1)}, bf16[128,256]{1,0:T(8,128)(2,1)S(1)}, u32[]{:S(2)}, u32[]{:S(2)}) collective-permute-start(bf16[128,256]{1,0:T(8,128)(2,1)S(1)} %after_part.1), channel_id=1, source_target_pairs={{1,0},{2,1},{3,2},{4,3},{5,4},{6,5},{7,6},{8,7},{9,8},{10,9},{11,1... | collective-permute-start | bytes 196616 | tf_op jit(solution)/shard_map/ppermute | solution.py:331
  63.2 1.9 %collective-permute-done.5 = bf16[128,256]{1,0:T(8,128)(2,1)S(1)} collective-permute-done((bf16[128,256]{1,0:T(8,128)(2,1)S(1)}, bf16[128,256]{1,0:T(8,128)(2,1)S(1)}, u32[]{:S(2)}, u32[]{:S(2)}) %collective-permute-start.5) | collective-permute-done | bytes 65568 | tf_op jit(solution)/shard_map/ppermute | solution.py:331
  65.1 0.7 %convert_add_fusion = f32[128,256]{1,0:T(8,128)} fusion(f32[128,256]{1,0:T(8,128)S(1)} %get-tuple-element.16, bf16[128,256]{1,0:T(8,128)(2,1)S(1)} %collective-permute-done.5), kind=kLoop, calls=%fused_computation | loop fusion | flops 65536 | bytes 327680 | tf_op jit(solution)/shard_map/add | solution.py:359
  (4 shorter events, 0.0 us)
Async XLA Ops:
  3.9 20.4 %copy-start.6 = (bf16[16,8,192]{2,1,0:T(8,128)(2,1)S(1)}, bf16[16,8,192]{2,1,0:T(8,128)(2,1)}, u32[]{:S(2)}) copy-start(bf16[16,8,192]{2,1,0:T(8,128)(2,1)} %param.11) | copy-start | bytes 147460
  3.9 43.5 %all-to-all-start = ((bf16[64,56,128]{2,1,0:T(8,128)(2,1)}), bf16[64,56,128]{2,1,0:T(8,128)(2,1)S(1)}, u32[]{:S(2)}, u32[]{:S(2)}) async-start(bf16[64,56,128]{2,1,0:T(8,128)(2,1)} %pack.1), calls=%async_computation | async-start | bytes 1835008 | tf_op jit(solution)/shard_map/all_to_all | solution.py:337
  24.4 3.1 %collective-permute-start = (bf16[12,16,128]{2,1,0:T(8,128)(2,1)S(1)}, bf16[12,16,128]{2,1,0:T(8,128)(2,1)S(1)}, u32[]{:S(2)}, u32[]{:S(2)}) collective-permute-start(bf16[12,16,128]{2,1,0:T(8,128)(2,1)S(1)} %maximum_maximum_fusion), channel_id=1, source_target_pairs={{0,1},{1,0},{2,3},{3,2},{4,5},{5,4},{6,7},{7,6},{8,9},{9,8},{10,11... | collective-permute-start | bytes 147464 | tf_op jit(solution)/shard_map/ppermute | solution.py:316
  27.5 19.8 %copy-start.4 = (s32[128,8]{0,1:T(8,128)S(1)}, s32[128,8]{0,1:T(8,128)}, u32[]{:S(2)}) copy-start(s32[128,8]{0,1:T(8,128)} %param.12) | copy-start | bytes 12292
  27.6 24.2 %collective-permute-start.3 = (bf16[2,12,16,128]{3,2,1,0:T(8,128)(2,1)S(1)}, bf16[2,12,16,128]{3,2,1,0:T(8,128)(2,1)S(1)}, u32[]{:S(2)}, u32[]{:S(2)}) collective-permute-start(bf16[2,12,16,128]{3,2,1,0:T(8,128)(2,1)S(1)} %pad_maximum_fusion.pair_ref), channel_id=1, source_target_pairs={{0,2},{1,3},{2,4},{3,5},{4,6},{5,7},{6,8},{7,9},{8,10},{9,11},{10,... | collective-permute-start | bytes 294920 | tf_op jit(solution)/shard_map/ppermute | solution.py:325
  30.2 21.7 %collective-permute-start.2 = (bf16[2,12,16,128]{3,2,1,0:T(8,128)(2,1)S(1)}, bf16[2,12,16,128]{3,2,1,0:T(8,128)(2,1)S(1)}, u32[]{:S(2)}, u32[]{:S(2)}) collective-permute-start(bf16[2,12,16,128]{3,2,1,0:T(8,128)(2,1)S(1)} %pad_maximum_fusion.pair_ref), channel_id=1, source_target_pairs={{0,4},{1,5},{2,6},{3,7},{4,8},{5,9},{6,10},{7,11},{8,12},{9,13},{1... | collective-permute-start | bytes 294920 | tf_op jit(solution)/shard_map/ppermute | solution.py:325
  34.2 17.7 %collective-permute-start.1 = (bf16[2,12,16,128]{3,2,1,0:T(8,128)(2,1)S(1)}, bf16[2,12,16,128]{3,2,1,0:T(8,128)(2,1)S(1)}, u32[]{:S(2)}, u32[]{:S(2)}) collective-permute-start(bf16[2,12,16,128]{3,2,1,0:T(8,128)(2,1)S(1)} %pad_maximum_fusion.pair_ref), channel_id=1, source_target_pairs={{0,14},{1,15},{2,0},{3,1},{4,2},{5,3},{6,4},{7,5},{8,6},{9,7},{10,... | collective-permute-start | bytes 294920 | tf_op jit(solution)/shard_map/ppermute | solution.py:325
  47.4 4.4 %copy-start = (bf16[512,256]{1,0:T(8,128)(2,1)S(1)}, bf16[512,256]{1,0:T(8,128)(2,1)}, u32[]{:S(2)}) copy-start(bf16[512,256]{1,0:T(8,128)(2,1)} %constant.12.clone.forward_ref) | copy-start | bytes 786436
  47.4 4.4 %copy-start.1 = (bf16[1024,64]{1,0:T(8,128)(2,1)S(1)}, bf16[1024,64]{1,0:T(8,128)(2,1)}, u32[]{:S(2)}) copy-start(bf16[1024,64]{1,0:T(8,128)(2,1)} %constant.15.clone.phase_ref) | copy-start | bytes 393220
  49.9 9.2 %collective-permute-start.4 = (f32[16,128]{1,0:T(8,128)S(1)}, f32[16,128]{1,0:T(8,128)S(1)}, u32[]{:S(2)}, u32[]{:S(2)}) collective-permute-start(f32[16,128]{1,0:T(8,128)S(1)} %get-tuple-element.14.factor_ref), channel_id=1, source_target_pairs={{0,1},{1,2},{2,3},{3,4},{4,5},{5,6},{6,7},{7,8},{8,9},{9,10},{10,1... | collective-permute-start | bytes 24584 | tf_op jit(solution)/shard_map/ppermute | solution.py:331
  51.8 0.7 %copy-start.5 = (s32[128,8]{0,1:T(8,128)S(1)}, s32[128,8]{0,1:T(8,128)}, u32[]{:S(2)}) copy-start(s32[128,8]{0,1:T(8,128)} %param.13) | copy-start | bytes 12292
  52.5 1.2 %copy-start.3 = (bf16[256,512]{1,0:T(8,128)(2,1)S(1)}, bf16[256,512]{1,0:T(8,128)(2,1)}, u32[]{:S(2)}) copy-start(bf16[256,512]{1,0:T(8,128)(2,1)} %constant.13.clone.inverse_ref) | copy-start | bytes 786436
  53.7 5.4 %copy-start.2 = (bf16[256,512]{1,0:T(8,128)(2,1)S(1)}, bf16[256,512]{1,0:T(8,128)(2,1)}, u32[]{:S(2)}) copy-start(bf16[256,512]{1,0:T(8,128)(2,1)} %constant.14.clone.inverse_ref) | copy-start | bytes 786436
  59.5 5.6 %collective-permute-start.5 = (bf16[128,256]{1,0:T(8,128)(2,1)S(1)}, bf16[128,256]{1,0:T(8,128)(2,1)S(1)}, u32[]{:S(2)}, u32[]{:S(2)}) collective-permute-start(bf16[128,256]{1,0:T(8,128)(2,1)S(1)} %after_part.1), channel_id=1, source_target_pairs={{1,0},{2,1},{3,2},{4,3},{5,4},{6,5},{7,6},{8,7},{9,8},{10,9},{11,1... | collective-permute-start | bytes 196616 | tf_op jit(solution)/shard_map/ppermute | solution.py:331

commit v4 on v3

v4 whole, which is shorter than its diff:
```python
import functools
import math

import jax
import jax.numpy as jnp
import numpy as np
from jax import lax
from jax.experimental import pallas as pl
from jax.experimental.pallas import tpu as pltpu
from jax.sharding import PartitionSpec as P

L = 192
SMAX = 64
CAP = 24
ROWS = 2 * CAP + 2
GROUP = 16
MISSING = 4096.0
LIMIT = 3e38

epsilon = 1e-05


def cosine_rows(span, width):
    half = span // 2
    frequency = np.arange(half)[:, None]
    sample = np.arange(width)[None, :]
    angle = (frequency * sample % span) * (2.0 * math.pi / span)
    real = np.cos(angle)
    imag = -np.sin(angle)
    imag[0] = np.cos(math.pi * np.arange(width))
    return real, imag


def forward_rows(span, width):
    real, imag = cosine_rows(span, width)
    return jnp.asarray(np.concatenate([real, imag]).astype(jnp.bfloat16))


def inverse_rows(span, width):
    real, imag = cosine_rows(span, width)
    real, imag = 2.0 * real, 2.0 * imag
    real[0] *= 0.5
    imag[0] *= 0.5
    table = np.concatenate([real, imag])
    flip = np.where(np.arange(span // 2) % 2 == 0, 1.0, -1.0)
    after = table * np.concatenate([flip, flip])[:, None]
    return (
        jnp.asarray(table.T.astype(jnp.bfloat16)),
        jnp.asarray(after.T.astype(jnp.bfloat16)),
    )


def phase_tables(span, moves):
    angle = (np.arange(span // 2)[:, None] * np.arange(moves)[None, :] % span) * (2.0 * math.pi / span)
    parts = []
    for value in (np.cos(angle), np.sin(angle)):
        high = value.astype(jnp.bfloat16)
        parts.append(high)
        parts.append((value - high.astype(np.float64)).astype(jnp.bfloat16))
    return jnp.asarray(np.concatenate(parts))


def dot(a, b):
    return jnp.dot(a, b, preferred_element_type=jnp.float32)


def dot_rows(a, b):
    return lax.dot_general(a, b, (((1,), (1,)), ((), ())), preferred_element_type=jnp.float32)


def iota(shape, dim):
    return lax.broadcasted_iota(jnp.int32, shape, dim)


def to_row(column, eye):
    return jnp.sum(jnp.where(eye, column, 0.0), axis=0, keepdims=True)


def to_column(row, eye):
    return jnp.sum(jnp.where(eye, row, 0.0), axis=1, keepdims=True)


def pack_kernel(avail_ref, raw_ref, out_ref, flags_ref, waves_ref, mover_ref, done_ref, flag_sem, get_sem, put_sem):
    count, windows, width = raw_ref.shape
    parts = windows // GROUP

    def fetch(part):
        rows = pl.ds(part * GROUP, GROUP)
        return pltpu.make_async_copy(raw_ref.at[:, rows, :], waves_ref.at[part], get_sem.at[part])

    def store(part):
        rows = pl.ds((windows - (part + 1) * GROUP) * ROWS, GROUP * ROWS)
        return pltpu.make_async_copy(done_ref.at[rows], out_ref.at[rows], put_sem.at[part])

    status = pltpu.make_async_copy(avail_ref, flags_ref, flag_sem)
    status.start()
    for part in range(parts):
        fetch(part).start()
    place = (iota((count, 128), 0) == iota((count, 128), 1)).astype(jnp.bfloat16)
    before = (iota((count, 128), 0) < iota((count, 128), 1)).astype(jnp.bfloat16)
    lanes = count * GROUP
    spread = (iota((128, lanes), 0) == iota((128, lanes), 1) // GROUP).astype(jnp.bfloat16)
    slot = iota((GROUP, CAP, lanes), 1).astype(jnp.float32)
    status.wait()
    flags = jnp.transpose(flags_ref[...].astype(jnp.float32)).astype(jnp.bfloat16)
    code = jnp.where(dot(flags, place) > 0.5, dot(flags, before), MISSING)
    wide = dot(code.astype(jnp.bfloat16), spread)
    wide = jnp.where(iota((windows, lanes), 1) % GROUP == iota((windows, lanes), 0) % GROUP, wide, -1.0)
    for part in range(parts):
        own = wide[part * GROUP : (part + 1) * GROUP]
        mover = jnp.where(own[:, None, :] == slot, 1.0, 0.0)
        mover_ref[part] = mover.reshape(GROUP * CAP, lanes).astype(jnp.bfloat16)
    for part in range(parts):
        fetch(part).wait()
        moved = dot(mover_ref[part], waves_ref[part].reshape(lanes, width))
        for index in range(GROUP):
            window = part * GROUP + index
            rows = moved[index * CAP : (index + 1) * CAP]
            note = jnp.broadcast_to(code[window : window + 1], (ROWS - 2 * CAP, 128))
            at = (windows - 1 - window) * ROWS
            block = jnp.concatenate([rows[:, :128], rows[:, 128:], note], axis=0)
            done_ref[at : at + ROWS, :] = block.astype(jnp.bfloat16)
        store(part).start()
    for part in range(parts):
        store(part).wait()


def wave_kernel(who_ref, pair_ref, right_ref, cross_ref, left_ref, lists_ref, forward_ref, phase_ref,
                wave_ref, top_ref, rows_ref):
    listed, span = wave_ref.shape[0], wave_ref.shape[1]
    half = span // 2
    chip, core = who_ref[0] // 2, who_ref[0] % 2
    group = pair_ref.shape[2]
    rows_ref[:, 128:] = jnp.zeros((listed * 128, rows_ref.shape[1] - 128), jnp.bfloat16)
    for away, ref in enumerate((pair_ref, right_ref, cross_ref, left_ref)):
        for other in range(2):
            owner = lax.rem(chip + away, 4) * 2 + lax.rem(core + other, 2)
            for q in range(listed):
                at = pl.ds(pl.multiple_of(q * 128 + owner * group, group), group)
                rows_ref[at, 0:128] = ref[other, q]
                tail = ref[other, listed + q % 4]
                rows_ref[at, 128:L] = tail[:, : L - 128] if q < 4 else tail[:, L - 128 :]
    zero = iota((half, 128), 0) == 0
    for q in range(listed):
        move = lists_ref[listed + q : listed + q + 1, :]
        angles = dot(phase_ref[...], (iota((SMAX, 128), 0) == move).astype(jnp.bfloat16))
        cosine = angles[:half] + angles[half : 2 * half]
        sine = angles[2 * half : 3 * half] + angles[3 * half :]
        sign = 1.0 - 2.0 * (move % 2).astype(jnp.float32)
        if q % 2 == 0:
            spectra = dot_rows(forward_ref[...], rows_ref[q * 128 : (q + 2) * 128, :])
        spectrum = spectra[:, q % 2 * 128 : (q % 2 + 1) * 128]
        real, imag = spectrum[:half], spectrum[half:]
        wave_ref[q, :half] = jnp.where(zero, real, real * cosine + imag * sine).astype(jnp.bfloat16)
        wave_ref[q, half:] = jnp.where(zero, 0.0, real * sine - imag * cosine).astype(jnp.bfloat16)
        top_ref[q : q + 1, :] = imag[0:1] * sign


def pick_kernel(got_ref, lists_ref, scaled_ref, level_ref, factor_ref):
    blocks = got_ref.shape[0] // ROWS
    slots = blocks * CAP
    listed = level_ref.shape[0]

    def gather(first, size):
        rows = [got_ref[block * ROWS + first : block * ROWS + first + size, :] for block in range(blocks)]
        return [value.astype(jnp.float32) for value in rows]

    low = jnp.concatenate(gather(0, CAP), axis=0).astype(jnp.bfloat16)
    high = jnp.concatenate(gather(CAP, CAP), axis=0).astype(jnp.bfloat16)
    waves = jnp.concatenate([low, high], axis=1)
    width = waves.shape[1]
    codes = jnp.concatenate([value[0:1] for value in gather(2 * CAP, 2)], axis=0)
    start = iota((blocks, 128), 0).astype(jnp.float32) * CAP
    codes = jnp.where(iota((blocks, 128), 1) == 64, start, codes).astype(jnp.bfloat16)
    codes = jnp.concatenate([codes, jnp.zeros((128 - blocks, 128), jnp.bfloat16)], axis=0)
    eye = iota((128, 128), 0) == iota((128, 128), 1)
    columns = [to_column(lists_ref[q : q + 1, :].astype(jnp.float32), eye) for q in range(listed)]
    station = jnp.concatenate(columns, axis=0).astype(jnp.int32)
    lane = iota((listed * 128, 128), 1)
    holder = (lane == blocks - 1 - station // 32).astype(jnp.bfloat16)
    mask = jnp.logical_or(lane == station % 32, lane == 64)
    targets = jnp.sum(jnp.where(mask, dot(holder, codes), 0.0), axis=1, keepdims=True)
    total = jnp.zeros((1, 128), jnp.float32)
    for pair in range(listed // 2):
        cols = slice(pair * 256, (pair + 1) * 256)
        target = targets[cols]
        chosen = jnp.where(iota((256, slots), 1).astype(jnp.float32) == target, 1.0, 0.0).astype(jnp.bfloat16)
        rows = dot(chosen, waves)
        power = jnp.sum(rows * rows, axis=1, keepdims=True) * (1.0 / width)
        present = jnp.where(target < MISSING * 0.5, 1.0, 0.0)
        safe = jnp.minimum(power, LIMIT) + epsilon
        scaled_ref[cols, :] = (rows * lax.rsqrt(safe)).astype(jnp.bfloat16)
        level = jnp.sqrt(safe)
        factor = present * lax.rsqrt(power + epsilon)
        for side in range(2):
            q = 2 * pair + side
            at = slice(side * 128, (side + 1) * 128)
            level_ref[q : q + 1, :] = to_row(level[at], eye)
            factor_ref[q : q + 1, :] = to_row(factor[at], eye)
            total = total + to_row(present[at], eye)
    factor_ref[listed : listed + 8, :] = jnp.broadcast_to(1.0 / jnp.maximum(total, 1.0), (8, 128))


def mix_kernel(wave_ref, scaled_ref, top_ref, forward_ref, mixed_ref):
    listed, span = wave_ref.shape[0], wave_ref.shape[1]
    half = span // 2
    zero = iota((half, 128), 0) == 0
    for q in range(listed):
        if q % 2 == 0:
            spectra = dot_rows(forward_ref[...], scaled_ref[q * 128 : (q + 2) * 128, :])
        spectrum = spectra[:, q % 2 * 128 : (q % 2 + 1) * 128]
        cols = slice(q * 128, (q + 1) * 128)
        real, imag = spectrum[:half], spectrum[half:]
        wave_real = wave_ref[q, :half].astype(jnp.float32)
        wave_imag = wave_ref[q, half:].astype(jnp.float32)
        straight = jnp.where(zero, top_ref[q : q + 1, :], wave_real)
        mixed_ref[:half, cols] = (wave_real * real - wave_imag * imag).astype(jnp.bfloat16)
        mixed_ref[half:, cols] = (straight * imag + wave_imag * real).astype(jnp.bfloat16)


def weighted_stack(mixed_ref, weights, scale, inverse_ref):
    span = mixed_ref.shape[0]
    total = jnp.zeros((span, 128), jnp.float32)
    for q in range(mixed_ref.shape[1] // 128):
        total = total + weights[q : q + 1, :] * mixed_ref[:, q * 128 : (q + 1) * 128].astype(jnp.float32)
    series = dot(inverse_ref[...], total.astype(jnp.bfloat16)) * (scale * (1.0 / span))
    return jnp.transpose(series)


def late_kernel(mixed_ref, level_ref, factor_ref, inverse_ref, out_ref):
    listed = level_ref.shape[0]
    weights = level_ref[...] * factor_ref[0:listed, :]
    out_ref[...] = weighted_stack(mixed_ref, weights, factor_ref[listed : listed + 1, :], inverse_ref).astype(jnp.bfloat16)


def own_kernel(mixed_ref, factor_ref, inverse_ref, late_ref, out_ref):
    listed = mixed_ref.shape[1] // 128
    weights = jnp.where(factor_ref[0:listed, :] > 0.0, 1.0, 0.0)
    out_ref[...] = weighted_stack(mixed_ref, weights, factor_ref[listed : listed + 1, :], inverse_ref)


def params(mebibytes=16):
    return pltpu.CompilerParams(vmem_limit_bytes=mebibytes * 1024 * 1024)


def vmem(n):
    return [pl.BlockSpec(memory_space=pltpu.VMEM)] * n


def pack(status, waves):
    count, windows, width = waves.shape
    parts = windows // GROUP
    shape = (windows * ROWS, 128)
    return pl.pallas_call(
        pack_kernel,
        out_shape=jax.ShapeDtypeStruct(shape, jnp.bfloat16),
        in_specs=[pl.BlockSpec(memory_space=pltpu.HBM)] * 2,
        out_specs=pl.BlockSpec(memory_space=pltpu.HBM),
        scratch_shapes=[
            pltpu.VMEM(status.shape, jnp.int32),
            pltpu.VMEM((parts, count, GROUP, width), jnp.bfloat16),
            pltpu.VMEM((parts, GROUP * CAP, count * GROUP), jnp.bfloat16),
            pltpu.VMEM(shape, jnp.bfloat16),
            pltpu.SemaphoreType.DMA,
            pltpu.SemaphoreType.DMA((parts,)),
            pltpu.SemaphoreType.DMA((parts,)),
        ],
        compiler_params=params(63),
        name="pack",
    )(status, waves)


def wave(who, blocks, lists, forward, phases):
    span = forward.shape[0]
    listed = lists.shape[0] // 2
    return pl.pallas_call(
        wave_kernel,
        out_shape=(
            jax.ShapeDtypeStruct((listed, span, 128), jnp.bfloat16),
            jax.ShapeDtypeStruct((listed, 128), jnp.float32),
        ),
        in_specs=[pl.BlockSpec(memory_space=pltpu.SMEM)] + vmem(7),
        out_specs=tuple(vmem(2)),
        scratch_shapes=[pltpu.VMEM((listed * 128, forward.shape[1]), jnp.bfloat16)],
        compiler_params=params(),
        name="wave",
    )(who, *blocks, lists, forward, phases)


def pick(got, lists):
    listed = lists.shape[0] // 2
    return pl.pallas_call(
        pick_kernel,
        out_shape=(
            jax.ShapeDtypeStruct((listed * 128, 256), jnp.bfloat16),
            jax.ShapeDtypeStruct((listed, 128), jnp.float32),
            jax.ShapeDtypeStruct((listed + 8, 128), jnp.float32),
        ),
        in_specs=vmem(2),
        out_specs=tuple(vmem(3)),
        compiler_params=params(),
        name="pick",
    )(got, lists)


def mix(waves, scaled, top, forward):
    listed, span = waves.shape[0], waves.shape[1]
    return pl.pallas_call(
        mix_kernel,
        out_shape=jax.ShapeDtypeStruct((span, listed * 128), jnp.bfloat16),
        in_specs=vmem(4),
        out_specs=vmem(1)[0],
        compiler_params=params(),
        name="mix",
    )(waves, scaled, top, forward)


def late_part(mixed, level, factor, inverse):
    return pl.pallas_call(
        late_kernel,
        out_shape=jax.ShapeDtypeStruct((128, inverse.shape[0]), jnp.bfloat16),
        in_specs=vmem(4),
        out_specs=vmem(1)[0],
        compiler_params=params(),
        name="late_part",
    )(mixed, level, factor, inverse)


def own_part(mixed, factor, inverse, late):
    return pl.pallas_call(
        own_kernel,
        out_shape=jax.ShapeDtypeStruct((128, inverse.shape[0]), jnp.float32),
        in_specs=vmem(3) + [pl.BlockSpec(memory_space=pl.ANY)],
        out_specs=vmem(1)[0],
        compiler_params=params(),
        name="own_part",
    )(mixed, factor, inverse, late)


def other_core(value):
    return lax.ppermute(value, "tmpl", [(i, i ^ 1) for i in range(8)])


def along_ring(value, by):
    pairs = []
    for i in range(lax.axis_size(("tm", "tmpl"))):
        tm, chip, core = i // 8, i // 2 % 4, i % 2
        to = (tm % 2 * 4 + chip + by) % 8
        pairs.append((i, (tm // 2 * 2 + to // 4) * 8 + to % 4 * 2 + core))
    return lax.ppermute(value, ("tm", "tmpl"), pairs)


def shifted(value, by):
    axis = ("tm", "tmpl")
    count = lax.axis_size(axis)
    return lax.ppermute(value, axis, [(i, i + by) for i in range(count) if 0 <= i + by < count])


def scatter_windows(value):
    count, width = lax.axis_size("tm"), lax.axis_size("tmpl")
    groups = [[(count - 1 - p) * width + j for p in range(count)] for j in range(width)]
    pairs = value.reshape(count, ROWS // 2, 2, 128)
    got = lax.all_to_all(pairs, ("tm", "tmpl"), split_axis=0, concat_axis=0, axis_index_groups=groups, tiled=True)
    return got.reshape(value.shape)


def shards(raw, avail, templates, stations, shifts):
    width = raw.shape[3]
    span = width + L + SMAX
    forward = forward_rows(span, width)
    inverse, inverse_after = inverse_rows(span, width)
    phases = phase_tables(span, SMAX)
    lists = jnp.concatenate([jnp.transpose(stations), jnp.transpose(shifts)], axis=0)
    got = scatter_windows(pack(jnp.transpose(avail[:, 0, :]), raw[:, :, 0, :]))
    own = jnp.transpose(templates, (1, 0, 2))
    tail = jnp.concatenate([own[:4, :, 128:], own[4:, :, 128:]], axis=2)
    own = jnp.concatenate([own[:, :, :128], tail], axis=0)
    pair = jnp.stack([own, other_core(own)])
    blocks = (pair, along_ring(pair, -1), along_ring(pair, 2), along_ring(pair, 1))
    who = lax.axis_index("tmpl").reshape(1)
    waves, top = wave(who, blocks, lists, forward, phases)
    scaled, level, factor = pick(got, lists)
    before = shifted(factor, 1)
    mixed = mix(waves, scaled, top, forward)
    late = late_part(mixed, level, before, inverse_after)
    stack = own_part(mixed, factor, inverse, late)
    return stack + shifted(late, -1).astype(jnp.float32)


def solution(mesh):
    return jax.shard_map(
        shards,
        mesh=mesh,
        in_specs=(
            P("tm", None, "tmpl", None),
            P(None, "tmpl", "tm"),
            P("tmpl", None, None),
            P(),
            P(),
        ),
        out_specs=P(None, ("tm", "tmpl")),
        check_vma=False,
    )
```

time: 66.3 us -> 62.8 us (0.947)
  waiting for transfers between devices: 16.9 us -> 15.1 us
  starting transfers between devices: 38.1 us -> 37.3 us
    all_to_all x1, waiting for transfers between devices: 9.66 us -> 7.39 us  [scatter_windows(): lax.all_to_all(pairs, ('tm', 'tmpl'), split_axis=0, concat_axis=0, axis_i...]
    ppermute x2, starting transfers between devices: 5.6 us -> 4.75 us  [shifted(): lax.ppermute(value, axis, [(i, i + by) for i in range(count) if 0 <= i +...]
    pallas_call x2 -> x3, Pallas kernels: 1.61 us -> 1.7 us  [the longest x1 0.76 us: mix(): pl.pallas_call(mix_kernel, out_shape=jax.ShapeDtypeStruct((span, listed *...]
  transfers between devices with their start and end apart: 7 -> 7, of which waited for: 4 -> 4; matrix products, arithmetic and copies ran while one was open for 0% -> 0% of each run, Pallas kernels for 7% -> 8%
where the time goes in v4:
time: 62.8 us; the launch traced here: 62.4 us
  starting transfers between devices  37.3 us (59%)
  waiting for transfers between devices  15.1 us (24%)
  Pallas kernels  8.77 us (14%)
  other arithmetic  0.85 us (1%)
    all_to_all x1, starting transfers between devices, scatter_windows(): lax.all_to_all(pairs, ('tm', 'tmpl'), split_axis=0, concat_axis=0, axis_i...  20.4 us
    ppermute x3, starting transfers between devices, along_ring(): return lax.ppermute(value, ('tm', 'tmpl'), pairs)  10.3 us
    all_to_all x1, waiting for transfers between devices, scatter_windows(): lax.all_to_all(pairs, ('tm', 'tmpl'), split_axis=0, concat_axis=0, axis_i...  7.39 us
    ppermute x2, waiting for transfers between devices, shifted(): lax.ppermute(value, axis, [(i, i + by) for i in range(count) if 0 <= i +...  6.61 us
    ppermute x2, starting transfers between devices, shifted(): lax.ppermute(value, axis, [(i, i + by) for i in range(count) if 0 <= i +...  4.75 us
    pallas_call x1, Pallas kernels, pack(): pl.pallas_call(pack_kernel, out_shape=jax.ShapeDtypeStruct(shape, jnp.bfl...  3.58 us
    pallas_call x1, Pallas kernels, pick(): pl.pallas_call(pick_kernel, out_shape=(jax.ShapeDtypeStruct((listed * 128...  2.28 us
    ppermute x1, starting transfers between devices, other_core(): return lax.ppermute(value, 'tmpl', [(i, i ^ 1) for i in range(8)])  1.91 us
  transfers between devices with their start and end apart: 7, of which 4 were waited for; matrix products, arithmetic and copies ran while one was open for 0% of the time, Pallas kernels for 8%

profile of v4, /device:TPU:2, one launch (start us, length us, event | category | flops | bytes accessed | tf_op | source)
XLA Modules:
  0.0 62.4 jit_solution(5669346280254159082)
XLA Ops:
  0.0 3.6 %pack.1 = bf16[3200,128]{1,0:T(8,128)(2,1)} custom-call(s32[32,64]{1,0:T(8,128)} %bitcast.21, bf16[32,64,256]{2,1,0:T(8,128)(2,1)} %bitcast.17), custom_call_target="tpu_custom_call" | custom-call | tf_op jit(solution)/shard_map/pack/pallas_call | solution.py:254
  3.6 0.0 copy-start.4
  3.6 20.4 %all-to-all-start = ((bf16[64,25,2,128]{3,2,1,0:T(2,128)(2,1)}), bf16[64,25,2,128]{3,2,1,0:T(2,128)(2,1)S(1)}, u32[]{:S(2)}, u32[]{:S(2)}) async-start(bf16[64,25,2,128]{3,2,1,0:T(2,128)(2,1)} %bitcast.16), calls=%async_computation | async-start | bytes 1638400 | tf_op jit(solution)/shard_map/all_to_all | solution.py:363
  24.0 0.0 copy-done.4
  24.1 0.1 maximum_maximum_fusion
  24.2 1.9 %collective-permute-start = (bf16[12,16,128]{2,1,0:T(8,128)(2,1)S(1)}, bf16[12,16,128]{2,1,0:T(8,128)(2,1)S(1)}, u32[]{:S(2)}, u32[]{:S(2)}) collective-permute-start(bf16[12,16,128]{2,1,0:T(8,128)(2,1)S(1)} %maximum_maximum_fusion), channel_id=1, source_target_pairs={{0,1},{1,0},{2,3},{3,2},{4,5},{5,4},{6,7},{7,6},{8,9},{9,8},{10,11... | collective-permute-start | bytes 147464 | tf_op jit(solution)/shard_map/ppermute | solution.py:341
  26.1 0.1 fusion.1
  26.1 1.1 %collective-permute-done = bf16[12,16,128]{2,1,0:T(8,128)(2,1)S(1)} collective-permute-done((bf16[12,16,128]{2,1,0:T(8,128)(2,1)S(1)}, bf16[12,16,128]{2,1,0:T(8,128)(2,1)S(1)}, u32[]{:S(2)}, u32[]{:S(2)}) %collective-permute-start) | collective-permute-done | bytes 49184 | tf_op jit(solution)/shard_map/ppermute | solution.py:341
  27.3 0.0 copy-start.5
  27.3 0.0 copy-start.6
  27.3 2.7 %collective-permute-start.3 = (bf16[2,12,16,128]{3,2,1,0:T(8,128)(2,1)S(1)}, bf16[2,12,16,128]{3,2,1,0:T(8,128)(2,1)S(1)}, u32[]{:S(2)}, u32[]{:S(2)}) collective-permute-start(bf16[2,12,16,128]{3,2,1,0:T(8,128)(2,1)S(1)} %pad_maximum_fusion.pair_ref), channel_id=1, source_target_pairs={{0,2},{1,3},{2,4},{3,5},{4,6},{5,7},{6,8},{7,9},{8,10},{9,11},{10,... | collective-permute-start | bytes 294920 | tf_op jit(solution)/shard_map/ppermute | solution.py:350
  30.0 4.0 %collective-permute-start.2 = (bf16[2,12,16,128]{3,2,1,0:T(8,128)(2,1)S(1)}, bf16[2,12,16,128]{3,2,1,0:T(8,128)(2,1)S(1)}, u32[]{:S(2)}, u32[]{:S(2)}) collective-permute-start(bf16[2,12,16,128]{3,2,1,0:T(8,128)(2,1)S(1)} %pad_maximum_fusion.pair_ref), channel_id=1, source_target_pairs={{0,4},{1,5},{2,6},{3,7},{4,8},{5,9},{6,10},{7,11},{8,12},{9,13},{1... | collective-permute-start | bytes 294920 | tf_op jit(solution)/shard_map/ppermute | solution.py:350
  34.0 3.6 %collective-permute-start.1 = (bf16[2,12,16,128]{3,2,1,0:T(8,128)(2,1)S(1)}, bf16[2,12,16,128]{3,2,1,0:T(8,128)(2,1)S(1)}, u32[]{:S(2)}, u32[]{:S(2)}) collective-permute-start(bf16[2,12,16,128]{3,2,1,0:T(8,128)(2,1)S(1)} %pad_maximum_fusion.pair_ref), channel_id=1, source_target_pairs={{0,14},{1,15},{2,0},{3,1},{4,2},{5,3},{6,4},{7,5},{8,6},{9,7},{10,... | collective-permute-start | bytes 294920 | tf_op jit(solution)/shard_map/ppermute | solution.py:350
  37.6 0.0 copy-done.5
  37.6 0.0 copy-done.6
  37.6 7.4 %all-to-all-done = bf16[64,25,2,128]{3,2,1,0:T(2,128)(2,1)S(1)} async-done(((bf16[64,25,2,128]{3,2,1,0:T(2,128)(2,1)}), bf16[64,25,2,128]{3,2,1,0:T(2,128)(2,1)S(1)}, u32[]{:S(2)}, u32[]{:S(2)}) %all-to-all-start) | async-done | bytes 819232 | tf_op jit(solution)/shard_map/all_to_all | solution.py:363
  45.0 0.0 copy-start
  45.0 0.0 copy-start.1
  45.0 2.3 %pick.1 = (bf16[1024,256]{1,0:T(8,128)(2,1)S(1)}, f32[8,128]{1,0:T(8,128)S(1)}, f32[16,128]{1,0:T(8,128)S(1)}) custom-call(bf16[3200,128]{1,0:T(8,128)(2,1)S(1)} %bitcast.15, s32[16,128]{1,0:T(8,128)S(1)} %pad_add_fusion.lists_ref), custom_call_target="tpu_custom_call" | custom-call | tf_op jit(solution)/shard_map/pick/pallas_call | solution.py:292
  47.3 1.9 %collective-permute-start.4 = (f32[16,128]{1,0:T(8,128)S(1)}, f32[16,128]{1,0:T(8,128)S(1)}, u32[]{:S(2)}, u32[]{:S(2)}) collective-permute-start(f32[16,128]{1,0:T(8,128)S(1)} %get-tuple-element.13.factor_ref), channel_id=1, source_target_pairs={{0,1},{1,2},{2,3},{3,4},{4,5},{5,6},{6,7},{7,8},{8,9},{9,10},{10,1... | collective-permute-start | bytes 24584 | tf_op jit(solution)/shard_map/ppermute | solution.py:356
  49.2 0.0 collective-permute-done.3.left_ref
  49.2 0.0 collective-permute-done.2.cross_ref
  49.3 0.0 collective-permute-done.1.right_ref
  49.3 0.0 copy-done
  49.3 0.0 copy-done.1
  49.3 1.2 %wave.1 = (bf16[8,512,128]{2,1,0:T(8,128)(2,1)S(1)}, f32[8,128]{1,0:T(8,128)S(1)}) custom-call(s32[1]{0:T(128)} %bitcast.who_ref, bf16[2,12,16,128]{3,2,1,0:T(8,128)(2,1)S(1)} %pad_maximum_fusion.pair_ref, bf16[2,12,16,128]{3,2,1,0:T(8,128)(2,1)S(1)} %collective-permute-done.1.right_ref, bf16[2,12,16,128]{3,2,1,0:T(8,128)(2,1)S(1)} %collective-permute-done.2.cross_ref, ...), custom_call_target="tpu_custom_call" | custom-call | tf_op jit(solution)/shard_map/wave/pallas_call | solution.py:276
  50.5 0.0 copy-start.3
  50.5 0.8 %mix.1.mixed_ref = bf16[512,1024]{1,0:T(8,128)(2,1)S(1)} custom-call(bf16[8,512,128]{2,1,0:T(8,128)(2,1)S(1)} %get-tuple-element.10.wave_ref, bf16[1024,256]{1,0:T(8,128)(2,1)S(1)} %get-tuple-element.11.scaled_ref, f32[8,128]{1,0:T(8,128)S(1)} %get-tuple-element.12.top_ref, bf16[512,256]{1,0:T(8,128)(2,1)S(1)} %copy-done), custom_call_target="tpu_custom_call" | custom-call | tf_op jit(solution)/shard_map/mix/pallas_call | solution.py:308
  51.3 5.2 %collective-permute-done.4.factor_ref = f32[16,128]{1,0:T(8,128)S(1)} collective-permute-done((f32[16,128]{1,0:T(8,128)S(1)}, f32[16,128]{1,0:T(8,128)S(1)}, u32[]{:S(2)}, u32[]{:S(2)}) %collective-permute-start.4) | collective-permute-done | bytes 8224 | tf_op jit(solution)/shard_map/ppermute | solution.py:356
  56.5 0.0 copy-done.3
  56.5 0.0 copy-start.2
  56.5 0.5 late_part.1.late_ref
  57.0 2.8 %collective-permute-start.5 = (bf16[128,256]{1,0:T(8,128)(2,1)S(1)}, bf16[128,256]{1,0:T(8,128)(2,1)S(1)}, u32[]{:S(2)}, u32[]{:S(2)}) collective-permute-start(bf16[128,256]{1,0:T(8,128)(2,1)S(1)} %late_part.1.late_ref), channel_id=1, source_target_pairs={{1,0},{2,1},{3,2},{4,3},{5,4},{6,5},{7,6},{8,7},{9,8},{10,9},{11,1... | collective-permute-start | bytes 196616 | tf_op jit(solution)/shard_map/ppermute | solution.py:356
  59.8 0.0 copy-done.2
  59.8 0.5 own_part.1
  60.3 1.4 %collective-permute-done.5 = bf16[128,256]{1,0:T(8,128)(2,1)S(1)} collective-permute-done((bf16[128,256]{1,0:T(8,128)(2,1)S(1)}, bf16[128,256]{1,0:T(8,128)(2,1)S(1)}, u32[]{:S(2)}, u32[]{:S(2)}) %collective-permute-start.5) | collective-permute-done | bytes 65568 | tf_op jit(solution)/shard_map/ppermute | solution.py:356
  61.7 0.7 %convert_add_fusion = f32[128,256]{1,0:T(8,128)} fusion(f32[128,256]{1,0:T(8,128)S(1)} %own_part.1, bf16[128,256]{1,0:T(8,128)(2,1)S(1)} %collective-permute-done.5), kind=kLoop, calls=%fused_computation | loop fusion | flops 65536 | bytes 327680 | tf_op jit(solution)/shard_map/add | solution.py:387
  (5 shorter events, 0.0 us)
Async XLA Ops:
  3.6 20.4 %copy-start.4 = (bf16[16,8,192]{2,1,0:T(8,128)(2,1)S(1)}, bf16[16,8,192]{2,1,0:T(8,128)(2,1)}, u32[]{:S(2)}) copy-start(bf16[16,8,192]{2,1,0:T(8,128)(2,1)} %param.11) | copy-start | bytes 147460
  3.6 41.4 %all-to-all-start = ((bf16[64,25,2,128]{3,2,1,0:T(2,128)(2,1)}), bf16[64,25,2,128]{3,2,1,0:T(2,128)(2,1)S(1)}, u32[]{:S(2)}, u32[]{:S(2)}) async-start(bf16[64,25,2,128]{3,2,1,0:T(2,128)(2,1)} %bitcast.16), calls=%async_computation | async-start | bytes 1638400 | tf_op jit(solution)/shard_map/all_to_all | solution.py:363
  24.2 3.1 %collective-permute-start = (bf16[12,16,128]{2,1,0:T(8,128)(2,1)S(1)}, bf16[12,16,128]{2,1,0:T(8,128)(2,1)S(1)}, u32[]{:S(2)}, u32[]{:S(2)}) collective-permute-start(bf16[12,16,128]{2,1,0:T(8,128)(2,1)S(1)} %maximum_maximum_fusion), channel_id=1, source_target_pairs={{0,1},{1,0},{2,3},{3,2},{4,5},{5,4},{6,7},{7,6},{8,9},{9,8},{10,11... | collective-permute-start | bytes 147464 | tf_op jit(solution)/shard_map/ppermute | solution.py:341
  27.3 10.3 %copy-start.5 = (s32[128,8]{0,1:T(8,128)S(1)}, s32[128,8]{0,1:T(8,128)}, u32[]{:S(2)}) copy-start(s32[128,8]{0,1:T(8,128)} %param.13) | copy-start | bytes 12292
  27.3 10.3 %copy-start.6 = (s32[128,8]{0,1:T(8,128)S(1)}, s32[128,8]{0,1:T(8,128)}, u32[]{:S(2)}) copy-start(s32[128,8]{0,1:T(8,128)} %param.12) | copy-start | bytes 12292
  27.3 22.0 %collective-permute-start.3 = (bf16[2,12,16,128]{3,2,1,0:T(8,128)(2,1)S(1)}, bf16[2,12,16,128]{3,2,1,0:T(8,128)(2,1)S(1)}, u32[]{:S(2)}, u32[]{:S(2)}) collective-permute-start(bf16[2,12,16,128]{3,2,1,0:T(8,128)(2,1)S(1)} %pad_maximum_fusion.pair_ref), channel_id=1, source_target_pairs={{0,2},{1,3},{2,4},{3,5},{4,6},{5,7},{6,8},{7,9},{8,10},{9,11},{10,... | collective-permute-start | bytes 294920 | tf_op jit(solution)/shard_map/ppermute | solution.py:350
  30.0 19.2 %collective-permute-start.2 = (bf16[2,12,16,128]{3,2,1,0:T(8,128)(2,1)S(1)}, bf16[2,12,16,128]{3,2,1,0:T(8,128)(2,1)S(1)}, u32[]{:S(2)}, u32[]{:S(2)}) collective-permute-start(bf16[2,12,16,128]{3,2,1,0:T(8,128)(2,1)S(1)} %pad_maximum_fusion.pair_ref), channel_id=1, source_target_pairs={{0,4},{1,5},{2,6},{3,7},{4,8},{5,9},{6,10},{7,11},{8,12},{9,13},{1... | collective-permute-start | bytes 294920 | tf_op jit(solution)/shard_map/ppermute | solution.py:350
  34.0 15.3 %collective-permute-start.1 = (bf16[2,12,16,128]{3,2,1,0:T(8,128)(2,1)S(1)}, bf16[2,12,16,128]{3,2,1,0:T(8,128)(2,1)S(1)}, u32[]{:S(2)}, u32[]{:S(2)}) collective-permute-start(bf16[2,12,16,128]{3,2,1,0:T(8,128)(2,1)S(1)} %pad_maximum_fusion.pair_ref), channel_id=1, source_target_pairs={{0,14},{1,15},{2,0},{3,1},{4,2},{5,3},{6,4},{7,5},{8,6},{9,7},{10,... | collective-permute-start | bytes 294920 | tf_op jit(solution)/shard_map/ppermute | solution.py:350
  45.0 4.3 %copy-start = (bf16[512,256]{1,0:T(8,128)(2,1)S(1)}, bf16[512,256]{1,0:T(8,128)(2,1)}, u32[]{:S(2)}) copy-start(bf16[512,256]{1,0:T(8,128)(2,1)} %constant.12.clone.forward_ref) | copy-start | bytes 786436
  45.0 4.3 %copy-start.1 = (bf16[1024,64]{1,0:T(8,128)(2,1)S(1)}, bf16[1024,64]{1,0:T(8,128)(2,1)}, u32[]{:S(2)}) copy-start(bf16[1024,64]{1,0:T(8,128)(2,1)} %constant.15.clone.phase_ref) | copy-start | bytes 393220
  47.3 9.2 %collective-permute-start.4 = (f32[16,128]{1,0:T(8,128)S(1)}, f32[16,128]{1,0:T(8,128)S(1)}, u32[]{:S(2)}, u32[]{:S(2)}) collective-permute-start(f32[16,128]{1,0:T(8,128)S(1)} %get-tuple-element.13.factor_ref), channel_id=1, source_target_pairs={{0,1},{1,2},{2,3},{3,4},{4,5},{5,6},{6,7},{7,8},{8,9},{9,10},{10,1... | collective-permute-start | bytes 24584 | tf_op jit(solution)/shard_map/ppermute | solution.py:356
  50.5 6.0 %copy-start.3 = (bf16[256,512]{1,0:T(8,128)(2,1)S(1)}, bf16[256,512]{1,0:T(8,128)(2,1)}, u32[]{:S(2)}) copy-start(bf16[256,512]{1,0:T(8,128)(2,1)} %constant.14.clone.inverse_ref) | copy-start | bytes 786436
  56.5 3.3 %copy-start.2 = (bf16[256,512]{1,0:T(8,128)(2,1)S(1)}, bf16[256,512]{1,0:T(8,128)(2,1)}, u32[]{:S(2)}) copy-start(bf16[256,512]{1,0:T(8,128)(2,1)} %constant.13.clone.inverse_ref) | copy-start | bytes 786436
  57.0 4.7 %collective-permute-start.5 = (bf16[128,256]{1,0:T(8,128)(2,1)S(1)}, bf16[128,256]{1,0:T(8,128)(2,1)S(1)}, u32[]{:S(2)}, u32[]{:S(2)}) collective-permute-start(bf16[128,256]{1,0:T(8,128)(2,1)S(1)} %late_part.1.late_ref), channel_id=1, source_target_pairs={{1,0},{2,1},{3,2},{4,3},{5,4},{6,5},{7,6},{8,7},{9,8},{10,9},{11,1... | collective-permute-start | bytes 196616 | tf_op jit(solution)/shard_map/ppermute | solution.py:356

commit v5 on v4

--- a/solution.py
+++ b/solution.py
@@ -14,6 +14,7 @@
 CAP = 24
 ROWS = 2 * CAP + 2
 GROUP = 16
+FIRST = 64
 MISSING = 4096.0
 LIMIT = 3e38
 
@@ -50,14 +51,9 @@
     )
 
 
-def phase_tables(span, moves):
+def phase_table(span, moves):
     angle = (np.arange(span // 2)[:, None] * np.arange(moves)[None, :] % span) * (2.0 * math.pi / span)
-    parts = []
-    for value in (np.cos(angle), np.sin(angle)):
-        high = value.astype(jnp.bfloat16)
-        parts.append(high)
-        parts.append((value - high.astype(np.float64)).astype(jnp.bfloat16))
-    return jnp.asarray(np.concatenate(parts))
+    return jnp.asarray(np.concatenate([np.cos(angle), np.sin(angle)]).astype(jnp.bfloat16))
 
 
 def dot(a, b):
@@ -96,10 +92,10 @@
     status.start()
     for part in range(parts):
         fetch(part).start()
-    place = (iota((count, 128), 0) == iota((count, 128), 1)).astype(jnp.bfloat16)
-    before = (iota((count, 128), 0) < iota((count, 128), 1)).astype(jnp.bfloat16)
+    place = (iota((count, 128), 0) == iota((count, 128), 1) - FIRST).astype(jnp.bfloat16)
+    before = (iota((count, 128), 0) < iota((count, 128), 1) - FIRST).astype(jnp.bfloat16)
     lanes = count * GROUP
-    spread = (iota((128, lanes), 0) == iota((128, lanes), 1) // GROUP).astype(jnp.bfloat16)
+    spread = (iota((128, lanes), 0) - FIRST == iota((128, lanes), 1) // GROUP).astype(jnp.bfloat16)
     slot = iota((GROUP, CAP, lanes), 1).astype(jnp.float32)
     status.wait()
     flags = jnp.transpose(flags_ref[...].astype(jnp.float32)).astype(jnp.bfloat16)
@@ -125,38 +121,18 @@
         store(part).wait()
 
 
-def wave_kernel(who_ref, pair_ref, right_ref, cross_ref, left_ref, lists_ref, forward_ref, phase_ref,
-                wave_ref, top_ref, rows_ref):
-    listed, span = wave_ref.shape[0], wave_ref.shape[1]
-    half = span // 2
-    chip, core = who_ref[0] // 2, who_ref[0] % 2
-    group = pair_ref.shape[2]
-    rows_ref[:, 128:] = jnp.zeros((listed * 128, rows_ref.shape[1] - 128), jnp.bfloat16)
-    for away, ref in enumerate((pair_ref, right_ref, cross_ref, left_ref)):
-        for other in range(2):
-            owner = lax.rem(chip + away, 4) * 2 + lax.rem(core + other, 2)
-            for q in range(listed):
-                at = pl.ds(pl.multiple_of(q * 128 + owner * group, group), group)
-                rows_ref[at, 0:128] = ref[other, q]
-                tail = ref[other, listed + q % 4]
-                rows_ref[at, 128:L] = tail[:, : L - 128] if q < 4 else tail[:, L - 128 :]
-    zero = iota((half, 128), 0) == 0
+def find_kernel(lists_ref, find_ref):
+    listed = lists_ref.shape[0] // 2
+    eye = iota((128, 128), 0) == iota((128, 128), 1)
+    lane = iota((128, 128), 1)
     for q in range(listed):
-        move = lists_ref[listed + q : listed + q + 1, :]
-        angles = dot(phase_ref[...], (iota((SMAX, 128), 0) == move).astype(jnp.bfloat16))
-        cosine = angles[:half] + angles[half : 2 * half]
-        sine = angles[2 * half : 3 * half] + angles[3 * half :]
-        sign = 1.0 - 2.0 * (move % 2).astype(jnp.float32)
-        if q % 2 == 0:
-            spectra = dot_rows(forward_ref[...], rows_ref[q * 128 : (q + 2) * 128, :])
-        spectrum = spectra[:, q % 2 * 128 : (q % 2 + 1) * 128]
-        real, imag = spectrum[:half], spectrum[half:]
-        wave_ref[q, :half] = jnp.where(zero, real, real * cosine + imag * sine).astype(jnp.bfloat16)
-        wave_ref[q, half:] = jnp.where(zero, 0.0, real * sine - imag * cosine).astype(jnp.bfloat16)
-        top_ref[q : q + 1, :] = imag[0:1] * sign
-
-
-def pick_kernel(got_ref, lists_ref, scaled_ref, level_ref, factor_ref):
+        station = to_column(lists_ref[q : q + 1, :].astype(jnp.float32), eye).astype(jnp.int32)
+        block = lane == FIRST - 1 - station // 32
+        place = jnp.logical_or(lane == FIRST + station % 32, lane == FIRST + 32)
+        find_ref[q * 128 : (q + 1) * 128, :] = jnp.logical_or(block, place).astype(jnp.bfloat16)
+
+
+def pick_kernel(got_ref, find_ref, scaled_ref, level_ref, factor_ref):
     blocks = got_ref.shape[0] // ROWS
     slots = blocks * CAP
     listed = level_ref.shape[0]
@@ -165,21 +141,18 @@
         rows = [got_ref[block * ROWS + first : block * ROWS + first + size, :] for block in range(blocks)]
         return [value.astype(jnp.float32) for value in rows]
 
+    codes = jnp.concatenate([value[0:1] for value in gather(2 * CAP, 2)], axis=0)
+    lane = iota((blocks, 128), 1)
+    codes = jnp.where(jnp.logical_and(lane >= FIRST, lane < FIRST + 32), codes, 0.0)
+    codes = jnp.where(lane == FIRST + 32, iota((blocks, 128), 0).astype(jnp.float32) * CAP, codes)
+    codes = jnp.concatenate([codes, jnp.zeros((128 - blocks, 128), jnp.float32)], axis=0).astype(jnp.bfloat16)
+    find = find_ref[...]
+    targets = jnp.sum(dot(find, codes) * find.astype(jnp.float32), axis=1, keepdims=True)
     low = jnp.concatenate(gather(0, CAP), axis=0).astype(jnp.bfloat16)
     high = jnp.concatenate(gather(CAP, CAP), axis=0).astype(jnp.bfloat16)
     waves = jnp.concatenate([low, high], axis=1)
     width = waves.shape[1]
-    codes = jnp.concatenate([value[0:1] for value in gather(2 * CAP, 2)], axis=0)
-    start = iota((blocks, 128), 0).astype(jnp.float32) * CAP
-    codes = jnp.where(iota((blocks, 128), 1) == 64, start, codes).astype(jnp.bfloat16)
-    codes = jnp.concatenate([codes, jnp.zeros((128 - blocks, 128), jnp.bfloat16)], axis=0)
     eye = iota((128, 128), 0) == iota((128, 128), 1)
-    columns = [to_column(lists_ref[q : q + 1, :].astype(jnp.float32), eye) for q in range(listed)]
-    station = jnp.concatenate(columns, axis=0).astype(jnp.int32)
-    lane = iota((listed * 128, 128), 1)
-    holder = (lane == blocks - 1 - station // 32).astype(jnp.bfloat16)
-    mask = jnp.logical_or(lane == station % 32, lane == 64)
-    targets = jnp.sum(jnp.where(mask, dot(holder, codes), 0.0), axis=1, keepdims=True)
     total = jnp.zeros((1, 128), jnp.float32)
     for pair in range(listed // 2):
         cols = slice(pair * 256, (pair + 1) * 256)
@@ -201,19 +174,37 @@
     factor_ref[listed : listed + 8, :] = jnp.broadcast_to(1.0 / jnp.maximum(total, 1.0), (8, 128))
 
 
-def mix_kernel(wave_ref, scaled_ref, top_ref, forward_ref, mixed_ref):
-    listed, span = wave_ref.shape[0], wave_ref.shape[1]
+def mix_kernel(who_ref, pair_ref, right_ref, cross_ref, left_ref, lists_ref, scaled_ref, forward_ref, phase_ref,
+               mixed_ref, rows_ref):
+    listed, span = lists_ref.shape[0] // 2, mixed_ref.shape[0]
     half = span // 2
-    zero = iota((half, 128), 0) == 0
-    for q in range(listed):
-        if q % 2 == 0:
-            spectra = dot_rows(forward_ref[...], scaled_ref[q * 128 : (q + 2) * 128, :])
-        spectrum = spectra[:, q % 2 * 128 : (q % 2 + 1) * 128]
-        cols = slice(q * 128, (q + 1) * 128)
+    chip, core = who_ref[0] // 2, who_ref[0] % 2
+    group = pair_ref.shape[2]
+    rows_ref[:, 128:] = jnp.zeros((listed * 128, rows_ref.shape[1] - 128), jnp.bfloat16)
+    for away, ref in enumerate((pair_ref, right_ref, cross_ref, left_ref)):
+        for other in range(2):
+            owner = lax.rem(chip + away, 4) * 2 + lax.rem(core + other, 2)
+            for q in range(listed):
+                at = pl.ds(pl.multiple_of(q * 128 + owner * group, group), group)
+                rows_ref[at, 0:128] = ref[other, q]
+                tail = ref[other, listed + q % 4]
+                rows_ref[at, 128:L] = tail[:, : L - 128] if q < 4 else tail[:, L - 128 :]
+    zero = iota((half, 256), 0) == 0
+    for pair in range(listed // 2):
+        cols = slice(pair * 256, (pair + 1) * 256)
+        first = listed + 2 * pair
+        move = jnp.concatenate([lists_ref[first : first + 1, :], lists_ref[first + 1 : first + 2, :]], axis=1)
+        angles = dot(phase_ref[...], (iota((SMAX, 256), 0) == move).astype(jnp.bfloat16))
+        cosine, sine = angles[:half], angles[half:]
+        sign = 1.0 - 2.0 * (move % 2).astype(jnp.float32)
+        template = dot_rows(forward_ref[...], rows_ref[cols, :])
+        spectrum = dot_rows(forward_ref[...], scaled_ref[cols, :])
         real, imag = spectrum[:half], spectrum[half:]
-        wave_real = wave_ref[q, :half].astype(jnp.float32)
-        wave_imag = wave_ref[q, half:].astype(jnp.float32)
-        straight = jnp.where(zero, top_ref[q : q + 1, :], wave_real)
+        wave_real = template[:half] * cosine + template[half:] * sine
+        wave_imag = template[:half] * sine - template[half:] * cosine
+        wave_real = jnp.where(zero, template[:half], wave_real)
+        wave_imag = jnp.where(zero, 0.0, wave_imag)
+        straight = jnp.where(zero, template[half:] * sign, wave_real)
         mixed_ref[:half, cols] = (wave_real * real - wave_imag * imag).astype(jnp.bfloat16)
         mixed_ref[half:, cols] = (straight * imag + wave_imag * real).astype(jnp.bfloat16)
 
@@ -270,29 +261,25 @@
     )(status, waves)
 
 
-def wave(who, blocks, lists, forward, phases):
-    span = forward.shape[0]
-    listed = lists.shape[0] // 2
-    return pl.pallas_call(
-        wave_kernel,
-        out_shape=(
-            jax.ShapeDtypeStruct((listed, span, 128), jnp.bfloat16),
-            jax.ShapeDtypeStruct((listed, 128), jnp.float32),
-        ),
-        in_specs=[pl.BlockSpec(memory_space=pltpu.SMEM)] + vmem(7),
-        out_specs=tuple(vmem(2)),
-        scratch_shapes=[pltpu.VMEM((listed * 128, forward.shape[1]), jnp.bfloat16)],
-        compiler_params=params(),
-        name="wave",
-    )(who, *blocks, lists, forward, phases)
-
-
-def pick(got, lists):
-    listed = lists.shape[0] // 2
+def find(lists):
+    columns = lists.shape[0] // 2 * 128
+    return pl.pallas_call(
+        find_kernel,
+        out_shape=jax.ShapeDtypeStruct((columns, 128), jnp.bfloat16),
+        in_specs=vmem(1),
+        out_specs=vmem(1)[0],
+        compiler_params=params(),
+        name="find",
+    )(lists)
+
+
+def pick(got, found):
+    columns = found.shape[0]
+    listed = columns // 128
     return pl.pallas_call(
         pick_kernel,
         out_shape=(
-            jax.ShapeDtypeStruct((listed * 128, 256), jnp.bfloat16),
+            jax.ShapeDtypeStruct((columns, 256), jnp.bfloat16),
             jax.ShapeDtypeStruct((listed, 128), jnp.float32),
             jax.ShapeDtypeStruct((listed + 8, 128), jnp.float32),
         ),
@@ -300,19 +287,20 @@
         out_specs=tuple(vmem(3)),
         compiler_params=params(),
         name="pick",
-    )(got, lists)
-
-
-def mix(waves, scaled, top, forward):
-    listed, span = waves.shape[0], waves.shape[1]
+    )(got, found)
+
+
+def mix(who, blocks, lists, scaled, forward, phases):
+    columns = scaled.shape[0]
     return pl.pallas_call(
         mix_kernel,
-        out_shape=jax.ShapeDtypeStruct((span, listed * 128), jnp.bfloat16),
-        in_specs=vmem(4),
+        out_shape=jax.ShapeDtypeStruct((forward.shape[0], columns), jnp.bfloat16),
+        in_specs=[pl.BlockSpec(memory_space=pltpu.SMEM)] + vmem(8),
         out_specs=vmem(1)[0],
+        scratch_shapes=[pltpu.VMEM((columns, forward.shape[1]), jnp.bfloat16)],
         compiler_params=params(),
         name="mix",
-    )(waves, scaled, top, forward)
+    )(who, *blocks, lists, scaled, forward, phases)
 
 
 def late_part(mixed, level, factor, inverse):
@@ -369,7 +357,7 @@
     span = width + L + SMAX
     forward = forward_rows(span, width)
     inverse, inverse_after = inverse_rows(span, width)
-    phases = phase_tables(span, SMAX)
+    phases = phase_table(span, SMAX)
     lists = jnp.concatenate([jnp.transpose(stations), jnp.transpose(shifts)], axis=0)
     got = scatter_windows(pack(jnp.transpose(avail[:, 0, :]), raw[:, :, 0, :]))
     own = jnp.transpose(templates, (1, 0, 2))
@@ -378,10 +366,9 @@
     pair = jnp.stack([own, other_core(own)])
     blocks = (pair, along_ring(pair, -1), along_ring(pair, 2), along_ring(pair, 1))
     who = lax.axis_index("tmpl").reshape(1)
-    waves, top = wave(who, blocks, lists, forward, phases)
-    scaled, level, factor = pick(got, lists)
+    scaled, level, factor = pick(got, find(lists))
     before = shifted(factor, 1)
-    mixed = mix(waves, scaled, top, forward)
+    mixed = mix(who, blocks, lists, scaled, forward, phases)
     late = late_part(mixed, level, before, inverse_after)
     stack = own_part(mixed, factor, inverse, late)
     return stack + shifted(late, -1).astype(jnp.float32)

time: 62.8 us -> 61.1 us (0.973)
  starting transfers between devices: 37.3 us -> 35.2 us
  waiting for transfers between devices: 15.1 us -> 16.5 us
  Pallas kernels: 8.77 us -> 7.85 us
    ppermute x3, starting transfers between devices: 10.3 us -> 9.06 us  [along_ring(): return lax.ppermute(value, ('tm', 'tmpl'), pairs)]
    pallas_call x3, Pallas kernels: 4.25 us -> 3.38 us  [the longest x1 1.53 us: pick(): pl.pallas_call(pick_kernel, out_shape=(jax.ShapeDtypeStruct((columns, 256...]
    ppermute x2, starting transfers between devices: 4.75 us -> 3.88 us  [shifted(): lax.ppermute(value, axis, [(i, i + by) for i in range(count) if 0 <= i +...]
    ppermute x2, waiting for transfers between devices: 6.61 us -> 7.33 us  [shifted(): lax.ppermute(value, axis, [(i, i + by) for i in range(count) if 0 <= i +...]
  transfers between devices with their start and end apart: 7 -> 7, of which waited for: 4 -> 4; matrix products, arithmetic and copies ran while one was open for 0% -> 0% of each run, Pallas kernels for 8% -> 6%
where the time goes in v5:
time: 61.1 us; the launch traced here: 60.7 us
  starting transfers between devices  35.2 us (58%)
  waiting for transfers between devices  16.5 us (27%)
  Pallas kernels  7.85 us (13%)
  other arithmetic  0.85 us (1%)
    all_to_all x1, starting transfers between devices, scatter_windows(): lax.all_to_all(pairs, ('tm', 'tmpl'), split_axis=0, concat_axis=0, axis_i...  20.4 us
    ppermute x3, starting transfers between devices, along_ring(): return lax.ppermute(value, ('tm', 'tmpl'), pairs)  9.06 us
    all_to_all x1, waiting for transfers between devices, scatter_windows(): lax.all_to_all(pairs, ('tm', 'tmpl'), split_axis=0, concat_axis=0, axis_i...  8 us
    ppermute x2, waiting for transfers between devices, shifted(): lax.ppermute(value, axis, [(i, i + by) for i in range(count) if 0 <= i +...  7.33 us
    ppermute x2, starting transfers between devices, shifted(): lax.ppermute(value, axis, [(i, i + by) for i in range(count) if 0 <= i +...  3.88 us
    pallas_call x1, Pallas kernels, pack(): pl.pallas_call(pack_kernel, out_shape=jax.ShapeDtypeStruct(shape, jnp.bfl...  3.52 us
    ppermute x1, starting transfers between devices, other_core(): return lax.ppermute(value, 'tmpl', [(i, i ^ 1) for i in range(8)])  1.91 us
    pallas_call x1, Pallas kernels, pick(): pl.pallas_call(pick_kernel, out_shape=(jax.ShapeDtypeStruct((columns, 256...  1.53 us
  transfers between devices with their start and end apart: 7, of which 4 were waited for; matrix products, arithmetic and copies ran while one was open for 0% of the time, Pallas kernels for 6%

profile of v5, /device:TPU:2, one launch (start us, length us, event | category | flops | bytes accessed | tf_op | source)
XLA Modules:
  0.0 60.7 jit_solution(13211027810793501457)
XLA Ops:
  0.0 3.5 %pack.1 = bf16[3200,128]{1,0:T(8,128)(2,1)} custom-call(s32[32,64]{1,0:T(8,128)} %bitcast.21, bf16[32,64,256]{2,1,0:T(8,128)(2,1)} %bitcast.17), custom_call_target="tpu_custom_call" | custom-call | tf_op jit(solution)/shard_map/pack/pallas_call | solution.py:245
  3.5 0.0 copy-start.4
  3.5 20.4 %all-to-all-start = ((bf16[64,25,2,128]{3,2,1,0:T(2,128)(2,1)}), bf16[64,25,2,128]{3,2,1,0:T(2,128)(2,1)S(1)}, u32[]{:S(2)}, u32[]{:S(2)}) async-start(bf16[64,25,2,128]{3,2,1,0:T(2,128)(2,1)} %bitcast.16), calls=%async_computation | async-start | bytes 1638400 | tf_op jit(solution)/shard_map/all_to_all | solution.py:351
  24.0 0.0 copy-done.4
  24.0 0.1 maximum_maximum_fusion
  24.1 1.9 %collective-permute-start = (bf16[12,16,128]{2,1,0:T(8,128)(2,1)S(1)}, bf16[12,16,128]{2,1,0:T(8,128)(2,1)S(1)}, u32[]{:S(2)}, u32[]{:S(2)}) collective-permute-start(bf16[12,16,128]{2,1,0:T(8,128)(2,1)S(1)} %maximum_maximum_fusion), channel_id=1, source_target_pairs={{0,1},{1,0},{2,3},{3,2},{4,5},{5,4},{6,7},{7,6},{8,9},{9,8},{10,11... | collective-permute-start | bytes 147464 | tf_op jit(solution)/shard_map/ppermute | solution.py:329
  26.0 0.1 fusion.1
  26.1 1.1 %collective-permute-done = bf16[12,16,128]{2,1,0:T(8,128)(2,1)S(1)} collective-permute-done((bf16[12,16,128]{2,1,0:T(8,128)(2,1)S(1)}, bf16[12,16,128]{2,1,0:T(8,128)(2,1)S(1)}, u32[]{:S(2)}, u32[]{:S(2)}) %collective-permute-start) | collective-permute-done | bytes 49184 | tf_op jit(solution)/shard_map/ppermute | solution.py:329
  27.2 0.0 copy-start.5
  27.2 0.0 copy-start.6
  27.2 2.1 %collective-permute-start.1 = (bf16[2,12,16,128]{3,2,1,0:T(8,128)(2,1)S(1)}, bf16[2,12,16,128]{3,2,1,0:T(8,128)(2,1)S(1)}, u32[]{:S(2)}, u32[]{:S(2)}) collective-permute-start(bf16[2,12,16,128]{3,2,1,0:T(8,128)(2,1)S(1)} %pad_maximum_fusion.pair_ref), channel_id=1, source_target_pairs={{0,14},{1,15},{2,0},{3,1},{4,2},{5,3},{6,4},{7,5},{8,6},{9,7},{10,... | collective-permute-start | bytes 294920 | tf_op jit(solution)/shard_map/ppermute | solution.py:338
  29.3 4.0 %collective-permute-start.2 = (bf16[2,12,16,128]{3,2,1,0:T(8,128)(2,1)S(1)}, bf16[2,12,16,128]{3,2,1,0:T(8,128)(2,1)S(1)}, u32[]{:S(2)}, u32[]{:S(2)}) collective-permute-start(bf16[2,12,16,128]{3,2,1,0:T(8,128)(2,1)S(1)} %pad_maximum_fusion.pair_ref), channel_id=1, source_target_pairs={{0,4},{1,5},{2,6},{3,7},{4,8},{5,9},{6,10},{7,11},{8,12},{9,13},{1... | collective-permute-start | bytes 294920 | tf_op jit(solution)/shard_map/ppermute | solution.py:338
  33.3 3.0 %collective-permute-start.3 = (bf16[2,12,16,128]{3,2,1,0:T(8,128)(2,1)S(1)}, bf16[2,12,16,128]{3,2,1,0:T(8,128)(2,1)S(1)}, u32[]{:S(2)}, u32[]{:S(2)}) collective-permute-start(bf16[2,12,16,128]{3,2,1,0:T(8,128)(2,1)S(1)} %pad_maximum_fusion.pair_ref), channel_id=1, source_target_pairs={{0,2},{1,3},{2,4},{3,5},{4,6},{5,7},{6,8},{7,9},{8,10},{9,11},{10,... | collective-permute-start | bytes 294920 | tf_op jit(solution)/shard_map/ppermute | solution.py:338
  36.3 0.0 copy-done.5
  36.3 0.0 copy-done.6
  36.3 0.6 find.1.find_ref
  36.9 8.0 %all-to-all-done = bf16[64,25,2,128]{3,2,1,0:T(2,128)(2,1)S(1)} async-done(((bf16[64,25,2,128]{3,2,1,0:T(2,128)(2,1)}), bf16[64,25,2,128]{3,2,1,0:T(2,128)(2,1)S(1)}, u32[]{:S(2)}, u32[]{:S(2)}) %all-to-all-start) | async-done | bytes 819232 | tf_op jit(solution)/shard_map/all_to_all | solution.py:351
  45.0 0.0 copy-start.2
  45.0 0.0 copy-start.3
  45.0 1.5 %pick.1 = (bf16[1024,256]{1,0:T(8,128)(2,1)S(1)}, f32[8,128]{1,0:T(8,128)S(1)}, f32[16,128]{1,0:T(8,128)S(1)}) custom-call(bf16[3200,128]{1,0:T(8,128)(2,1)S(1)} %bitcast.15, bf16[1024,128]{1,0:T(8,128)(2,1)S(1)} %find.1.find_ref), custom_call_target="tpu_custom_call" | custom-call | tf_op jit(solution)/shard_map/pick/pallas_call | solution.py:279
  46.5 1.9 %collective-permute-start.4 = (f32[16,128]{1,0:T(8,128)S(1)}, f32[16,128]{1,0:T(8,128)S(1)}, u32[]{:S(2)}, u32[]{:S(2)}) collective-permute-start(f32[16,128]{1,0:T(8,128)S(1)} %get-tuple-element.9.factor_ref), channel_id=1, source_target_pairs={{0,1},{1,2},{2,3},{3,4},{4,5},{5,6},{6,7},{7,8},{8,9},{9,10},{10,1... | collective-permute-start | bytes 24584 | tf_op jit(solution)/shard_map/ppermute | solution.py:344
  48.4 0.0 collective-permute-done.1.right_ref
  48.4 0.0 collective-permute-done.2.cross_ref
  48.4 0.0 collective-permute-done.3.left_ref
  48.5 0.0 copy-done.2
  48.5 0.0 copy-done.3
  48.5 0.0 copy-start.1
  48.5 1.3 %mix.1.mixed_ref = bf16[512,1024]{1,0:T(8,128)(2,1)S(1)} custom-call(s32[1]{0:T(128)} %bitcast.who_ref, bf16[2,12,16,128]{3,2,1,0:T(8,128)(2,1)S(1)} %pad_maximum_fusion.pair_ref, bf16[2,12,16,128]{3,2,1,0:T(8,128)(2,1)S(1)} %collective-permute-done.1.right_ref, bf16[2,12,16,128]{3,2,1,0:T(8,128)(2,1)S(1)} %collective-permute-done.2.cross_ref, ...), custom_call_target="tpu_custom_call" | custom-call | tf_op jit(solution)/shard_map/mix/pallas_call | solution.py:295
  49.8 5.9 %collective-permute-done.4.factor_ref = f32[16,128]{1,0:T(8,128)S(1)} collective-permute-done((f32[16,128]{1,0:T(8,128)S(1)}, f32[16,128]{1,0:T(8,128)S(1)}, u32[]{:S(2)}, u32[]{:S(2)}) %collective-permute-start.4) | collective-permute-done | bytes 8224 | tf_op jit(solution)/shard_map/ppermute | solution.py:344
  55.7 0.0 copy-done.1
  55.7 0.0 copy-start
  55.7 0.5 late_part.1.late_ref
  56.2 2.0 %collective-permute-start.5 = (bf16[128,256]{1,0:T(8,128)(2,1)S(1)}, bf16[128,256]{1,0:T(8,128)(2,1)S(1)}, u32[]{:S(2)}, u32[]{:S(2)}) collective-permute-start(bf16[128,256]{1,0:T(8,128)(2,1)S(1)} %late_part.1.late_ref), channel_id=1, source_target_pairs={{1,0},{2,1},{3,2},{4,3},{5,4},{6,5},{7,6},{8,7},{9,8},{10,9},{11,1... | collective-permute-start | bytes 196616 | tf_op jit(solution)/shard_map/ppermute | solution.py:344
  58.1 0.0 copy-done
  58.1 0.5 own_part.1
  58.6 1.4 %collective-permute-done.5 = bf16[128,256]{1,0:T(8,128)(2,1)S(1)} collective-permute-done((bf16[128,256]{1,0:T(8,128)(2,1)S(1)}, bf16[128,256]{1,0:T(8,128)(2,1)S(1)}, u32[]{:S(2)}, u32[]{:S(2)}) %collective-permute-start.5) | collective-permute-done | bytes 65568 | tf_op jit(solution)/shard_map/ppermute | solution.py:344
  60.0 0.7 %convert_add_fusion = f32[128,256]{1,0:T(8,128)} fusion(f32[128,256]{1,0:T(8,128)S(1)} %own_part.1, bf16[128,256]{1,0:T(8,128)(2,1)S(1)} %collective-permute-done.5), kind=kLoop, calls=%fused_computation | loop fusion | flops 65536 | bytes 327680 | tf_op jit(solution)/shard_map/add | solution.py:374
  (5 shorter events, 0.0 us)
Async XLA Ops:
  3.5 20.4 %copy-start.4 = (bf16[16,8,192]{2,1,0:T(8,128)(2,1)S(1)}, bf16[16,8,192]{2,1,0:T(8,128)(2,1)}, u32[]{:S(2)}) copy-start(bf16[16,8,192]{2,1,0:T(8,128)(2,1)} %param.11) | copy-start | bytes 147460
  3.5 41.4 %all-to-all-start = ((bf16[64,25,2,128]{3,2,1,0:T(2,128)(2,1)}), bf16[64,25,2,128]{3,2,1,0:T(2,128)(2,1)S(1)}, u32[]{:S(2)}, u32[]{:S(2)}) async-start(bf16[64,25,2,128]{3,2,1,0:T(2,128)(2,1)} %bitcast.16), calls=%async_computation | async-start | bytes 1638400 | tf_op jit(solution)/shard_map/all_to_all | solution.py:351
  24.1 3.1 %collective-permute-start = (bf16[12,16,128]{2,1,0:T(8,128)(2,1)S(1)}, bf16[12,16,128]{2,1,0:T(8,128)(2,1)S(1)}, u32[]{:S(2)}, u32[]{:S(2)}) collective-permute-start(bf16[12,16,128]{2,1,0:T(8,128)(2,1)S(1)} %maximum_maximum_fusion), channel_id=1, source_target_pairs={{0,1},{1,0},{2,3},{3,2},{4,5},{5,4},{6,7},{7,6},{8,9},{9,8},{10,11... | collective-permute-start | bytes 147464 | tf_op jit(solution)/shard_map/ppermute | solution.py:329
  27.2 9.1 %copy-start.5 = (s32[128,8]{0,1:T(8,128)S(1)}, s32[128,8]{0,1:T(8,128)}, u32[]{:S(2)}) copy-start(s32[128,8]{0,1:T(8,128)} %param.13) | copy-start | bytes 12292
  27.2 9.1 %copy-start.6 = (s32[128,8]{0,1:T(8,128)S(1)}, s32[128,8]{0,1:T(8,128)}, u32[]{:S(2)}) copy-start(s32[128,8]{0,1:T(8,128)} %param.12) | copy-start | bytes 12292
  27.2 21.2 %collective-permute-start.1 = (bf16[2,12,16,128]{3,2,1,0:T(8,128)(2,1)S(1)}, bf16[2,12,16,128]{3,2,1,0:T(8,128)(2,1)S(1)}, u32[]{:S(2)}, u32[]{:S(2)}) collective-permute-start(bf16[2,12,16,128]{3,2,1,0:T(8,128)(2,1)S(1)} %pad_maximum_fusion.pair_ref), channel_id=1, source_target_pairs={{0,14},{1,15},{2,0},{3,1},{4,2},{5,3},{6,4},{7,5},{8,6},{9,7},{10,... | collective-permute-start | bytes 294920 | tf_op jit(solution)/shard_map/ppermute | solution.py:338
  29.3 19.1 %collective-permute-start.2 = (bf16[2,12,16,128]{3,2,1,0:T(8,128)(2,1)S(1)}, bf16[2,12,16,128]{3,2,1,0:T(8,128)(2,1)S(1)}, u32[]{:S(2)}, u32[]{:S(2)}) collective-permute-start(bf16[2,12,16,128]{3,2,1,0:T(8,128)(2,1)S(1)} %pad_maximum_fusion.pair_ref), channel_id=1, source_target_pairs={{0,4},{1,5},{2,6},{3,7},{4,8},{5,9},{6,10},{7,11},{8,12},{9,13},{1... | collective-permute-start | bytes 294920 | tf_op jit(solution)/shard_map/ppermute | solution.py:338
  33.3 15.1 %collective-permute-start.3 = (bf16[2,12,16,128]{3,2,1,0:T(8,128)(2,1)S(1)}, bf16[2,12,16,128]{3,2,1,0:T(8,128)(2,1)S(1)}, u32[]{:S(2)}, u32[]{:S(2)}) collective-permute-start(bf16[2,12,16,128]{3,2,1,0:T(8,128)(2,1)S(1)} %pad_maximum_fusion.pair_ref), channel_id=1, source_target_pairs={{0,2},{1,3},{2,4},{3,5},{4,6},{5,7},{6,8},{7,9},{8,10},{9,11},{10,... | collective-permute-start | bytes 294920 | tf_op jit(solution)/shard_map/ppermute | solution.py:338
  45.0 3.5 %copy-start.2 = (bf16[512,256]{1,0:T(8,128)(2,1)S(1)}, bf16[512,256]{1,0:T(8,128)(2,1)}, u32[]{:S(2)}) copy-start(bf16[512,256]{1,0:T(8,128)(2,1)} %constant.12.clone.forward_ref) | copy-start | bytes 786436
  45.0 3.5 %copy-start.3 = (bf16[512,64]{1,0:T(8,128)(2,1)S(1)}, bf16[512,64]{1,0:T(8,128)(2,1)}, u32[]{:S(2)}) copy-start(bf16[512,64]{1,0:T(8,128)(2,1)} %constant.15.clone.phase_ref) | copy-start | bytes 196612
  46.5 9.2 %collective-permute-start.4 = (f32[16,128]{1,0:T(8,128)S(1)}, f32[16,128]{1,0:T(8,128)S(1)}, u32[]{:S(2)}, u32[]{:S(2)}) collective-permute-start(f32[16,128]{1,0:T(8,128)S(1)} %get-tuple-element.9.factor_ref), channel_id=1, source_target_pairs={{0,1},{1,2},{2,3},{3,4},{4,5},{5,6},{6,7},{7,8},{8,9},{9,10},{10,1... | collective-permute-start | bytes 24584 | tf_op jit(solution)/shard_map/ppermute | solution.py:344
  48.5 7.2 %copy-start.1 = (bf16[256,512]{1,0:T(8,128)(2,1)S(1)}, bf16[256,512]{1,0:T(8,128)(2,1)}, u32[]{:S(2)}) copy-start(bf16[256,512]{1,0:T(8,128)(2,1)} %constant.14.clone.inverse_ref) | copy-start | bytes 786436
  55.7 2.4 %copy-start = (bf16[256,512]{1,0:T(8,128)(2,1)S(1)}, bf16[256,512]{1,0:T(8,128)(2,1)}, u32[]{:S(2)}) copy-start(bf16[256,512]{1,0:T(8,128)(2,1)} %constant.13.clone.inverse_ref) | copy-start | bytes 786436
  56.2 3.9 %collective-permute-start.5 = (bf16[128,256]{1,0:T(8,128)(2,1)S(1)}, bf16[128,256]{1,0:T(8,128)(2,1)S(1)}, u32[]{:S(2)}, u32[]{:S(2)}) collective-permute-start(bf16[128,256]{1,0:T(8,128)(2,1)S(1)} %late_part.1.late_ref), channel_id=1, source_target_pairs={{1,0},{2,1},{3,2},{4,3},{5,4},{6,5},{7,6},{8,7},{9,8},{10,9},{11,1... | collective-permute-start | bytes 196616 | tf_op jit(solution)/shard_map/ppermute | solution.py:344

commit v6 on v5

--- a/solution.py
+++ b/solution.py
@@ -90,7 +90,7 @@
 
     status = pltpu.make_async_copy(avail_ref, flags_ref, flag_sem)
     status.start()
-    for part in range(parts):
+    for part in range(parts // 2):
         fetch(part).start()
     place = (iota((count, 128), 0) == iota((count, 128), 1) - FIRST).astype(jnp.bfloat16)
     before = (iota((count, 128), 0) < iota((count, 128), 1) - FIRST).astype(jnp.bfloat16)
@@ -106,6 +106,8 @@
         own = wide[part * GROUP : (part + 1) * GROUP]
         mover = jnp.where(own[:, None, :] == slot, 1.0, 0.0)
         mover_ref[part] = mover.reshape(GROUP * CAP, lanes).astype(jnp.bfloat16)
+    for part in range(parts // 2, parts):
+        fetch(part).start()
     for part in range(parts):
         fetch(part).wait()
         moved = dot(mover_ref[part], waves_ref[part].reshape(lanes, width))
@@ -174,11 +176,12 @@
     factor_ref[listed : listed + 8, :] = jnp.broadcast_to(1.0 / jnp.maximum(total, 1.0), (8, 128))
 
 
-def mix_kernel(who_ref, pair_ref, right_ref, cross_ref, left_ref, lists_ref, scaled_ref, forward_ref, phase_ref,
+def mix_kernel(pair_ref, right_ref, cross_ref, left_ref, lists_ref, scaled_ref, forward_ref, phase_ref,
                mixed_ref, rows_ref):
     listed, span = lists_ref.shape[0] // 2, mixed_ref.shape[0]
     half = span // 2
-    chip, core = who_ref[0] // 2, who_ref[0] % 2
+    who = lax.axis_index("tmpl")
+    chip, core = who // 2, who % 2
     group = pair_ref.shape[2]
     rows_ref[:, 128:] = jnp.zeros((listed * 128, rows_ref.shape[1] - 128), jnp.bfloat16)
     for away, ref in enumerate((pair_ref, right_ref, cross_ref, left_ref)):
@@ -290,17 +293,17 @@
     )(got, found)
 
 
-def mix(who, blocks, lists, scaled, forward, phases):
+def mix(blocks, lists, scaled, forward, phases):
     columns = scaled.shape[0]
     return pl.pallas_call(
         mix_kernel,
         out_shape=jax.ShapeDtypeStruct((forward.shape[0], columns), jnp.bfloat16),
-        in_specs=[pl.BlockSpec(memory_space=pltpu.SMEM)] + vmem(8),
+        in_specs=vmem(8),
         out_specs=vmem(1)[0],
         scratch_shapes=[pltpu.VMEM((columns, forward.shape[1]), jnp.bfloat16)],
         compiler_params=params(),
         name="mix",
-    )(who, *blocks, lists, scaled, forward, phases)
+    )(*blocks, lists, scaled, forward, phases)
 
 
 def late_part(mixed, level, factor, inverse):
@@ -365,10 +368,9 @@
     own = jnp.concatenate([own[:, :, :128], tail], axis=0)
     pair = jnp.stack([own, other_core(own)])
     blocks = (pair, along_ring(pair, -1), along_ring(pair, 2), along_ring(pair, 1))
-    who = lax.axis_index("tmpl").reshape(1)
     scaled, level, factor = pick(got, find(lists))
     before = shifted(factor, 1)
-    mixed = mix(who, blocks, lists, scaled, forward, phases)
+    mixed = mix(blocks, lists, scaled, forward, phases)
     late = late_part(mixed, level, before, inverse_after)
     stack = own_part(mixed, factor, inverse, late)
     return stack + shifted(late, -1).astype(jnp.float32)

time: 61.1 us -> 60.9 us (level)
  no operation moved by 1% of the time
where the time goes in v6:
time: 60.9 us; the launch traced here: 60.5 us
  starting transfers between devices  35.2 us (58%)
  waiting for transfers between devices  16.5 us (27%)
  Pallas kernels  7.69 us (13%)
  other arithmetic  0.85 us (1%)
    all_to_all x1, starting transfers between devices, scatter_windows(): lax.all_to_all(pairs, ('tm', 'tmpl'), split_axis=0, concat_axis=0, axis_i...  20.4 us
    ppermute x3, starting transfers between devices, along_ring(): return lax.ppermute(value, ('tm', 'tmpl'), pairs)  9.06 us
    all_to_all x1, waiting for transfers between devices, scatter_windows(): lax.all_to_all(pairs, ('tm', 'tmpl'), split_axis=0, concat_axis=0, axis_i...  8 us
    ppermute x2, waiting for transfers between devices, shifted(): lax.ppermute(value, axis, [(i, i + by) for i in range(count) if 0 <= i +...  7.34 us
    ppermute x2, starting transfers between devices, shifted(): lax.ppermute(value, axis, [(i, i + by) for i in range(count) if 0 <= i +...  3.87 us
    pallas_call x1, Pallas kernels, pack(): pl.pallas_call(pack_kernel, out_shape=jax.ShapeDtypeStruct(shape, jnp.bfl...  3.36 us
    ppermute x1, starting transfers between devices, other_core(): return lax.ppermute(value, 'tmpl', [(i, i ^ 1) for i in range(8)])  1.91 us
    pallas_call x1, Pallas kernels, pick(): pl.pallas_call(pick_kernel, out_shape=(jax.ShapeDtypeStruct((columns, 256...  1.54 us
  transfers between devices with their start and end apart: 7, of which 4 were waited for; matrix products, arithmetic and copies ran while one was open for 0% of the time, Pallas kernels for 6%

profile of v6, /device:TPU:2, one launch (start us, length us, event | category | flops | bytes accessed | tf_op | source)
XLA Modules:
  0.0 60.5 jit_solution(1468212538310183721)
XLA Ops:
  0.0 3.4 %pack.1 = bf16[3200,128]{1,0:T(8,128)(2,1)} custom-call(s32[32,64]{1,0:T(8,128)} %bitcast.20, bf16[32,64,256]{2,1,0:T(8,128)(2,1)} %bitcast.16), custom_call_target="tpu_custom_call" | custom-call | tf_op jit(solution)/shard_map/pack/pallas_call | solution.py:248
  3.4 0.0 copy-start.4
  3.4 20.4 %all-to-all-start = ((bf16[64,25,2,128]{3,2,1,0:T(2,128)(2,1)}), bf16[64,25,2,128]{3,2,1,0:T(2,128)(2,1)S(1)}, u32[]{:S(2)}, u32[]{:S(2)}) async-start(bf16[64,25,2,128]{3,2,1,0:T(2,128)(2,1)} %bitcast.15), calls=%async_computation | async-start | bytes 1638400 | tf_op jit(solution)/shard_map/all_to_all | solution.py:354
  23.8 0.0 copy-done.4
  23.9 0.1 maximum_maximum_fusion
  23.9 1.9 %collective-permute-start = (bf16[12,16,128]{2,1,0:T(8,128)(2,1)S(1)}, bf16[12,16,128]{2,1,0:T(8,128)(2,1)S(1)}, u32[]{:S(2)}, u32[]{:S(2)}) collective-permute-start(bf16[12,16,128]{2,1,0:T(8,128)(2,1)S(1)} %maximum_maximum_fusion), channel_id=1, source_target_pairs={{0,1},{1,0},{2,3},{3,2},{4,5},{5,4},{6,7},{7,6},{8,9},{9,8},{10,11... | collective-permute-start | bytes 147464 | tf_op jit(solution)/shard_map/ppermute | solution.py:332
  25.9 0.1 fusion.1
  25.9 1.1 %collective-permute-done = bf16[12,16,128]{2,1,0:T(8,128)(2,1)S(1)} collective-permute-done((bf16[12,16,128]{2,1,0:T(8,128)(2,1)S(1)}, bf16[12,16,128]{2,1,0:T(8,128)(2,1)S(1)}, u32[]{:S(2)}, u32[]{:S(2)}) %collective-permute-start) | collective-permute-done | bytes 49184 | tf_op jit(solution)/shard_map/ppermute | solution.py:332
  27.1 0.0 copy-start.5
  27.1 0.0 copy-start.6
  27.1 2.1 %collective-permute-start.1 = (bf16[2,12,16,128]{3,2,1,0:T(8,128)(2,1)S(1)}, bf16[2,12,16,128]{3,2,1,0:T(8,128)(2,1)S(1)}, u32[]{:S(2)}, u32[]{:S(2)}) collective-permute-start(bf16[2,12,16,128]{3,2,1,0:T(8,128)(2,1)S(1)} %pad_maximum_fusion.pair_ref), channel_id=1, source_target_pairs={{0,14},{1,15},{2,0},{3,1},{4,2},{5,3},{6,4},{7,5},{8,6},{9,7},{10,... | collective-permute-start | bytes 294920 | tf_op jit(solution)/shard_map/ppermute | solution.py:341
  29.1 4.0 %collective-permute-start.2 = (bf16[2,12,16,128]{3,2,1,0:T(8,128)(2,1)S(1)}, bf16[2,12,16,128]{3,2,1,0:T(8,128)(2,1)S(1)}, u32[]{:S(2)}, u32[]{:S(2)}) collective-permute-start(bf16[2,12,16,128]{3,2,1,0:T(8,128)(2,1)S(1)} %pad_maximum_fusion.pair_ref), channel_id=1, source_target_pairs={{0,4},{1,5},{2,6},{3,7},{4,8},{5,9},{6,10},{7,11},{8,12},{9,13},{1... | collective-permute-start | bytes 294920 | tf_op jit(solution)/shard_map/ppermute | solution.py:341
  33.2 3.0 %collective-permute-start.3 = (bf16[2,12,16,128]{3,2,1,0:T(8,128)(2,1)S(1)}, bf16[2,12,16,128]{3,2,1,0:T(8,128)(2,1)S(1)}, u32[]{:S(2)}, u32[]{:S(2)}) collective-permute-start(bf16[2,12,16,128]{3,2,1,0:T(8,128)(2,1)S(1)} %pad_maximum_fusion.pair_ref), channel_id=1, source_target_pairs={{0,2},{1,3},{2,4},{3,5},{4,6},{5,7},{6,8},{7,9},{8,10},{9,11},{10,... | collective-permute-start | bytes 294920 | tf_op jit(solution)/shard_map/ppermute | solution.py:341
  36.2 0.0 copy-done.5
  36.2 0.0 copy-done.6
  36.2 0.6 find.1.find_ref
  36.8 8.0 %all-to-all-done = bf16[64,25,2,128]{3,2,1,0:T(2,128)(2,1)S(1)} async-done(((bf16[64,25,2,128]{3,2,1,0:T(2,128)(2,1)}), bf16[64,25,2,128]{3,2,1,0:T(2,128)(2,1)S(1)}, u32[]{:S(2)}, u32[]{:S(2)}) %all-to-all-start) | async-done | bytes 819232 | tf_op jit(solution)/shard_map/all_to_all | solution.py:354
  44.8 0.0 copy-start
  44.8 0.0 copy-start.3
  44.8 1.5 %pick.1 = (bf16[1024,256]{1,0:T(8,128)(2,1)S(1)}, f32[8,128]{1,0:T(8,128)S(1)}, f32[16,128]{1,0:T(8,128)S(1)}) custom-call(bf16[3200,128]{1,0:T(8,128)(2,1)S(1)} %bitcast.14, bf16[1024,128]{1,0:T(8,128)(2,1)S(1)} %find.1.find_ref), custom_call_target="tpu_custom_call" | custom-call | tf_op jit(solution)/shard_map/pick/pallas_call | solution.py:282
  46.3 1.9 %collective-permute-start.4 = (f32[16,128]{1,0:T(8,128)S(1)}, f32[16,128]{1,0:T(8,128)S(1)}, u32[]{:S(2)}, u32[]{:S(2)}) collective-permute-start(f32[16,128]{1,0:T(8,128)S(1)} %get-tuple-element.9.factor_ref), channel_id=1, source_target_pairs={{0,1},{1,2},{2,3},{3,4},{4,5},{5,6},{6,7},{7,8},{8,9},{9,10},{10,1... | collective-permute-start | bytes 24584 | tf_op jit(solution)/shard_map/ppermute | solution.py:347
  48.3 0.0 collective-permute-done.1.right_ref
  48.3 0.0 collective-permute-done.2.cross_ref
  48.3 0.0 collective-permute-done.3.left_ref
  48.3 0.0 copy-done
  48.3 0.0 copy-done.3
  48.3 0.0 copy-start.2
  48.3 1.3 %mix.1.mixed_ref = bf16[512,1024]{1,0:T(8,128)(2,1)S(1)} custom-call(bf16[2,12,16,128]{3,2,1,0:T(8,128)(2,1)S(1)} %pad_maximum_fusion.pair_ref, bf16[2,12,16,128]{3,2,1,0:T(8,128)(2,1)S(1)} %collective-permute-done.1.right_ref, bf16[2,12,16,128]{3,2,1,0:T(8,128)(2,1)S(1)} %collective-permute-done.2.cross_ref, ...), custom_call_target="tpu_custom_call" | custom-call | tf_op jit(solution)/shard_map/mix/pallas_call | solution.py:298
  49.6 5.9 %collective-permute-done.4.factor_ref = f32[16,128]{1,0:T(8,128)S(1)} collective-permute-done((f32[16,128]{1,0:T(8,128)S(1)}, f32[16,128]{1,0:T(8,128)S(1)}, u32[]{:S(2)}, u32[]{:S(2)}) %collective-permute-start.4) | collective-permute-done | bytes 8224 | tf_op jit(solution)/shard_map/ppermute | solution.py:347
  55.5 0.0 copy-done.2
  55.5 0.0 copy-start.1
  55.5 0.5 late_part.1.late_ref
  56.0 2.0 %collective-permute-start.5 = (bf16[128,256]{1,0:T(8,128)(2,1)S(1)}, bf16[128,256]{1,0:T(8,128)(2,1)S(1)}, u32[]{:S(2)}, u32[]{:S(2)}) collective-permute-start(bf16[128,256]{1,0:T(8,128)(2,1)S(1)} %late_part.1.late_ref), channel_id=1, source_target_pairs={{1,0},{2,1},{3,2},{4,3},{5,4},{6,5},{7,6},{8,7},{9,8},{10,9},{11,1... | collective-permute-start | bytes 196616 | tf_op jit(solution)/shard_map/ppermute | solution.py:347
  58.0 0.0 copy-done.1
  58.0 0.5 own_part.1
  58.4 1.4 %collective-permute-done.5 = bf16[128,256]{1,0:T(8,128)(2,1)S(1)} collective-permute-done((bf16[128,256]{1,0:T(8,128)(2,1)S(1)}, bf16[128,256]{1,0:T(8,128)(2,1)S(1)}, u32[]{:S(2)}, u32[]{:S(2)}) %collective-permute-start.5) | collective-permute-done | bytes 65568 | tf_op jit(solution)/shard_map/ppermute | solution.py:347
  59.9 0.7 %convert_add_fusion = f32[128,256]{1,0:T(8,128)} fusion(f32[128,256]{1,0:T(8,128)S(1)} %own_part.1, bf16[128,256]{1,0:T(8,128)(2,1)S(1)} %collective-permute-done.5), kind=kLoop, calls=%fused_computation | loop fusion | flops 65536 | bytes 327680 | tf_op jit(solution)/shard_map/add | solution.py:376
  (5 shorter events, 0.0 us)
Async XLA Ops:
  3.4 20.4 %copy-start.4 = (bf16[16,8,192]{2,1,0:T(8,128)(2,1)S(1)}, bf16[16,8,192]{2,1,0:T(8,128)(2,1)}, u32[]{:S(2)}) copy-start(bf16[16,8,192]{2,1,0:T(8,128)(2,1)} %param.11) | copy-start | bytes 147460
  3.4 41.4 %all-to-all-start = ((bf16[64,25,2,128]{3,2,1,0:T(2,128)(2,1)}), bf16[64,25,2,128]{3,2,1,0:T(2,128)(2,1)S(1)}, u32[]{:S(2)}, u32[]{:S(2)}) async-start(bf16[64,25,2,128]{3,2,1,0:T(2,128)(2,1)} %bitcast.15), calls=%async_computation | async-start | bytes 1638400 | tf_op jit(solution)/shard_map/all_to_all | solution.py:354
  23.9 3.1 %collective-permute-start = (bf16[12,16,128]{2,1,0:T(8,128)(2,1)S(1)}, bf16[12,16,128]{2,1,0:T(8,128)(2,1)S(1)}, u32[]{:S(2)}, u32[]{:S(2)}) collective-permute-start(bf16[12,16,128]{2,1,0:T(8,128)(2,1)S(1)} %maximum_maximum_fusion), channel_id=1, source_target_pairs={{0,1},{1,0},{2,3},{3,2},{4,5},{5,4},{6,7},{7,6},{8,9},{9,8},{10,11... | collective-permute-start | bytes 147464 | tf_op jit(solution)/shard_map/ppermute | solution.py:332
  27.1 9.1 %copy-start.5 = (s32[128,8]{0,1:T(8,128)S(1)}, s32[128,8]{0,1:T(8,128)}, u32[]{:S(2)}) copy-start(s32[128,8]{0,1:T(8,128)} %param.13) | copy-start | bytes 12292
  27.1 9.1 %copy-start.6 = (s32[128,8]{0,1:T(8,128)S(1)}, s32[128,8]{0,1:T(8,128)}, u32[]{:S(2)}) copy-start(s32[128,8]{0,1:T(8,128)} %param.12) | copy-start | bytes 12292
  27.1 21.2 %collective-permute-start.1 = (bf16[2,12,16,128]{3,2,1,0:T(8,128)(2,1)S(1)}, bf16[2,12,16,128]{3,2,1,0:T(8,128)(2,1)S(1)}, u32[]{:S(2)}, u32[]{:S(2)}) collective-permute-start(bf16[2,12,16,128]{3,2,1,0:T(8,128)(2,1)S(1)} %pad_maximum_fusion.pair_ref), channel_id=1, source_target_pairs={{0,14},{1,15},{2,0},{3,1},{4,2},{5,3},{6,4},{7,5},{8,6},{9,7},{10,... | collective-permute-start | bytes 294920 | tf_op jit(solution)/shard_map/ppermute | solution.py:341
  29.1 19.1 %collective-permute-start.2 = (bf16[2,12,16,128]{3,2,1,0:T(8,128)(2,1)S(1)}, bf16[2,12,16,128]{3,2,1,0:T(8,128)(2,1)S(1)}, u32[]{:S(2)}, u32[]{:S(2)}) collective-permute-start(bf16[2,12,16,128]{3,2,1,0:T(8,128)(2,1)S(1)} %pad_maximum_fusion.pair_ref), channel_id=1, source_target_pairs={{0,4},{1,5},{2,6},{3,7},{4,8},{5,9},{6,10},{7,11},{8,12},{9,13},{1... | collective-permute-start | bytes 294920 | tf_op jit(solution)/shard_map/ppermute | solution.py:341
  33.2 15.1 %collective-permute-start.3 = (bf16[2,12,16,128]{3,2,1,0:T(8,128)(2,1)S(1)}, bf16[2,12,16,128]{3,2,1,0:T(8,128)(2,1)S(1)}, u32[]{:S(2)}, u32[]{:S(2)}) collective-permute-start(bf16[2,12,16,128]{3,2,1,0:T(8,128)(2,1)S(1)} %pad_maximum_fusion.pair_ref), channel_id=1, source_target_pairs={{0,2},{1,3},{2,4},{3,5},{4,6},{5,7},{6,8},{7,9},{8,10},{9,11},{10,... | collective-permute-start | bytes 294920 | tf_op jit(solution)/shard_map/ppermute | solution.py:341
  44.8 3.5 %copy-start = (bf16[512,256]{1,0:T(8,128)(2,1)S(1)}, bf16[512,256]{1,0:T(8,128)(2,1)}, u32[]{:S(2)}) copy-start(bf16[512,256]{1,0:T(8,128)(2,1)} %constant.8.clone.forward_ref) | copy-start | bytes 786436
  44.8 3.5 %copy-start.3 = (bf16[512,64]{1,0:T(8,128)(2,1)S(1)}, bf16[512,64]{1,0:T(8,128)(2,1)}, u32[]{:S(2)}) copy-start(bf16[512,64]{1,0:T(8,128)(2,1)} %constant.11.clone.phase_ref) | copy-start | bytes 196612
  46.3 9.2 %collective-permute-start.4 = (f32[16,128]{1,0:T(8,128)S(1)}, f32[16,128]{1,0:T(8,128)S(1)}, u32[]{:S(2)}, u32[]{:S(2)}) collective-permute-start(f32[16,128]{1,0:T(8,128)S(1)} %get-tuple-element.9.factor_ref), channel_id=1, source_target_pairs={{0,1},{1,2},{2,3},{3,4},{4,5},{5,6},{6,7},{7,8},{8,9},{9,10},{10,1... | collective-permute-start | bytes 24584 | tf_op jit(solution)/shard_map/ppermute | solution.py:347
  48.3 7.2 %copy-start.2 = (bf16[256,512]{1,0:T(8,128)(2,1)S(1)}, bf16[256,512]{1,0:T(8,128)(2,1)}, u32[]{:S(2)}) copy-start(bf16[256,512]{1,0:T(8,128)(2,1)} %constant.10.clone.inverse_ref) | copy-start | bytes 786436
  55.5 2.4 %copy-start.1 = (bf16[256,512]{1,0:T(8,128)(2,1)S(1)}, bf16[256,512]{1,0:T(8,128)(2,1)}, u32[]{:S(2)}) copy-start(bf16[256,512]{1,0:T(8,128)(2,1)} %constant.9.clone.inverse_ref) | copy-start | bytes 786436
  56.0 3.8 %collective-permute-start.5 = (bf16[128,256]{1,0:T(8,128)(2,1)S(1)}, bf16[128,256]{1,0:T(8,128)(2,1)S(1)}, u32[]{:S(2)}, u32[]{:S(2)}) collective-permute-start(bf16[128,256]{1,0:T(8,128)(2,1)S(1)} %late_part.1.late_ref), channel_id=1, source_target_pairs={{1,0},{2,1},{3,2},{4,3},{5,4},{6,5},{7,6},{8,7},{9,8},{10,9},{11,1... | collective-permute-start | bytes 196616 | tf_op jit(solution)/shard_map/ppermute | solution.py:347
